TPU v7x, 1024 devices: a whole 8x8x8 slice. The times are simulated.
1024 devices in a mesh: batch: 32 (over y, z_lo), mp: 32 (over x, z_hi, core).
Axes of the slice: x: 8, y: 8, z: 8 (z_hi: 2, z_lo: 4; z = z_hi * 4 + z_lo), core: 2. Of those that a mesh axis runs over, the one named last changes fastest.
Arguments:
- panels: bfloat16 [32, 256, 256, 256], P('mp', None, 'batch'), may hold values from -6 to 6
- cotangent: bfloat16 [32, 256, 256, 256], P('mp', 'batch'), may hold values from -6 to 6
- fm_proj: bfloat16 [256, 16], replicated, may hold values from -0.0234375 to 0.0234375
- mlp_weight: bfloat16 [4096, 16384], P(None, 'mp'), may hold values from -0.09375 to 0.09375
- compress_weight: bfloat16 [192, 256], replicated, may hold values from -0.375 to 0.375
Outputs:
- layer_result_panels: bfloat16 [32, 256, 256, 256], P('mp', 'batch')
- mlp_grad: float32 [4096, 16384], P('batch', 'mp')
All inputs are finite; a program needn't handle non-finite values.
Results may differ from a plain program's by a relative error of at most 0.03.
Values may be sent and summed in bfloat16 or wider, within the bound.
No kernel may reach another device: no remote copies, remote signals or barrier semaphores. Data moves between devices by JAX's collectives and lax.ppermute only.
A program may use at most 64 MiB of HBM per device.

v0:
```python
import jax
import jax.numpy as jnp
from jax import lax
from jax.sharding import PartitionSpec as P

NF = 64


def layer_norm(value_entries):
    mean = jnp.mean(value_entries, axis=-1, keepdims=True)
    centred = value_entries - mean
    variance = jnp.mean(centred * centred, axis=-1, keepdims=True)
    return centred * lax.rsqrt(variance + 1e-05)


def silu_slope(pre):
    sigma = jax.nn.sigmoid(pre)
    return sigma * (1.0 + pre * (1.0 - sigma))


def shards(panels, cotangent, fm_proj, mlp_weight, compress_weight):
    top_precision = lax.Precision.HIGHEST
    owned = lax.all_to_all(panels, "batch", split_axis=1, concat_axis=2, tiled=True)
    samples = owned.shape[1]
    feats = owned.shape[2]
    width = owned.shape[3]
    rank = fm_proj.shape[1]
    out_feats = NF
    device_local = owned[0]
    wide_panels = device_local.astype(jnp.float32)
    inner = jnp.einsum("snd,nk->sdk", device_local, fm_proj, preferred_element_type=jnp.float32)
    codes = (
        jnp.einsum("snd,sdk->snk", wide_panels, inner, precision=top_precision)
        .astype(jnp.bfloat16)
        .reshape(samples, feats * rank)
    )
    group_codes = lax.all_gather(codes, "mp", axis=0, tiled=True)
    pre = jnp.dot(group_codes, mlp_weight, preferred_element_type=jnp.float32)
    fmb_cols = jax.nn.silu(pre).astype(jnp.bfloat16)
    fmb = lax.all_to_all(fmb_cols, "mp", split_axis=0, concat_axis=1, tiled=True)
    linear_compress_block = jnp.einsum(
        "pm,qmo->qpo", compress_weight, device_local, preferred_element_type=jnp.float32
    )
    summed = (
        jnp.concatenate(
            [fmb.reshape(samples, out_feats, width).astype(jnp.float32), linear_compress_block],
            axis=1,
        )
        + wide_panels
    )
    normed, pull = jax.vjp(layer_norm, summed)
    grad_summed = pull(cotangent[0].astype(jnp.float32))[0]
    grad_fmb = grad_summed[:, :out_feats].reshape(samples, out_feats * width).astype(jnp.bfloat16)
    grad_cols = lax.all_to_all(grad_fmb, "mp", split_axis=1, concat_axis=0, tiled=True)
    grad_pre = (grad_cols.astype(jnp.float32) * silu_slope(pre)).astype(jnp.bfloat16)
    term = jnp.einsum(
        "sc,so->co", group_codes, grad_pre, preferred_element_type=jnp.float32
    ).astype(jnp.bfloat16)
    mlp_grad = lax.psum_scatter(
        lax.optimization_barrier(term).astype(jnp.float32).astype(jnp.bfloat16),
        "batch",
        scatter_dimension=0,
        tiled=True,
    ).astype(jnp.float32)
    return (normed.astype(jnp.bfloat16)[None], mlp_grad)


def solution(mesh):
    in_specs = (P("mp", None, "batch", None), P("mp", "batch", None, None), P(), P(None, "mp"), P())
    out_specs = (P("mp", "batch", None, None), P("batch", "mp"))
    return jax.shard_map(shards, mesh=mesh, in_specs=in_specs, out_specs=out_specs, check_vma=False)
```

profile of v0, /device:TPU:2, one launch (start us, length us, event | category | flops | bytes accessed | tf_op | source)
XLA Modules:
  0.0 393.1 jit_solution(16163578883600814163)
XLA Ops:
  7.2 0.0 copy-start
  7.2 0.0 copy-start.3
  7.2 0.0 all-gather.2.cloned.1.call-start
  7.2 44.8 %all_to_all.38 = bf16[1,256,8,256]{3,2,0,1:T(8,128)(2,1)S(1)} all-to-all(bf16[1,256,8,256]{3,2,0,1:T(8,128)(2,1)} %bitcast.89), channel_id=1, replica_groups=mesh['batch'=32,'mp'=32] {'batch'}, dimensions={1} | all-to-all | bytes 2097152 | tf_op jit(solution)/shard_map/all_to_all | solution.py:23
  52.0 0.0 copy-done.3
  52.0 0.2 fusion.8
  52.3 0.9 fusion.7
  53.2 0.3 copy.16
  53.5 1.4 reshape.133
  54.9 0.0 all-gather.2.cloned.1.call-update
  54.9 102.5 %all-gather.2.cloned.1.call-done = bf16[256,4096]{1,0:T(8,128)(2,1)} async-done(((bf16[8,4096]{1,0:T(8,128)(2,1)}), bf16[256,4096]{1,0:T(8,128)(2,1)}) %all-gather.2.cloned.1.call-update) | async-done | bytes 2097168 | tf_op jit(solution)/shard_map/all_gather | solution.py:37
  157.4 4.1 %fusion.26 = f32[256,512]{1,0:T(8,128)S(1)} fusion(bf16[256,4096]{1,0:T(8,128)(2,1)} %all-gather.2.cloned.1.call-done, bf16[4096,512]{1,0:T(8,128)(2,1)} %param.8), kind=kOutput, calls=%fused_computation.43 | convolution fusion | flops 1073741824 | bytes 6815744 | tf_op jit(solution)/shard_map/dot_general | solution.py:38
  161.5 0.0 copy-start.2
  161.5 0.9 fusion.20
  162.4 5.5 %all-to-all-start.1 = ((bf16[32,8,512]{2,1,0:T(8,128)(2,1)}), bf16[32,8,512]{2,1,0:T(8,128)(2,1)S(1)}, u32[]{:S(2)}, u32[]{:S(2)}) async-start(bf16[32,8,512]{2,1,0:T(8,128)(2,1)} %fusion.20), calls=%async_computation.1 | async-start | bytes 524288 | tf_op jit(solution)/shard_map/all_to_all | solution.py:40
  167.9 0.0 copy-done.2
  167.9 0.0 reduce-scatter.2.cloned.1.call-start
  167.9 0.0 copy-done
  168.0 0.4 fusion.11
  168.3 15.0 %all-to-all-done.1 = bf16[32,8,512]{2,1,0:T(8,128)(2,1)S(1)} async-done(((bf16[32,8,512]{2,1,0:T(8,128)(2,1)}), bf16[32,8,512]{2,1,0:T(8,128)(2,1)S(1)}, u32[]{:S(2)}, u32[]{:S(2)}) %all-to-all-start.1) | async-done | bytes 262176 | tf_op jit(solution)/shard_map/all_to_all | solution.py:40
  183.3 1.1 copy.17
  184.4 1.1 convert_element_type.104
  185.6 0.4 fusion.24
  186.0 0.1 div.27
  186.1 3.1 fusion.6
  189.2 1.0 reduce_sum.49
  190.3 0.1 add.48
  190.4 2.4 fusion.25
  192.8 0.1 fusion.13
  192.9 0.1 convert_element_type.112
  193.0 0.2 copy.19
  193.2 19.3 %all_to_all.39 = bf16[8,32,512]{2,0,1:T(8,128)(2,1)S(1)} all-to-all(bf16[8,32,512]{2,0,1:T(8,128)(2,1)S(1)} %copy.19), channel_id=1, replica_groups=mesh['batch'=32,'mp'=32] {'mp'}, dimensions={1} | all-to-all | bytes 524288 | tf_op jit(solution)/shard_map/all_to_all | solution.py:54
  212.5 5.0 %convolution_convert_fusion = bf16[4096,512]{1,0:T(8,128)(2,1)} fusion(bf16[256,4096]{1,0:T(8,128)(2,1)} %all-gather.2.cloned.1.call-done, bf16[8,32,512]{2,0,1:T(8,128)(2,1)S(1)} %all_to_all.39, f32[256,512]{1,0:T(8,128)} %copy-done.2), kind=kOutput, calls=%fused_computation | convolution fusion | flops 1077149696 | bytes 7077888 | tf_op jit(solution)/shard_map/sc,so->co/dot_general | solution.py:56
  217.5 0.0 copy-start.1
  217.5 0.0 reduce-scatter.2.cloned.1.call-update
  217.5 1.0 copy-done.1
  218.5 0.9 concatenate.18
  219.4 2.4 fusion.3
  221.9 162.8 %reduce-scatter.2.cloned.1.call-done = bf16[128,512]{1,0:T(8,128)(2,1)} async-done(((bf16[4096,512]{1,0:T(8,128)(2,1)}), bf16[128,512]{1,0:T(8,128)(2,1)}) %reduce-scatter.2.cloned.1.call-update) | async-done | bytes 131088 | tf_op jit(solution)/shard_map/reduce_scatter | solution.py:59
  384.6 1.6 convert_element_type.118
  (6 shorter events, 0.1 us)
Async XLA Ops:
  7.2 160.8 %copy-start = (bf16[192,256]{1,0:T(8,128)(2,1)S(1)}, bf16[192,256]{1,0:T(8,128)(2,1)}, u32[]{:S(2)}) copy-start(bf16[192,256]{1,0:T(8,128)(2,1)} %param.9) | copy-start | bytes 294916
  7.2 44.8 %copy-start.3 = (bf16[256,16]{0,1:T(8,128)(2,1)S(1)}, bf16[256,16]{0,1:T(8,128)(2,1)}, u32[]{:S(2)}) copy-start(bf16[256,16]{0,1:T(8,128)(2,1)} %param.7) | copy-start | bytes 24580
  7.2 150.2 %all-gather.2.cloned.1.call-start = ((), (), s32[]{:S(2)}) async-start(), calls=%async_computation.4 | async-start | bytes 2162688 | tf_op jit(solution)/shard_map/all_gather | solution.py:37
  161.5 6.4 %copy-start.2 = (f32[256,512]{1,0:T(8,128)}, f32[256,512]{1,0:T(8,128)S(1)}, u32[]{:S(2)}) copy-start(f32[256,512]{1,0:T(8,128)S(1)} %fusion.26) | copy-start | bytes 1572868
  162.4 20.9 %all-to-all-start.1 = ((bf16[32,8,512]{2,1,0:T(8,128)(2,1)}), bf16[32,8,512]{2,1,0:T(8,128)(2,1)S(1)}, u32[]{:S(2)}, u32[]{:S(2)}) async-start(bf16[32,8,512]{2,1,0:T(8,128)(2,1)} %fusion.20), calls=%async_computation.1 | async-start | bytes 524288 | tf_op jit(solution)/shard_map/all_to_all | solution.py:40
  167.9 216.7 %reduce-scatter.2.cloned.1.call-start = ((), (), s32[]{:S(2)}) async-start(), calls=%async_computation.5 | async-start | bytes 4325376 | tf_op jit(solution)/shard_map/reduce_scatter | solution.py:59
  217.5 1.0 copy-start.1
Sparse Core Ops, SparseCore 0:
  55.0 102.3 all-gather.1
  217.6 166.9 reduce-scatter.1
where the time goes:
time: 394 us; the launch traced here: 393 us
  waiting for transfers between devices  280 us (71%)
  blocking collectives  64.1 us (16%)
  between operations  14.2 us (4%)
  other arithmetic  11 us (3%)
  matrix products  10.7 us (3%)
  local copies, waits for them, and re-layouts  7.3 us (2%)
  starting transfers between devices  5.57 us (1%)
    reduce_scatter x1, waiting for transfers between devices, shards(): lax.psum_scatter(lax.optimization_barrier(term).astype(jnp.float32).astyp...  163 us
    all_gather x1, waiting for transfers between devices, shards(): group_codes = lax.all_gather(codes, 'mp', axis=0, tiled=True)  103 us
    all_to_all x1, blocking collectives, shards(): lax.all_to_all(panels, 'batch', split_axis=1, concat_axis=2, tiled=True)  44.8 us
    all_to_all x1, blocking collectives, shards(): lax.all_to_all(grad_fmb, 'mp', split_axis=1, concat_axis=0, tiled=True)  19.3 us
    all_to_all x1, waiting for transfers between devices, shards(): lax.all_to_all(fmb_cols, 'mp', split_axis=0, concat_axis=1, tiled=True)  15 us
  transfers between devices with their start and end apart: 3, of which 3 were waited for; matrix products, arithmetic and copies ran while one was open for 1% of the time, Pallas kernels for 0%

commit v1 on v0

v1 whole, which is shorter than its diff:
```python
import jax
import jax.numpy as jnp
from jax import lax
from jax.sharding import Mesh
from jax.sharding import PartitionSpec as P

NF = 64
EPS = 1e-05
FINE = (("y", 8), ("pair", 2), ("twin", 2), ("x", 8), ("far", 2), ("core", 2))
BATCH = ("y", "pair", "twin")
MP = ("x", "far", "core")
OTHER = [(0, 1), (1, 0)]


def swap(chunks, axes):
    return lax.all_to_all(chunks, axes, split_axis=0, concat_axis=0, tiled=True)


def normalise(rows):
    mean = jnp.mean(rows, axis=-1, keepdims=True)
    centred = rows - mean
    variance = jnp.mean(centred * centred, axis=-1, keepdims=True)
    inverse = lax.rsqrt(variance + EPS)
    return centred * inverse, inverse


def column_block(codes, weight, rows, grads):
    samples = codes.shape[0]
    own_feats, _, width = rows.shape
    pre = jnp.dot(codes, weight, preferred_element_type=jnp.float32)
    normed, grad_pre = [], []
    for f in range(own_feats):
        v = pre[:, f * width : (f + 1) * width]
        sigma = jax.nn.sigmoid(v)
        fmb = (v * sigma).astype(jnp.bfloat16).astype(jnp.float32)
        y, inverse = normalise(fmb + rows[f].astype(jnp.float32))
        g = grads[f].astype(jnp.float32)
        mean_g = jnp.mean(g, axis=-1, keepdims=True)
        mean_gy = jnp.mean(g * y, axis=-1, keepdims=True)
        grad_fmb = (inverse * (g - mean_g - y * mean_gy)).astype(jnp.bfloat16).astype(jnp.float32)
        normed.append(y.astype(jnp.bfloat16))
        grad_pre.append((grad_fmb * (sigma * (1.0 + v * (1.0 - sigma)))).astype(jnp.bfloat16))
    return jnp.stack(normed), jnp.concatenate(grad_pre, axis=1)


def shards(panels, cotangent, fm_proj, mlp_weight, compress_weight):
    blocks = lax.axis_size(BATCH)
    owners = lax.axis_size(MP)
    peers = owners // 2
    core = lax.axis_index("core")
    twin = lax.axis_index("twin")
    group, feats_dev, width = panels.shape[1:]
    samples = group // blocks
    feats = feats_dev * blocks
    rank = fm_proj.shape[1]
    own_feats = NF // owners
    half = peers * samples
    code_cols = feats * rank
    code_blocks = code_cols // width
    lanes = width // 2

    owned = swap(panels.reshape(blocks, samples, feats_dev, width), BATCH)
    wide = owned.transpose(1, 0, 2, 3).reshape(samples, feats, width)
    inner = jnp.einsum("snd,nk->sdk", wide, fm_proj, preferred_element_type=jnp.float32)
    codes = jnp.einsum(
        "snd,sdk->snk", wide.astype(jnp.float32), inner, precision=lax.Precision.HIGHEST
    )
    codes = codes.astype(jnp.bfloat16).reshape(samples, code_blocks, width).transpose(1, 0, 2)

    def by_peer(rows):
        rows = rows.reshape(samples, peers, 2, own_feats, width).transpose(1, 2, 3, 0, 4)
        return jnp.where(core == 0, rows, rows[:, ::-1])

    head_rows = by_peer(wide[:, :NF])
    head_grads = by_peer(cotangent[0, :, :NF])
    parcel = jnp.concatenate(
        [
            jnp.broadcast_to(codes, (peers, *codes.shape)),
            head_rows[:, 0],
            head_grads[:, 0],
            head_rows[:, 1],
            head_grads[:, 1],
        ],
        axis=1,
    )
    parcel = swap(parcel, ("x", "far"))
    ends = [code_blocks + own_feats * i for i in range(5)]

    def rows_of(first):
        return parcel[:, ends[first] : ends[first + 1]]

    mine = (parcel[:, :code_blocks], rows_of(0), rows_of(1))
    other = lax.ppermute(
        jnp.concatenate([mine[0], rows_of(2), rows_of(3)], axis=1), "core", OTHER
    )
    other = (other[:, :code_blocks], other[:, ends[0] : ends[1]], other[:, ends[1] : ends[2]])

    def lane_half(blocked, which):
        return jnp.where(which == 0, blocked[..., :lanes], blocked[..., lanes:])

    sent = lane_half(mine[0], 1 - twin)
    twin_mine = lax.ppermute(sent, "twin", OTHER)
    twin_other = lax.ppermute(twin_mine, "core", OTHER)

    normed, grad_pre = [], []
    for blocked, rows, grads in (mine, other):
        flat = blocked.transpose(0, 2, 1, 3).reshape(half, code_cols)
        tall = [a.transpose(1, 0, 2, 3).reshape(own_feats, half, width) for a in (rows, grads)]
        y, g = column_block(flat, mlp_weight, *tall)
        normed.append(y)
        grad_pre.append(g)
    grad_pre = jnp.concatenate(grad_pre, axis=0)
    twin_grad = lax.ppermute(grad_pre, "twin", OTHER)

    def columns(blocked):
        return blocked.transpose(0, 2, 1, 3).reshape(half, code_blocks * lanes)

    left = jnp.concatenate(
        [columns(a) for a in (lane_half(mine[0], twin), lane_half(other[0], twin), twin_mine, twin_other)]
    )
    right = jnp.concatenate([grad_pre, twin_grad])
    term = jnp.einsum("sc,so->co", left, right, preferred_element_type=jnp.float32)
    term = term.astype(jnp.bfloat16).reshape(code_blocks, lanes, -1)
    mlp_grad = jnp.sum(swap(term, ("y", "pair")).astype(jnp.float32), axis=0)

    back = jnp.stack(normed).reshape(2, own_feats, peers, samples, width)
    back = jnp.where(core == 0, back, back[::-1]).transpose(2, 0, 1, 3, 4)
    back = swap(back.reshape(owners, own_feats, samples, width), MP)
    head = back.transpose(2, 0, 1, 3).reshape(samples, NF, width)
    lcb = jnp.einsum("pm,qmo->qpo", compress_weight, wide, preferred_element_type=jnp.float32)
    tail, _ = normalise(lcb + wide[:, NF:].astype(jnp.float32))
    result = jnp.concatenate([head, tail.astype(jnp.bfloat16)], axis=1)
    return result[None], mlp_grad


def solution(mesh):
    fine = Mesh(mesh.devices.reshape([n for _, n in FINE]), [name for name, _ in FINE])
    in_specs = (P(MP, None, BATCH, None), P(MP, BATCH, None, None), P(), P(None, MP), P())
    out_specs = (P(MP, BATCH, None, None), P(BATCH, MP))
    return jax.shard_map(shards, mesh=fine, in_specs=in_specs, out_specs=out_specs, check_vma=False)
```

time: 394 us -> 254 us (0.64)
  the two profiles are of different devices: /device:TPU:2 before, /device:TPU:32 now
where the time goes in v1:
time: 254 us; the launch traced here: 253 us
  waiting for transfers between devices  164 us (65%)
  starting transfers between devices  58.8 us (23%)
  matrix products  11.2 us (4%)
  local copies, waits for them, and re-layouts  9.02 us (4%)
  other arithmetic  8.76 us (3%)
    all_to_all x4, waiting for transfers between devices, swap(): return lax.all_to_all(chunks, axes, split_axis=0, concat_axis=0, tiled=True)  139 us
    all_to_all x4, starting transfers between devices, swap(): return lax.all_to_all(chunks, axes, split_axis=0, concat_axis=0, tiled=True)  50.9 us
    ppermute x1, waiting for transfers between devices, shards(): twin_mine = lax.ppermute(sent, 'twin', OTHER)  13.8 us
    ppermute x1, waiting for transfers between devices, shards(): twin_grad = lax.ppermute(grad_pre, 'twin', OTHER)  10.7 us
    dot_general x2, matrix products, column_block(): pre = jnp.dot(codes, weight, preferred_element_type=jnp.float32)  5.87 us
  transfers between devices with their start and end apart: 8, of which 5 were waited for; matrix products, arithmetic and copies ran while one was open for 7% of the time, Pallas kernels for 0%

profile of v1, /device:TPU:32, one launch (start us, length us, event | category | flops | bytes accessed | tf_op | source)
XLA Modules:
  0.0 253.0 jit_solution(5652523047148537605)
XLA Ops:
  0.7 16.5 %all-to-all-start = ((bf16[32,8,8,256]{3,2,1,0:T(8,128)(2,1)}), bf16[32,8,8,256]{3,2,1,0:T(8,128)(2,1)S(1)}, u32[]{:S(2)}, u32[]{:S(2)}) async-start(bf16[32,8,8,256]{3,2,1,0:T(8,128)(2,1)} %bitcast.217), calls=%async_computation | async-start | bytes 2097152 | tf_op jit(solution)/shard_map/all_to_all | solution.py:16
  17.2 0.2 copy.32
  17.4 28.1 %all-to-all-done = bf16[32,8,8,256]{3,2,1,0:T(8,128)(2,1)S(1)} async-done(((bf16[32,8,8,256]{3,2,1,0:T(8,128)(2,1)}), bf16[32,8,8,256]{3,2,1,0:T(8,128)(2,1)S(1)}, u32[]{:S(2)}, u32[]{:S(2)}) %all-to-all-start) | async-done | bytes 1048608 | tf_op jit(solution)/shard_map/all_to_all | solution.py:16
  45.6 0.2 copy.31
  45.8 0.3 fusion.68
  46.0 0.9 fusion.7
  47.0 0.3 copy.25
  47.3 0.5 reshape.210
  47.8 1.1 broadcast_dynamic-update-slice_fusion
  48.8 0.2 reverse_select_fusion.1
  49.0 0.7 fusion.46
  49.7 0.7 fusion.45
  50.4 0.7 fusion.44
  51.1 0.7 fusion.43
  51.7 16.2 %all-to-all-start.1 = ((bf16[16,24,8,256]{3,2,1,0:T(8,128)(2,1)}), bf16[16,24,8,256]{3,2,1,0:T(8,128)(2,1)S(1)}, u32[]{:S(2)}, u32[]{:S(2)}) async-start(bf16[16,24,8,256]{3,2,1,0:T(8,128)(2,1)} %fusion.43), calls=%async_computation.1 | async-start | bytes 3145728 | tf_op jit(solution)/shard_map/all_to_all | solution.py:16
  68.0 50.5 %all-to-all-done.1 = bf16[16,24,8,256]{3,2,1,0:T(8,128)(2,1)S(1)} async-done(((bf16[16,24,8,256]{3,2,1,0:T(8,128)(2,1)}), bf16[16,24,8,256]{3,2,1,0:T(8,128)(2,1)S(1)}, u32[]{:S(2)}, u32[]{:S(2)}) %all-to-all-start.1) | async-done | bytes 1572896 | tf_op jit(solution)/shard_map/all_to_all | solution.py:16
  118.6 2.9 %fusion.72 = f32[128,512]{1,0:T(8,128)S(1)} fusion(bf16[128,4096]{1,0:T(8,128)(2,1)S(1)} %bitcast.214, bf16[4096,512]{1,0:T(8,128)(2,1)} %param.8), kind=kOutput, calls=%fused_computation.148 | convolution fusion | flops 536870912 | bytes 5505024 | tf_op jit(solution)/shard_map/dot_general | solution.py:30
  121.6 0.2 fusion.48
  121.8 0.2 multiply_reduce_fusion.4
  122.0 1.2 pad_maximum_fusion
  123.2 1.9 collective-permute-start
  125.1 1.1 select_bitcast_fusion
  126.3 1.9 collective-permute-start.1
  128.2 0.2 fusion.30
  128.6 0.2 multiply_convert_fusion.4
  128.9 13.8 %collective-permute-done.1 = bf16[16,16,8,128]{3,2,1,0:T(8,128)(2,1)S(1)} collective-permute-done((bf16[16,16,8,128]{3,2,1,0:T(8,128)(2,1)}, bf16[16,16,8,128]{3,2,1,0:T(8,128)(2,1)S(1)}, u32[]{:S(2)}, u32[]{:S(2)}) %collective-permute-start.1) | collective-permute-done | bytes 524320 | tf_op jit(solution)/shard_map/ppermute | solution.py:102
  142.7 1.9 collective-permute-start.2
  144.6 1.0 slice_bitcast_fusion
  145.9 1.3 slice.148
  147.3 3.0 %fusion.73 = f32[128,512]{1,0:T(8,128)S(1)} fusion(bf16[128,4096]{1,0:T(8,128)(2,1)S(1)} %bitcast.215, bf16[4096,512]{1,0:T(8,128)(2,1)} %param.8), kind=kOutput, calls=%fused_computation.149 | convolution fusion | flops 536870912 | bytes 5505024 | tf_op jit(solution)/shard_map/dot_general | solution.py:30
  150.2 0.2 fusion.52
  150.4 0.2 multiply_reduce_fusion.2
  150.6 0.2 fusion.38
  150.9 0.2 multiply_convert_fusion.2
  151.2 1.0 copy.29
  152.2 10.2 %all-to-all-start.2 = ((bf16[32,2,8,256]{3,1,2,0:T(2,128)(2,1)}), bf16[32,2,8,256]{3,1,2,0:T(2,128)(2,1)S(1)}, u32[]{:S(2)}, u32[]{:S(2)}) async-start(bf16[32,2,8,256]{3,1,2,0:T(2,128)(2,1)} %bitcast.31), calls=%async_computation.2 | async-start | bytes 524288 | tf_op jit(solution)/shard_map/all_to_all | solution.py:16
  162.4 2.2 collective-permute-start.3
  164.6 1.3 fusion.8
  165.9 10.7 %collective-permute-done.3 = bf16[256,512]{1,0:T(8,128)(2,1)S(1)} collective-permute-done((bf16[256,512]{1,0:T(8,128)(2,1)S(1)}, bf16[256,512]{1,0:T(8,128)(2,1)S(1)}, u32[]{:S(2)}, u32[]{:S(2)}) %collective-permute-start.3) | collective-permute-done | bytes 262176 | tf_op jit(solution)/shard_map/ppermute | solution.py:113
  176.6 3.7 %convolution_convert_fusion = bf16[2048,512]{1,0:T(8,128)(2,1)} fusion(bf16[128,2048]{1,0:T(8,128)(2,1)} %bitcast.43, bf16[128,2048]{1,0:T(8,128)(2,1)S(1)} %bitcast.222, bf16[128,2048]{1,0:T(8,128)(2,1)S(1)} %fusion.8, bf16[128,2048]{1,0:T(8,128)(2,1)S(1)} %copy-done.1, bf16[256,512]{1,0:T(8,128)(2,1)S(1)} %collective-permute-done.3, ...), kind=kOutput, calls=%fused_computation.1 | convolution fusion | flops 1085800448 | bytes 4718592 | tf_op jit(solution)/shard_map/sc,so->co/dot_general | solution.py:122
  180.3 8.0 %all-to-all-start.3 = ((bf16[16,128,512]{2,1,0:T(8,128)(2,1)}), bf16[16,128,512]{2,1,0:T(8,128)(2,1)S(1)}, u32[]{:S(2)}, u32[]{:S(2)}) async-start(bf16[16,128,512]{2,1,0:T(8,128)(2,1)} %bitcast.216), calls=%async_computation.3 | async-start | bytes 4194304 | tf_op jit(solution)/shard_map/all_to_all | solution.py:16
  188.3 0.5 fusion.71
  188.8 0.6 multiply_reduce_fusion
  189.4 0.5 multiply_convert_fusion
  189.9 0.2 copy.30
  190.2 1.0 maximum_bitcast_fusion
  191.2 60.8 %all-to-all-done.3 = bf16[16,128,512]{2,1,0:T(8,128)(2,1)S(1)} async-done(((bf16[16,128,512]{2,1,0:T(8,128)(2,1)}), bf16[16,128,512]{2,1,0:T(8,128)(2,1)S(1)}, u32[]{:S(2)}, u32[]{:S(2)}) %all-to-all-start.3) | async-done | bytes 2097184 | tf_op jit(solution)/shard_map/all_to_all | solution.py:16
  252.1 1.0 convert_reduce_fusion
  (45 shorter events, 1.1 us)
Async XLA Ops:
  0.6 187.6 %copy-start = (bf16[192,256]{1,0:T(8,128)(2,1)S(1)}, bf16[192,256]{1,0:T(8,128)(2,1)}, u32[]{:S(2)}) copy-start(bf16[192,256]{1,0:T(8,128)(2,1)} %param.9) | copy-start | bytes 294916
  0.6 16.6 %slice-start = ((bf16[1,8,256,256]{3,2,1,0:T(8,128)(2,1)}), bf16[1,8,64,256]{3,2,1,0:T(8,128)(2,1)S(1)}, s32[]{:S(2)}) async-start(bf16[1,8,256,256]{3,2,1,0:T(8,128)(2,1)} %param.6), calls=%async_computation.4 | async-start | bytes 524288 | tf_op jit(solution)/shard_map/slice | solution.py:75
  0.7 44.9 %all-to-all-start = ((bf16[32,8,8,256]{3,2,1,0:T(8,128)(2,1)}), bf16[32,8,8,256]{3,2,1,0:T(8,128)(2,1)S(1)}, u32[]{:S(2)}, u32[]{:S(2)}) async-start(bf16[32,8,8,256]{3,2,1,0:T(8,128)(2,1)} %bitcast.217), calls=%async_computation | async-start | bytes 2097152 | tf_op jit(solution)/shard_map/all_to_all | solution.py:16
  17.4 28.4 %copy-start.2 = (bf16[256,16]{0,1:T(8,128)(2,1)S(1)}, bf16[256,16]{0,1:T(8,128)(2,1)}, u32[]{:S(2)}) copy-start(bf16[256,16]{0,1:T(8,128)(2,1)} %param.7) | copy-start | bytes 24580
  51.7 66.8 %all-to-all-start.1 = ((bf16[16,24,8,256]{3,2,1,0:T(8,128)(2,1)}), bf16[16,24,8,256]{3,2,1,0:T(8,128)(2,1)S(1)}, u32[]{:S(2)}, u32[]{:S(2)}) async-start(bf16[16,24,8,256]{3,2,1,0:T(8,128)(2,1)} %fusion.43), calls=%async_computation.1 | async-start | bytes 3145728 | tf_op jit(solution)/shard_map/all_to_all | solution.py:16
  123.2 21.4 %collective-permute-start = (bf16[16,20,8,256]{3,2,1,0:T(8,128)(2,1)}, bf16[16,20,8,256]{3,2,1,0:T(8,128)(2,1)}, u32[]{:S(2)}, u32[]{:S(2)}) collective-permute-start(bf16[16,20,8,256]{3,2,1,0:T(8,128)(2,1)} %pad_maximum_fusion), channel_id=1, source_target_pairs={{0,1},{1,0},{2,3},{3,2},{4,5},{5,4},{6,7},{7,6},{8,9},{9,8},{10,11... | collective-permute-start | bytes 3932168 | tf_op jit(solution)/shard_map/ppermute | solution.py:93
  126.3 16.4 %collective-permute-start.1 = (bf16[16,16,8,128]{3,2,1,0:T(8,128)(2,1)}, bf16[16,16,8,128]{3,2,1,0:T(8,128)(2,1)S(1)}, u32[]{:S(2)}, u32[]{:S(2)}) collective-permute-start(bf16[16,16,8,128]{3,2,1,0:T(8,128)(2,1)} %get-tuple-element.25), channel_id=1, source_target_pairs={{0,32},{32,0},{1,33},{33,1},{2,34},{34,2},{3,35},{35,3},{4,36},{36... | collective-permute-start | bytes 1572872 | tf_op jit(solution)/shard_map/ppermute | solution.py:102
  142.7 23.2 %collective-permute-start.2 = (bf16[16,16,8,128]{3,2,1,0:T(8,128)(2,1)S(1)}, bf16[16,16,8,128]{3,2,1,0:T(8,128)(2,1)}, u32[]{:S(2)}, u32[]{:S(2)}) collective-permute-start(bf16[16,16,8,128]{3,2,1,0:T(8,128)(2,1)S(1)} %collective-permute-done.1), channel_id=1, source_target_pairs={{0,1},{1,0},{2,3},{3,2},{4,5},{5,4},{6,7},{7,6},{8,9},{9,8},{10,11... | collective-permute-start | bytes 1572872 | tf_op jit(solution)/shard_map/ppermute | solution.py:103
  151.2 25.4 %copy-start.1 = (bf16[128,2048]{1,0:T(8,128)(2,1)S(1)}, bf16[128,2048]{1,0:T(8,128)(2,1)}, u32[]{:S(2)}) copy-start(bf16[128,2048]{1,0:T(8,128)(2,1)} %get-tuple-element.24) | copy-start | bytes 1572868
  152.2 28.1 %all-to-all-start.2 = ((bf16[32,2,8,256]{3,1,2,0:T(2,128)(2,1)}), bf16[32,2,8,256]{3,1,2,0:T(2,128)(2,1)S(1)}, u32[]{:S(2)}, u32[]{:S(2)}) async-start(bf16[32,2,8,256]{3,1,2,0:T(2,128)(2,1)} %bitcast.31), calls=%async_computation.2 | async-start | bytes 524288 | tf_op jit(solution)/shard_map/all_to_all | solution.py:16
  162.4 14.2 %collective-permute-start.3 = (bf16[256,512]{1,0:T(8,128)(2,1)S(1)}, bf16[256,512]{1,0:T(8,128)(2,1)S(1)}, u32[]{:S(2)}, u32[]{:S(2)}) collective-permute-start(bf16[256,512]{1,0:T(8,128)(2,1)S(1)} %maximum_maximum_fusion.1), channel_id=1, source_target_pairs={{0,32},{32,0},{1,33},{33,1},{2,34},{34,2},{3,35},{35,3},{4,36},{36... | collective-permute-start | bytes 786440 | tf_op jit(solution)/shard_map/ppermute | solution.py:113
  180.3 71.8 %all-to-all-start.3 = ((bf16[16,128,512]{2,1,0:T(8,128)(2,1)}), bf16[16,128,512]{2,1,0:T(8,128)(2,1)S(1)}, u32[]{:S(2)}, u32[]{:S(2)}) async-start(bf16[16,128,512]{2,1,0:T(8,128)(2,1)} %bitcast.216), calls=%async_computation.3 | async-start | bytes 4194304 | tf_op jit(solution)/shard_map/all_to_all | solution.py:16

commit v2 on v1

v2 whole, which is shorter than its diff:
```python
import jax
import jax.numpy as jnp
from jax import lax
from jax.sharding import Mesh
from jax.sharding import PartitionSpec as P

NF = 64
EPS = 1e-05
FINE = (("yh", 4), ("yl", 2), ("pair", 2), ("twin", 2), ("x", 8), ("far", 2), ("core", 2))
BATCH = ("yh", "yl", "pair", "twin")
MP = ("x", "far", "core")


def swap(chunks, axes):
    return lax.all_to_all(chunks, axes, split_axis=0, concat_axis=0, tiled=True)


def across(array, axis, distance=1):
    count = lax.axis_size(axis)
    return lax.ppermute(array, axis, [(i, i ^ distance) for i in range(count)])


def after(array, *others):
    return lax.optimization_barrier((array, *others))[0]


def pick(array, axis, index):
    return jnp.where(
        index == 0, lax.index_in_dim(array, 0, axis, False), lax.index_in_dim(array, 1, axis, False)
    )


def ordered(own, other, axis, index):
    return jnp.where(index == 0, jnp.stack([own, other], axis), jnp.stack([other, own], axis))


def cube_swap(buffer, axis, index, name, distance=1):
    sent = pick(buffer, axis, 1 - index)
    received = across(sent.reshape(-1, sent.shape[-1]), name, distance).reshape(sent.shape)
    return ordered(pick(buffer, axis, index), received, axis, index)


def normalise(rows):
    mean = jnp.mean(rows, axis=-1, keepdims=True)
    centred = rows - mean
    variance = jnp.mean(centred * centred, axis=-1, keepdims=True)
    inverse = lax.rsqrt(variance + EPS)
    return centred * inverse, inverse


def column_block(codes, weight, rows, grads):
    own_feats, _, width = rows.shape
    pre = jnp.dot(codes, weight, preferred_element_type=jnp.float32)
    normed, grad_pre = [], []
    for f in range(own_feats):
        v = pre[:, f * width : (f + 1) * width]
        sigma = jax.nn.sigmoid(v)
        fmb = (v * sigma).astype(jnp.bfloat16).astype(jnp.float32)
        y, inverse = normalise(fmb + rows[f].astype(jnp.float32))
        g = grads[f].astype(jnp.float32)
        mean_g = jnp.mean(g, axis=-1, keepdims=True)
        mean_gy = jnp.mean(g * y, axis=-1, keepdims=True)
        grad_fmb = (inverse * (g - mean_g - y * mean_gy)).astype(jnp.bfloat16).astype(jnp.float32)
        normed.append(y.astype(jnp.bfloat16))
        grad_pre.append((grad_fmb * (sigma * (1.0 + v * (1.0 - sigma)))).astype(jnp.bfloat16))
    return jnp.stack(normed), jnp.concatenate(grad_pre, axis=1)


def shards(panels, cotangent, fm_proj, mlp_weight, compress_weight):
    blocks = lax.axis_size(BATCH)
    owners = lax.axis_size(MP)
    peers = owners // 2
    lines = lax.axis_size("x")
    core, twin, yl, x = (lax.axis_index(name) for name in ("core", "twin", "yl", "x"))
    far = lax.axis_index("far")
    group, feats_dev, width = panels.shape[1:]
    samples = group // blocks
    feats = feats_dev * blocks
    rank = fm_proj.shape[1]
    own_feats = NF // owners
    half = peers * samples
    code_cols = feats * rank
    code_blocks = code_cols // width
    lanes = width // 2

    owned = swap(panels.reshape(blocks, samples, feats_dev, width), BATCH)
    wide = owned.transpose(1, 0, 2, 3).reshape(samples, feats, width)
    inner = jnp.einsum("snd,nk->sdk", wide, fm_proj, preferred_element_type=jnp.float32)
    codes = jnp.einsum(
        "snd,sdk->snk", wide.astype(jnp.float32), inner, precision=lax.Precision.HIGHEST
    )
    codes = codes.astype(jnp.bfloat16).reshape(samples, code_blocks, width).transpose(1, 0, 2)

    def gathered(block):
        wide_block = block.reshape(-1, block.shape[-1])
        pair = ordered(wide_block, across(wide_block, "far"), 0, far)
        pair = lax.all_gather(pair.reshape(-1, pair.shape[-1]), "x", axis=0, tiled=True)
        return pair.reshape(peers, *block.shape)

    def twin_lanes(blocked, which):
        return pick(blocked.reshape(*blocked.shape[:-1], 2, lanes), -2, which)

    def yl_blocks(blocked, which):
        lead = blocked.shape[: blocked.ndim - 3]
        split = blocked.reshape(*lead, code_blocks // 4, 2, 2, *blocked.shape[-2:])
        return pick(split, len(lead) + 1, which).reshape(*lead, code_blocks // 2, *blocked.shape[-2:])

    own = twin_lanes(codes, twin)
    from_twin = across(twin_lanes(codes, 1 - twin), "twin")
    two = jnp.stack([own, from_twin])
    from_near = across(yl_blocks(two, 1 - yl).reshape(-1, lanes), "yl")
    own_two = yl_blocks(two, yl)
    four = jnp.concatenate([own_two, from_near.reshape(own_two.shape)])

    def by_owner(rows):
        return rows.reshape(samples, owners, own_feats, width).transpose(1, 2, 0, 3)

    heads = jnp.concatenate([by_owner(wide[:, :NF]), by_owner(cotangent[0, :, :NF])], axis=1)
    heads = swap(after(heads.reshape(owners, -1, width), from_twin), MP)
    heads = heads.reshape(peers, 2, 2, own_feats, samples, width).transpose(1, 2, 3, 0, 4, 5)
    heads = heads.reshape(2, 2, own_feats, half, width)

    mine = gathered(codes)
    other = across(mine.reshape(-1, width), "core").reshape(mine.shape)
    left_mine = gathered(after(four, mine))

    normed, grad_pre = [], []
    for codes_half, index in ((mine, core), (other, 1 - core)):
        flat = codes_half.transpose(0, 2, 1, 3).reshape(half, code_cols)
        y, g = column_block(flat, mlp_weight, *pick(heads, 0, index))
        normed.append(y)
        grad_pre.append(g)
    grad_pre = jnp.concatenate(grad_pre, axis=0)
    twin_grads = across(grad_pre, "twin")
    near_grads = jnp.concatenate([across(grad_pre, "yl"), across(twin_grads, "yl")], axis=0)
    grads = jnp.concatenate([grad_pre, twin_grads], axis=0)
    left_mine = after(left_mine, twin_grads)
    left_other = across(left_mine.reshape(-1, lanes), "core").reshape(left_mine.shape)

    def product(neighbour, right):
        flat = [
            part[:, i].transpose(0, 2, 1, 3).reshape(half, code_blocks // 2 * lanes)
            for i in (neighbour, neighbour + 1)
            for part in (left_mine, left_other)
        ]
        left = jnp.concatenate(flat, axis=0)
        return jnp.einsum("sc,so->co", left, right, preferred_element_type=jnp.float32)

    term = product(0, grads) + product(2, near_grads)
    term = term.astype(jnp.bfloat16).reshape(code_blocks // 2, lanes, -1)
    mlp_grad = jnp.sum(swap(term, ("yh", "pair")).astype(jnp.float32), axis=0)

    back = jnp.stack(normed).reshape(2, own_feats, lines, 2, samples, width)
    back = after(back, twin_grads)
    back = ordered(back[0], back[1], 0, core).transpose(2, 3, 0, 1, 4, 5)
    back = cube_swap(back, 2, core, "core")
    back = cube_swap(back, 1, far, "far")
    back = after(back, term)
    for step in range(lines.bit_length() - 1):
        distance = 1 << step
        split = back.reshape(lines // distance // 2, 2, distance, *back.shape[1:])
        bit = (x >> step) & 1
        back = cube_swap(split, 1, bit, "x", distance).reshape(back.shape)
    head = back.transpose(4, 0, 1, 2, 3, 5).reshape(samples, NF, width)

    lcb = jnp.einsum("pm,qmo->qpo", compress_weight, wide, preferred_element_type=jnp.float32)
    tail, _ = normalise(lcb + wide[:, NF:].astype(jnp.float32))
    result = jnp.concatenate([head, tail.astype(jnp.bfloat16)], axis=1)
    return result[None], mlp_grad


def solution(mesh):
    fine = Mesh(mesh.devices.reshape([n for _, n in FINE]), [name for name, _ in FINE])
    in_specs = (P(MP, None, BATCH, None), P(MP, BATCH, None, None), P(), P(None, MP), P())
    out_specs = (P(MP, BATCH, None, None), P(BATCH, MP))
    return jax.shard_map(shards, mesh=fine, in_specs=in_specs, out_specs=out_specs, check_vma=False)
```

time: 254 us -> 234 us (0.921)
  waiting for transfers between devices: 164 us -> 70.9 us
  blocking collectives: 0 us -> 44.7 us
  starting transfers between devices: 58.8 us -> 83 us
  between operations: 1.1 us -> 14.7 us
  local copies, waits for them, and re-layouts: 9.02 us -> 3.69 us
  matrix products: 11.2 us -> 8.24 us
    all_to_all x4 -> x2, waiting for transfers between devices: 139 us -> 2.8 us  [swap(): return lax.all_to_all(chunks, axes, split_axis=0, concat_axis=0, tiled=True)]
    ppermute x4 -> x14, starting transfers between devices: 7.93 us -> 59 us  [across(): return lax.ppermute(array, axis, [(i, i ^ distance) for i in range(count)])]
    all_to_all x0 -> x1, blocking collectives: none -> 44.7 us  [swap(): return lax.all_to_all(chunks, axes, split_axis=0, concat_axis=0, tiled=True)]
    all_gather x0 -> x2, waiting for transfers between devices: none -> 27.1 us  [gathered(): lax.all_gather(pair.reshape(-1, pair.shape[-1]), 'x', axis=0, tiled=True)]
    all_to_all x4 -> x2, starting transfers between devices: 50.9 us -> 23.9 us  [swap(): return lax.all_to_all(chunks, axes, split_axis=0, concat_axis=0, tiled=True)]
    ppermute x4 -> x14, waiting for transfers between devices: 24.6 us -> 41 us  [across(): return lax.ppermute(array, axis, [(i, i ^ distance) for i in range(count)])]
    unnamed x11 -> x12, local copies, waits for them, and re-layouts: 3.31 us -> 0.63 us
  transfers between devices with their start and end apart: 8 -> 18, of which waited for: 5 -> 13; matrix products, arithmetic and copies ran while one was open for 7% -> 6% of each run, Pallas kernels for 0% -> 0%
where the time goes in v2:
time: 234 us; the launch traced here: 233 us
  starting transfers between devices  83 us (35%)
  waiting for transfers between devices  70.9 us (30%)
  blocking collectives  44.7 us (19%)
  between operations  14.7 us (6%)
  matrix products  8.24 us (4%)
  other arithmetic  7.81 us (3%)
  local copies, waits for them, and re-layouts  3.69 us (2%)
    ppermute x14, starting transfers between devices, across(): return lax.ppermute(array, axis, [(i, i ^ distance) for i in range(count)])  59 us
    all_to_all x1, blocking collectives, swap(): return lax.all_to_all(chunks, axes, split_axis=0, concat_axis=0, tiled=True)  44.7 us
    ppermute x14, waiting for transfers between devices, across(): return lax.ppermute(array, axis, [(i, i ^ distance) for i in range(count)])  41 us
    all_gather x2, waiting for transfers between devices, gathered(): lax.all_gather(pair.reshape(-1, pair.shape[-1]), 'x', axis=0, tiled=True)  27.1 us
    all_to_all x2, starting transfers between devices, swap(): return lax.all_to_all(chunks, axes, split_axis=0, concat_axis=0, tiled=True)  23.9 us
  transfers between devices with their start and end apart: 18, of which 13 were waited for; matrix products, arithmetic and copies ran while one was open for 6% of the time, Pallas kernels for 0%

profile of v2, /device:TPU:32, one launch (start us, length us, event | category | flops | bytes accessed | tf_op | source)
XLA Modules:
  0.0 233.1 jit_solution(9865330913036201188)
XLA Ops:
  7.2 44.7 %all_to_all.15 = bf16[32,8,8,256]{3,2,1,0:T(8,128)(2,1)S(1)} all-to-all(bf16[32,8,8,256]{3,2,1,0:T(8,128)(2,1)} %bitcast.296), channel_id=1, replica_groups=mesh['yh'=4,'yl'=2,'pair'=2,'twin'=2,'x'=8,'far'=2,'core'=2] {'yh','yl',..., dimensions={0} | all-to-all | bytes 2097152 | tf_op jit(solution)/shard_map/all_to_all | solution.py:15
  52.0 0.2 fusion.71
  52.2 0.9 fusion
  53.1 0.3 copy.54
  53.4 0.5 reshape.387
  53.9 11.9 %collective-permute-start = (bf16[128,256]{1,0:T(8,128)(2,1)S(1)}, bf16[128,256]{1,0:T(8,128)(2,1)S(1)}, u32[]{:S(2)}, u32[]{:S(2)}) collective-permute-start(bf16[128,256]{1,0:T(8,128)(2,1)S(1)} %bitcast.317), channel_id=1, source_target_pairs={{0,2},{2,0},{1,3},{3,1},{4,6},{6,4},{5,7},{7,5},{8,10},{10,8},{9,1... | collective-permute-start | bytes 196616 | tf_op jit(solution)/shard_map/ppermute | solution.py:20
  66.0 2.1 collective-permute-done
  68.2 0.7 maximum_select_fusion.6
  69.3 1.9 collective-permute-start.1
  71.2 0.8 maximum_bitcast_fusion.1
  72.0 3.0 %collective-permute-done.1 = bf16[16,8,128]{2,1,0:T(8,128)(2,1)S(1)} collective-permute-done((bf16[16,8,128]{2,1,0:T(8,128)(2,1)S(1)}, bf16[16,8,128]{2,1,0:T(8,128)(2,1)S(1)}, u32[]{:S(2)}, u32[]{:S(2)}) %collective-permute-start.1) | collective-permute-done | bytes 32800 | tf_op jit(solution)/shard_map/ppermute | solution.py:20
  75.1 12.4 %all-to-all-start.1 = ((bf16[32,32,256]{2,1,0:T(8,128)(2,1)}), bf16[32,32,256]{2,1,0:T(8,128)(2,1)S(1)}, u32[]{:S(2)}, u32[]{:S(2)}) async-start(bf16[32,32,256]{2,1,0:T(8,128)(2,1)} %maximum_bitcast_fusion.1), calls=%async_computation.1 | async-start | bytes 1048576 | tf_op jit(solution)/shard_map/all_to_all | solution.py:15
  87.6 1.9 collective-permute-start.6
  89.5 3.9 %collective-permute-done.6 = bf16[128,128]{1,0:T(8,128)(2,1)S(1)} collective-permute-done((bf16[128,128]{1,0:T(8,128)(2,1)S(1)}, bf16[128,128]{1,0:T(8,128)(2,1)S(1)}, u32[]{:S(2)}, u32[]{:S(2)}) %collective-permute-start.6) | collective-permute-done | bytes 32800 | tf_op jit(solution)/shard_map/ppermute | solution.py:20
  93.4 7.6 %collective-permute-start.7 = (bf16[256,128]{1,0:T(8,128)(2,1)S(1)}, bf16[256,128]{1,0:T(8,128)(2,1)S(1)}, u32[]{:S(2)}, u32[]{:S(2)}) collective-permute-start(bf16[256,128]{1,0:T(8,128)(2,1)S(1)} %bitcast.315), channel_id=1, source_target_pairs={{0,2},{2,0},{1,3},{3,1},{4,6},{6,4},{5,7},{7,5},{8,10},{10,8},{9,1... | collective-permute-start | bytes 196616 | tf_op jit(solution)/shard_map/ppermute | solution.py:20
  101.1 6.0 %collective-permute-done.7 = bf16[256,128]{1,0:T(8,128)(2,1)S(1)} collective-permute-done((bf16[256,128]{1,0:T(8,128)(2,1)S(1)}, bf16[256,128]{1,0:T(8,128)(2,1)S(1)}, u32[]{:S(2)}, u32[]{:S(2)}) %collective-permute-start.7) | collective-permute-done | bytes 65568 | tf_op jit(solution)/shard_map/ppermute | solution.py:20
  107.1 0.7 maximum_select_fusion.7
  107.8 2.8 %all-to-all-done.1 = bf16[32,32,256]{2,1,0:T(8,128)(2,1)S(1)} async-done(((bf16[32,32,256]{2,1,0:T(8,128)(2,1)}), bf16[32,32,256]{2,1,0:T(8,128)(2,1)S(1)}, u32[]{:S(2)}, u32[]{:S(2)}) %all-to-all-start.1) | async-done | bytes 524320 | tf_op jit(solution)/shard_map/all_to_all | solution.py:15
  110.9 4.3 %all-gather.3.cloned.1.call-done = bf16[2048,256]{1,0:T(8,128)(2,1)} async-done(((bf16[256,256]{1,0:T(8,128)(2,1)}), bf16[2048,256]{1,0:T(8,128)(2,1)}) %all-gather.3.cloned.1.call-update) | async-done | bytes 1048592 | tf_op jit(solution)/shard_map/all_gather | solution.py:97
  115.3 3.4 %fusion.79 = f32[128,512]{1,0:T(8,128)S(1)} fusion(bf16[128,4096]{1,0:T(8,128)(2,1)} %bitcast.304, bf16[4096,512]{1,0:T(8,128)(2,1)} %param.8), kind=kOutput, calls=%fused_computation.181 | convolution fusion | flops 536870912 | bytes 5505024 | tf_op jit(solution)/shard_map/dot_general | solution.py:53
  119.0 1.9 collective-permute-start.2
  121.6 2.0 collective-permute-done.2
  123.5 0.7 fusion.80
  125.3 3.5 %collective-permute-start.3 = (bf16[256,512]{1,0:T(8,128)(2,1)S(1)}, bf16[256,512]{1,0:T(8,128)(2,1)S(1)}, u32[]{:S(2)}, u32[]{:S(2)}) collective-permute-start(bf16[256,512]{1,0:T(8,128)(2,1)S(1)} %maximum_maximum_fusion.1), channel_id=1, source_target_pairs={{0,32},{32,0},{1,33},{33,1},{2,34},{34,2},{3,35},{35,3},{4,36},{36... | collective-permute-start | bytes 786440 | tf_op jit(solution)/shard_map/ppermute | solution.py:20
  128.8 0.5 fusion.78
  129.4 6.2 %collective-permute-done.3 = bf16[256,512]{1,0:T(8,128)(2,1)S(1)} collective-permute-done((bf16[256,512]{1,0:T(8,128)(2,1)S(1)}, bf16[256,512]{1,0:T(8,128)(2,1)S(1)}, u32[]{:S(2)}, u32[]{:S(2)}) %collective-permute-start.3) | collective-permute-done | bytes 262176 | tf_op jit(solution)/shard_map/ppermute | solution.py:20
  135.6 0.6 copy-done.4
  136.2 1.9 collective-permute-start.4
  138.1 22.8 %all-gather.5.cloned.1.call-done = bf16[4096,128]{1,0:T(8,128)(2,1)} async-done(((bf16[512,128]{1,0:T(8,128)(2,1)}), bf16[4096,128]{1,0:T(8,128)(2,1)}) %all-gather.5.cloned.1.call-update) | async-done | bytes 1048592 | tf_op jit(solution)/shard_map/all_gather | solution.py:97
  160.9 1.9 collective-permute-start.8
  162.9 3.4 %collective-permute-start.9 = (bf16[256,512]{1,0:T(8,128)(2,1)S(1)}, bf16[256,512]{1,0:T(8,128)(2,1)S(1)}, u32[]{:S(2)}, u32[]{:S(2)}) collective-permute-start(bf16[256,512]{1,0:T(8,128)(2,1)S(1)} %maximum_maximum_fusion.1), channel_id=1, source_target_pairs={{0,128},{128,0},{1,129},{129,1},{2,130},{130,2},{3,131},{131,3},{4... | collective-permute-start | bytes 786440 | tf_op jit(solution)/shard_map/ppermute | solution.py:20
  166.3 2.4 %collective-permute-start.10 = (bf16[256,512]{1,0:T(8,128)(2,1)}, bf16[256,512]{1,0:T(8,128)(2,1)S(1)}, u32[]{:S(2)}, u32[]{:S(2)}) collective-permute-start(bf16[256,512]{1,0:T(8,128)(2,1)} %copy-done.4), channel_id=1, source_target_pairs={{0,128},{128,0},{1,129},{129,1},{2,130},{130,2},{3,131},{131,3},{4... | collective-permute-start | bytes 786440 | tf_op jit(solution)/shard_map/ppermute | solution.py:20
  168.8 8.9 %collective-permute-start.5 = (bf16[256,256]{1,0:T(8,128)(2,1)S(1)}, bf16[256,256]{1,0:T(8,128)(2,1)S(1)}, u32[]{:S(2)}, u32[]{:S(2)}) collective-permute-start(bf16[256,256]{1,0:T(8,128)(2,1)S(1)} %bitcast.324), channel_id=1, source_target_pairs={{0,2},{2,0},{1,3},{3,1},{4,6},{6,4},{5,7},{7,5},{8,10},{10,8},{9,1... | collective-permute-start | bytes 393224 | tf_op jit(solution)/shard_map/ppermute | solution.py:20
  177.7 1.3 slice_bitcast_fusion.5
  179.0 2.4 %collective-permute-done.5 = bf16[256,256]{1,0:T(8,128)(2,1)S(1)} collective-permute-done((bf16[256,256]{1,0:T(8,128)(2,1)S(1)}, bf16[256,256]{1,0:T(8,128)(2,1)S(1)}, u32[]{:S(2)}, u32[]{:S(2)}) %collective-permute-start.5) | collective-permute-done | bytes 131104 | tf_op jit(solution)/shard_map/ppermute | solution.py:20
  181.6 0.8 fusion.1
  182.3 1.7 add_convert_fusion
  184.1 11.5 %all-to-all-start.2 = ((bf16[8,128,512]{2,1,0:T(8,128)(2,1)}), bf16[8,128,512]{2,1,0:T(8,128)(2,1)S(1)}, u32[]{:S(2)}, u32[]{:S(2)}) async-start(bf16[8,128,512]{2,1,0:T(8,128)(2,1)} %bitcast.298), calls=%async_computation.2 | async-start | bytes 2097152 | tf_op jit(solution)/shard_map/all_to_all | solution.py:15
  195.6 3.1 %collective-permute-start.11 = (bf16[256,256]{1,0:T(8,128)(2,1)S(1)}, bf16[256,256]{1,0:T(8,128)(2,1)S(1)}, u32[]{:S(2)}, u32[]{:S(2)}) collective-permute-start(bf16[256,256]{1,0:T(8,128)(2,1)S(1)} %bitcast.328), channel_id=1, source_target_pairs={{0,4},{4,0},{8,12},{12,8},{16,20},{20,16},{24,28},{28,24},{1,5},{5... | collective-permute-start | bytes 393224 | tf_op jit(solution)/shard_map/ppermute | solution.py:20
  198.7 0.6 multiply_reduce_fusion
  199.3 3.1 %collective-permute-done.11 = bf16[256,256]{1,0:T(8,128)(2,1)S(1)} collective-permute-done((bf16[256,256]{1,0:T(8,128)(2,1)S(1)}, bf16[256,256]{1,0:T(8,128)(2,1)S(1)}, u32[]{:S(2)}, u32[]{:S(2)}) %collective-permute-start.11) | collective-permute-done | bytes 131104 | tf_op jit(solution)/shard_map/ppermute | solution.py:20
  202.6 3.6 %collective-permute-start.12 = (bf16[256,256]{1,0:T(8,128)(2,1)S(1)}, bf16[256,256]{1,0:T(8,128)(2,1)S(1)}, u32[]{:S(2)}, u32[]{:S(2)}) collective-permute-start(bf16[256,256]{1,0:T(8,128)(2,1)S(1)} %bitcast.325), channel_id=1, source_target_pairs={{0,8},{4,12},{8,0},{12,4},{16,24},{20,28},{24,16},{28,20},{1,9},{5... | collective-permute-start | bytes 393224 | tf_op jit(solution)/shard_map/ppermute | solution.py:20
  206.2 5.6 %collective-permute-done.12 = bf16[256,256]{1,0:T(8,128)(2,1)S(1)} collective-permute-done((bf16[256,256]{1,0:T(8,128)(2,1)S(1)}, bf16[256,256]{1,0:T(8,128)(2,1)S(1)}, u32[]{:S(2)}, u32[]{:S(2)}) %collective-permute-start.12) | collective-permute-done | bytes 131104 | tf_op jit(solution)/shard_map/ppermute | solution.py:20
  211.8 5.0 %collective-permute-start.13 = (bf16[256,256]{1,0:T(8,128)(2,1)S(1)}, bf16[256,256]{1,0:T(8,128)(2,1)S(1)}, u32[]{:S(2)}, u32[]{:S(2)}) collective-permute-start(bf16[256,256]{1,0:T(8,128)(2,1)S(1)} %bitcast.327), channel_id=1, source_target_pairs={{0,16},{4,20},{8,24},{12,28},{16,0},{20,4},{24,8},{28,12},{1,17},{... | collective-permute-start | bytes 393224 | tf_op jit(solution)/shard_map/ppermute | solution.py:20
  216.9 0.5 multiply_convert_fusion
  217.3 6.7 %collective-permute-done.13 = bf16[256,256]{1,0:T(8,128)(2,1)S(1)} collective-permute-done((bf16[256,256]{1,0:T(8,128)(2,1)S(1)}, bf16[256,256]{1,0:T(8,128)(2,1)S(1)}, u32[]{:S(2)}, u32[]{:S(2)}) %collective-permute-start.13) | collective-permute-done | bytes 131104 | tf_op jit(solution)/shard_map/ppermute | solution.py:20
  224.4 1.0 maximum_bitcast_fusion
  225.4 0.8 convert_reduce_fusion
  (82 shorter events, 3.9 us)
Async XLA Ops:
  7.2 121.6 %copy-start = (bf16[192,256]{1,0:T(8,128)(2,1)S(1)}, bf16[192,256]{1,0:T(8,128)(2,1)}, u32[]{:S(2)}) copy-start(bf16[192,256]{1,0:T(8,128)(2,1)} %param.9) | copy-start | bytes 294916
  7.2 44.8 %copy-start.3 = (bf16[256,16]{0,1:T(8,128)(2,1)S(1)}, bf16[256,16]{0,1:T(8,128)(2,1)}, u32[]{:S(2)}) copy-start(bf16[256,16]{0,1:T(8,128)(2,1)} %param.7) | copy-start | bytes 24580
  7.2 108.1 %all-gather.3.cloned.1.call-start = ((), (), s32[]{:S(2)}) async-start(), calls=%async_computation.3 | async-start | bytes 1179648 | tf_op jit(solution)/shard_map/all_gather | solution.py:97
  52.0 13.8 %slice-start = ((bf16[1,8,256,256]{3,2,1,0:T(8,128)(2,1)}), bf16[1,8,64,256]{3,2,1,0:T(8,128)(2,1)S(1)}, s32[]{:S(2)}) async-start(bf16[1,8,256,256]{3,2,1,0:T(8,128)(2,1)} %param.6), calls=%async_computation.5 | async-start | bytes 524288 | tf_op jit(solution)/shard_map/slice | solution.py:118
  53.9 14.2 %collective-permute-start = (bf16[128,256]{1,0:T(8,128)(2,1)S(1)}, bf16[128,256]{1,0:T(8,128)(2,1)S(1)}, u32[]{:S(2)}, u32[]{:S(2)}) collective-permute-start(bf16[128,256]{1,0:T(8,128)(2,1)S(1)} %bitcast.317), channel_id=1, source_target_pairs={{0,2},{2,0},{1,3},{3,1},{4,6},{6,4},{5,7},{7,5},{8,10},{10,8},{9,1... | collective-permute-start | bytes 196616 | tf_op jit(solution)/shard_map/ppermute | solution.py:20
  69.3 5.8 %collective-permute-start.1 = (bf16[16,8,128]{2,1,0:T(8,128)(2,1)S(1)}, bf16[16,8,128]{2,1,0:T(8,128)(2,1)S(1)}, u32[]{:S(2)}, u32[]{:S(2)}) collective-permute-start(bf16[16,8,128]{2,1,0:T(8,128)(2,1)S(1)} %get-tuple-element.63), channel_id=1, source_target_pairs={{0,32},{32,0},{1,33},{33,1},{2,34},{34,2},{3,35},{35,3},{4,36},{36... | collective-permute-start | bytes 98312 | tf_op jit(solution)/shard_map/ppermute | solution.py:20
  75.1 35.5 %all-to-all-start.1 = ((bf16[32,32,256]{2,1,0:T(8,128)(2,1)}), bf16[32,32,256]{2,1,0:T(8,128)(2,1)S(1)}, u32[]{:S(2)}, u32[]{:S(2)}) async-start(bf16[32,32,256]{2,1,0:T(8,128)(2,1)} %maximum_bitcast_fusion.1), calls=%async_computation.1 | async-start | bytes 1048576 | tf_op jit(solution)/shard_map/all_to_all | solution.py:15
  87.5 73.4 %all-gather.5.cloned.1.call-start = ((), (), s32[]{:S(2)}) async-start(), calls=%async_computation.4 | async-start | bytes 1179648 | tf_op jit(solution)/shard_map/all_gather | solution.py:97
  87.6 5.8 %collective-permute-start.6 = (bf16[128,128]{1,0:T(8,128)(2,1)S(1)}, bf16[128,128]{1,0:T(8,128)(2,1)S(1)}, u32[]{:S(2)}, u32[]{:S(2)}) collective-permute-start(bf16[128,128]{1,0:T(8,128)(2,1)S(1)} %bitcast.334), channel_id=1, source_target_pairs={{0,128},{128,0},{1,129},{129,1},{2,130},{130,2},{3,131},{131,3},{4... | collective-permute-start | bytes 98312 | tf_op jit(solution)/shard_map/ppermute | solution.py:20
  93.4 13.7 %collective-permute-start.7 = (bf16[256,128]{1,0:T(8,128)(2,1)S(1)}, bf16[256,128]{1,0:T(8,128)(2,1)S(1)}, u32[]{:S(2)}, u32[]{:S(2)}) collective-permute-start(bf16[256,128]{1,0:T(8,128)(2,1)S(1)} %bitcast.315), channel_id=1, source_target_pairs={{0,2},{2,0},{1,3},{3,1},{4,6},{6,4},{5,7},{7,5},{8,10},{10,8},{9,1... | collective-permute-start | bytes 196616 | tf_op jit(solution)/shard_map/ppermute | solution.py:20
  115.2 3.7 %copy-start.2 = (bf16[2048,256]{1,0:T(8,128)(2,1)S(1)}, bf16[2048,256]{1,0:T(8,128)(2,1)}, u32[]{:S(2)}) copy-start(bf16[2048,256]{1,0:T(8,128)(2,1)} %all-gather.3.cloned.1.call-done) | copy-start | bytes 3145732
  115.3 8.3 %copy-start.1 = (bf16[4096,512]{1,0:T(8,128)(2,1)S(1)}, bf16[4096,512]{1,0:T(8,128)(2,1)}, u32[]{:S(2)}) copy-start(bf16[4096,512]{1,0:T(8,128)(2,1)} %param.8) | copy-start | bytes 12582916
  119.0 4.6 %collective-permute-start.2 = (bf16[2048,256]{1,0:T(8,128)(2,1)S(1)}, bf16[2048,256]{1,0:T(8,128)(2,1)S(1)}, u32[]{:S(2)}, u32[]{:S(2)}) collective-permute-start(bf16[2048,256]{1,0:T(8,128)(2,1)S(1)} %copy-done.2), channel_id=1, source_target_pairs={{0,1},{1,0},{2,3},{3,2},{4,5},{5,4},{6,7},{7,6},{8,9},{9,8},{10,11... | collective-permute-start | bytes 3145736 | tf_op jit(solution)/shard_map/ppermute | solution.py:20
  125.3 10.2 %collective-permute-start.3 = (bf16[256,512]{1,0:T(8,128)(2,1)S(1)}, bf16[256,512]{1,0:T(8,128)(2,1)S(1)}, u32[]{:S(2)}, u32[]{:S(2)}) collective-permute-start(bf16[256,512]{1,0:T(8,128)(2,1)S(1)} %maximum_maximum_fusion.1), channel_id=1, source_target_pairs={{0,32},{32,0},{1,33},{33,1},{2,34},{34,2},{3,35},{35,3},{4,36},{36... | collective-permute-start | bytes 786440 | tf_op jit(solution)/shard_map/ppermute | solution.py:20
  135.5 0.7 copy-start.4
  136.2 32.5 %collective-permute-start.4 = (bf16[256,256]{1,0:T(8,128)(2,1)S(1)}, bf16[256,256]{1,0:T(8,128)(2,1)S(1)}, u32[]{:S(2)}, u32[]{:S(2)}) collective-permute-start(bf16[256,256]{1,0:T(8,128)(2,1)S(1)} %bitcast.326), channel_id=1, source_target_pairs={{0,1},{1,0},{2,3},{3,2},{4,5},{5,4},{6,7},{7,6},{8,9},{9,8},{10,11... | collective-permute-start | bytes 393224 | tf_op jit(solution)/shard_map/ppermute | solution.py:20
  160.9 20.5 %collective-permute-start.8 = (bf16[4096,128]{1,0:T(8,128)(2,1)}, bf16[4096,128]{1,0:T(8,128)(2,1)S(1)}, u32[]{:S(2)}, u32[]{:S(2)}) collective-permute-start(bf16[4096,128]{1,0:T(8,128)(2,1)} %all-gather.5.cloned.1.call-done), channel_id=1, source_target_pairs={{0,1},{1,0},{2,3},{3,2},{4,5},{5,4},{6,7},{7,6},{8,9},{9,8},{10,11... | collective-permute-start | bytes 3145736 | tf_op jit(solution)/shard_map/ppermute | solution.py:20
  162.9 19.5 %collective-permute-start.9 = (bf16[256,512]{1,0:T(8,128)(2,1)S(1)}, bf16[256,512]{1,0:T(8,128)(2,1)S(1)}, u32[]{:S(2)}, u32[]{:S(2)}) collective-permute-start(bf16[256,512]{1,0:T(8,128)(2,1)S(1)} %maximum_maximum_fusion.1), channel_id=1, source_target_pairs={{0,128},{128,0},{1,129},{129,1},{2,130},{130,2},{3,131},{131,3},{4... | collective-permute-start | bytes 786440 | tf_op jit(solution)/shard_map/ppermute | solution.py:20
  166.3 16.1 %collective-permute-start.10 = (bf16[256,512]{1,0:T(8,128)(2,1)}, bf16[256,512]{1,0:T(8,128)(2,1)S(1)}, u32[]{:S(2)}, u32[]{:S(2)}) collective-permute-start(bf16[256,512]{1,0:T(8,128)(2,1)} %copy-done.4), channel_id=1, source_target_pairs={{0,128},{128,0},{1,129},{129,1},{2,130},{130,2},{3,131},{131,3},{4... | collective-permute-start | bytes 786440 | tf_op jit(solution)/shard_map/ppermute | solution.py:20
  168.8 12.7 %copy-start.5 = (bf16[256,512]{1,0:T(8,128)(2,1)S(1)}, bf16[256,512]{1,0:T(8,128)(2,1)}, u32[]{:S(2)}) copy-start(bf16[256,512]{1,0:T(8,128)(2,1)} %copy-done.4) | copy-start | bytes 786436
  168.8 12.6 %collective-permute-start.5 = (bf16[256,256]{1,0:T(8,128)(2,1)S(1)}, bf16[256,256]{1,0:T(8,128)(2,1)S(1)}, u32[]{:S(2)}, u32[]{:S(2)}) collective-permute-start(bf16[256,256]{1,0:T(8,128)(2,1)S(1)} %bitcast.324), channel_id=1, source_target_pairs={{0,2},{2,0},{1,3},{3,1},{4,6},{6,4},{5,7},{7,5},{8,10},{10,8},{9,1... | collective-permute-start | bytes 393224 | tf_op jit(solution)/shard_map/ppermute | solution.py:20
  184.1 41.3 %all-to-all-start.2 = ((bf16[8,128,512]{2,1,0:T(8,128)(2,1)}), bf16[8,128,512]{2,1,0:T(8,128)(2,1)S(1)}, u32[]{:S(2)}, u32[]{:S(2)}) async-start(bf16[8,128,512]{2,1,0:T(8,128)(2,1)} %bitcast.298), calls=%async_computation.2 | async-start | bytes 2097152 | tf_op jit(solution)/shard_map/all_to_all | solution.py:15
  195.6 6.9 %collective-permute-start.11 = (bf16[256,256]{1,0:T(8,128)(2,1)S(1)}, bf16[256,256]{1,0:T(8,128)(2,1)S(1)}, u32[]{:S(2)}, u32[]{:S(2)}) collective-permute-start(bf16[256,256]{1,0:T(8,128)(2,1)S(1)} %bitcast.328), channel_id=1, source_target_pairs={{0,4},{4,0},{8,12},{12,8},{16,20},{20,16},{24,28},{28,24},{1,5},{5... | collective-permute-start | bytes 393224 | tf_op jit(solution)/shard_map/ppermute | solution.py:20
  202.6 9.2 %collective-permute-start.12 = (bf16[256,256]{1,0:T(8,128)(2,1)S(1)}, bf16[256,256]{1,0:T(8,128)(2,1)S(1)}, u32[]{:S(2)}, u32[]{:S(2)}) collective-permute-start(bf16[256,256]{1,0:T(8,128)(2,1)S(1)} %bitcast.325), channel_id=1, source_target_pairs={{0,8},{4,12},{8,0},{12,4},{16,24},{20,28},{24,16},{28,20},{1,9},{5... | collective-permute-start | bytes 393224 | tf_op jit(solution)/shard_map/ppermute | solution.py:20
  211.8 12.2 %collective-permute-start.13 = (bf16[256,256]{1,0:T(8,128)(2,1)S(1)}, bf16[256,256]{1,0:T(8,128)(2,1)S(1)}, u32[]{:S(2)}, u32[]{:S(2)}) collective-permute-start(bf16[256,256]{1,0:T(8,128)(2,1)S(1)} %bitcast.327), channel_id=1, source_target_pairs={{0,16},{4,20},{8,24},{12,28},{16,0},{20,4},{24,8},{28,12},{1,17},{... | collective-permute-start | bytes 393224 | tf_op jit(solution)/shard_map/ppermute | solution.py:20
Sparse Core Ops, SparseCore 0:
  69.0 46.2 all-gather.2
  117.9 42.9 all-gather.4

commit v3 on v2

--- a/solution.py
+++ b/solution.py
@@ -91,12 +91,6 @@
     )
     codes = codes.astype(jnp.bfloat16).reshape(samples, code_blocks, width).transpose(1, 0, 2)
 
-    def gathered(block):
-        wide_block = block.reshape(-1, block.shape[-1])
-        pair = ordered(wide_block, across(wide_block, "far"), 0, far)
-        pair = lax.all_gather(pair.reshape(-1, pair.shape[-1]), "x", axis=0, tiled=True)
-        return pair.reshape(peers, *block.shape)
-
     def twin_lanes(blocked, which):
         return pick(blocked.reshape(*blocked.shape[:-1], 2, lanes), -2, which)
 
@@ -105,41 +99,72 @@
         split = blocked.reshape(*lead, code_blocks // 4, 2, 2, *blocked.shape[-2:])
         return pick(split, len(lead) + 1, which).reshape(*lead, code_blocks // 2, *blocked.shape[-2:])
 
-    own = twin_lanes(codes, twin)
-    from_twin = across(twin_lanes(codes, 1 - twin), "twin")
-    two = jnp.stack([own, from_twin])
-    from_near = across(yl_blocks(two, 1 - yl).reshape(-1, lanes), "yl")
-    own_two = yl_blocks(two, yl)
-    four = jnp.concatenate([own_two, from_near.reshape(own_two.shape)])
+    def x_swap(buffer, step):
+        distance = 1 << step
+        split = buffer.reshape(lines // distance // 2, 2, distance, *buffer.shape[1:])
+        return cube_swap(split, 1, (x >> step) & 1, "x", distance).reshape(buffer.shape)
 
     def by_owner(rows):
-        return rows.reshape(samples, owners, own_feats, width).transpose(1, 2, 0, 3)
+        rows = rows.reshape(samples, owners, own_feats, width).transpose(1, 2, 0, 3)
+        return rows.reshape(lines, 2, 2, own_feats, samples, width)
 
-    heads = jnp.concatenate([by_owner(wide[:, :NF]), by_owner(cotangent[0, :, :NF])], axis=1)
-    heads = swap(after(heads.reshape(owners, -1, width), from_twin), MP)
-    heads = heads.reshape(peers, 2, 2, own_feats, samples, width).transpose(1, 2, 3, 0, 4, 5)
-    heads = heads.reshape(2, 2, own_feats, half, width)
+    steps = range(lines.bit_length() - 1)
+    head_grads = x_swap(by_owner(cotangent[0, :, :NF]), 0)
 
-    mine = gathered(codes)
-    other = across(mine.reshape(-1, width), "core").reshape(mine.shape)
-    left_mine = gathered(after(four, mine))
+    code_rows = code_blocks * samples
+    head_rows = own_feats * samples
+    parcel = jnp.broadcast_to(codes.reshape(-1, width), (peers, code_rows, width))
+    heads = by_owner(wide[:, :NF])
+    heads = jnp.where(core == 0, heads, heads[:, :, ::-1]).reshape(peers, 2 * head_rows, width)
+    parcel = jnp.concatenate([parcel, heads], axis=1)
+    parcel_mine = swap(parcel, ("x", "far"))
+    parcel_other = across(parcel_mine.reshape(-1, width), "core").reshape(parcel_mine.shape)
+    mine, other = (
+        p[:, :code_rows].reshape(peers, code_blocks, samples, width)
+        for p in (parcel_mine, parcel_other)
+    )
+    rows_mine = parcel_mine[:, code_rows : code_rows + head_rows]
+    rows_other = parcel_other[:, code_rows + head_rows :]
+
+    head_grads = after(head_grads, parcel)
+    for step in steps[1:]:
+        head_grads = x_swap(head_grads, step)
+    head_grads = cube_swap(head_grads, 1, far, "far").reshape(peers, 2, head_rows, width)
+    grads_mine = pick(head_grads, 1, core)
+    grads_other = after(pick(head_grads, 1, 1 - core), parcel_mine)
+    grads_other = across(grads_other.reshape(-1, width), "core").reshape(grads_mine.shape)
+
+    def tall(rows):
+        rows = rows.reshape(peers, own_feats, samples, width).transpose(1, 0, 2, 3)
+        return rows.reshape(own_feats, half, width)
+
+    def exchanged(blocked, axis):
+        return across(blocked.reshape(-1, lanes), axis).reshape(blocked.shape)
+
+    own_codes = twin_lanes(mine, twin)
+    twin_codes = exchanged(twin_lanes(mine, 1 - twin), "twin")
+    near_codes = exchanged(yl_blocks(own_codes, 1 - yl), "yl")
 
     normed, grad_pre = [], []
-    for codes_half, index in ((mine, core), (other, 1 - core)):
-        flat = codes_half.transpose(0, 2, 1, 3).reshape(half, code_cols)
-        y, g = column_block(flat, mlp_weight, *pick(heads, 0, index))
+    for part, rows, cots in ((mine, rows_mine, grads_mine), (other, rows_other, grads_other)):
+        flat = part.transpose(0, 2, 1, 3).reshape(half, code_cols)
+        y, g = column_block(flat, mlp_weight, tall(rows), tall(cots))
         normed.append(y)
         grad_pre.append(g)
     grad_pre = jnp.concatenate(grad_pre, axis=0)
     twin_grads = across(grad_pre, "twin")
     near_grads = jnp.concatenate([across(grad_pre, "yl"), across(twin_grads, "yl")], axis=0)
     grads = jnp.concatenate([grad_pre, twin_grads], axis=0)
-    left_mine = after(left_mine, twin_grads)
-    left_other = across(left_mine.reshape(-1, lanes), "core").reshape(left_mine.shape)
+
+    twin_codes = after(twin_codes, grad_pre)
+    near_twin = exchanged(yl_blocks(twin_codes, 1 - yl), "yl")
+    others = jnp.stack([yl_blocks(twin_codes, yl), near_codes, near_twin])
+    left_mine = (yl_blocks(own_codes, yl), *others)
+    left_other = (yl_blocks(twin_lanes(other, twin), yl), *exchanged(others, "core"))
 
     def product(neighbour, right):
         flat = [
-            part[:, i].transpose(0, 2, 1, 3).reshape(half, code_blocks // 2 * lanes)
+            part[i].transpose(0, 2, 1, 3).reshape(half, code_blocks // 2 * lanes)
             for i in (neighbour, neighbour + 1)
             for part in (left_mine, left_other)
         ]
@@ -156,11 +181,8 @@
     back = cube_swap(back, 2, core, "core")
     back = cube_swap(back, 1, far, "far")
     back = after(back, term)
-    for step in range(lines.bit_length() - 1):
-        distance = 1 << step
-        split = back.reshape(lines // distance // 2, 2, distance, *back.shape[1:])
-        bit = (x >> step) & 1
-        back = cube_swap(split, 1, bit, "x", distance).reshape(back.shape)
+    for step in steps:
+        back = x_swap(back, step)
     head = back.transpose(4, 0, 1, 2, 3, 5).reshape(samples, NF, width)
 
     lcb = jnp.einsum("pm,qmo->qpo", compress_weight, wide, preferred_element_type=jnp.float32)

time: 234 us -> 245 us (1.047)
  the two profiles are of different devices: /device:TPU:32 before, /device:TPU:94 now
where the time goes in v3:
time: 245 us; the launch traced here: 244 us
  waiting for transfers between devices  117 us (48%)
  starting transfers between devices  102 us (42%)
  matrix products  10.1 us (4%)
  local copies, waits for them, and re-layouts  7.17 us (3%)
  other arithmetic  6.96 us (3%)
    ppermute x18, waiting for transfers between devices, across(): return lax.ppermute(array, axis, [(i, i ^ distance) for i in range(count)])  91.5 us
    ppermute x18, starting transfers between devices, across(): return lax.ppermute(array, axis, [(i, i ^ distance) for i in range(count)])  59.7 us
    all_to_all x3, starting transfers between devices, swap(): return lax.all_to_all(chunks, axes, split_axis=0, concat_axis=0, tiled=True)  42.3 us
    all_to_all x3, waiting for transfers between devices, swap(): return lax.all_to_all(chunks, axes, split_axis=0, concat_axis=0, tiled=True)  25.3 us
    dot_general x2, matrix products, column_block(): pre = jnp.dot(codes, weight, preferred_element_type=jnp.float32)  5.93 us
  transfers between devices with their start and end apart: 21, of which 13 were waited for; matrix products, arithmetic and copies ran while one was open for 5% of the time, Pallas kernels for 0%

profile of v3, /device:TPU:94, one launch (start us, length us, event | category | flops | bytes accessed | tf_op | source)
XLA Modules:
  0.0 244.4 jit_solution(14576714037031190670)
XLA Ops:
  0.7 15.5 %all-to-all-start = ((bf16[32,8,8,256]{3,2,1,0:T(8,128)(2,1)}), bf16[32,8,8,256]{3,2,1,0:T(8,128)(2,1)S(1)}, u32[]{:S(2)}, u32[]{:S(2)}) async-start(bf16[32,8,8,256]{3,2,1,0:T(8,128)(2,1)} %bitcast.332), calls=%async_computation | async-start | bytes 2097152 | tf_op jit(solution)/shard_map/all_to_all | solution.py:15
  16.3 25.3 %all-to-all-done = bf16[32,8,8,256]{3,2,1,0:T(8,128)(2,1)S(1)} async-done(((bf16[32,8,8,256]{3,2,1,0:T(8,128)(2,1)}), bf16[32,8,8,256]{3,2,1,0:T(8,128)(2,1)S(1)}, u32[]{:S(2)}, u32[]{:S(2)}) %all-to-all-start) | async-done | bytes 1048608 | tf_op jit(solution)/shard_map/all_to_all | solution.py:15
  42.3 0.9 fusion
  44.2 1.2 pad_maximum_fusion
  45.4 16.5 %all-to-all-start.1 = ((bf16[16,160,256]{2,1,0:T(8,128)(2,1)}), bf16[16,160,256]{2,1,0:T(8,128)(2,1)}, u32[]{:S(2)}, u32[]{:S(2)}) async-start(bf16[16,160,256]{2,1,0:T(8,128)(2,1)} %pad_maximum_fusion), calls=%async_computation.1 | async-start | bytes 2621440 | tf_op jit(solution)/shard_map/all_to_all | solution.py:15
  61.9 3.4 %collective-permute-start.1 = (bf16[256,256]{1,0:T(8,128)(2,1)S(1)}, bf16[256,256]{1,0:T(8,128)(2,1)S(1)}, u32[]{:S(2)}, u32[]{:S(2)}) collective-permute-start(bf16[256,256]{1,0:T(8,128)(2,1)S(1)} %bitcast.374), channel_id=1, source_target_pairs={{0,4},{4,0},{8,12},{12,8},{16,20},{20,16},{24,28},{28,24},{1,5},{5... | collective-permute-start | bytes 393224 | tf_op jit(solution)/shard_map/ppermute | solution.py:20
  65.3 33.1 %collective-permute-done.1 = bf16[256,256]{1,0:T(8,128)(2,1)S(1)} collective-permute-done((bf16[256,256]{1,0:T(8,128)(2,1)S(1)}, bf16[256,256]{1,0:T(8,128)(2,1)S(1)}, u32[]{:S(2)}, u32[]{:S(2)}) %collective-permute-start.1) | collective-permute-done | bytes 131104 | tf_op jit(solution)/shard_map/ppermute | solution.py:20
  98.5 1.9 collective-permute-start.2
  100.4 8.6 %collective-permute-done.2 = bf16[256,256]{1,0:T(8,128)(2,1)S(1)} collective-permute-done((bf16[256,256]{1,0:T(8,128)(2,1)S(1)}, bf16[256,256]{1,0:T(8,128)(2,1)S(1)}, u32[]{:S(2)}, u32[]{:S(2)}) %collective-permute-start.2) | collective-permute-done | bytes 131104 | tf_op jit(solution)/shard_map/ppermute | solution.py:20
  109.1 1.9 collective-permute-start.3
  111.0 8.8 %collective-permute-done.3 = bf16[256,256]{1,0:T(8,128)(2,1)S(1)} collective-permute-done((bf16[256,256]{1,0:T(8,128)(2,1)S(1)}, bf16[256,256]{1,0:T(8,128)(2,1)S(1)}, u32[]{:S(2)}, u32[]{:S(2)}) %collective-permute-start.3) | collective-permute-done | bytes 131104 | tf_op jit(solution)/shard_map/ppermute | solution.py:20
  119.9 8.8 %collective-permute-start.4 = (bf16[256,256]{1,0:T(8,128)(2,1)S(1)}, bf16[256,256]{1,0:T(8,128)(2,1)S(1)}, u32[]{:S(2)}, u32[]{:S(2)}) collective-permute-start(bf16[256,256]{1,0:T(8,128)(2,1)S(1)} %bitcast.376), channel_id=1, source_target_pairs={{0,2},{2,0},{1,3},{3,1},{4,6},{6,4},{5,7},{7,5},{8,10},{10,8},{9,1... | collective-permute-start | bytes 393224 | tf_op jit(solution)/shard_map/ppermute | solution.py:20
  128.7 0.5 fusion.76
  129.3 2.6 %collective-permute-done.4 = bf16[256,256]{1,0:T(8,128)(2,1)S(1)} collective-permute-done((bf16[256,256]{1,0:T(8,128)(2,1)S(1)}, bf16[256,256]{1,0:T(8,128)(2,1)S(1)}, u32[]{:S(2)}, u32[]{:S(2)}) %collective-permute-start.4) | collective-permute-done | bytes 131104 | tf_op jit(solution)/shard_map/ppermute | solution.py:20
  132.2 1.9 collective-permute-start.5
  134.2 2.4 collective-permute-start
  136.6 1.5 slice_bitcast_fusion.7
  138.1 3.0 %fusion.77 = f32[128,512]{1,0:T(8,128)S(1)} fusion(bf16[128,4096]{1,0:T(8,128)(2,1)S(1)} %bitcast.317, bf16[4096,512]{1,0:T(8,128)(2,1)} %param.8), kind=kOutput, calls=%fused_computation.184 | convolution fusion | flops 536870912 | bytes 5505024 | tf_op jit(solution)/shard_map/dot_general | solution.py:53
  141.1 0.9 slice_bitcast_fusion.1
  143.2 0.9 slice_bitcast_fusion
  144.1 1.6 slice_bitcast_fusion.6
  145.8 3.0 %fusion.78 = f32[128,512]{1,0:T(8,128)S(1)} fusion(bf16[128,4096]{1,0:T(8,128)(2,1)S(1)} %bitcast.316, bf16[4096,512]{1,0:T(8,128)(2,1)} %param.8), kind=kOutput, calls=%fused_computation.185 | convolution fusion | flops 536870912 | bytes 5505024 | tf_op jit(solution)/shard_map/dot_general | solution.py:53
  149.6 1.9 collective-permute-start.6
  151.7 3.9 %collective-permute-start.9 = (bf16[2048,128]{1,0:T(8,128)(2,1)S(1)}, bf16[2048,128]{1,0:T(8,128)(2,1)S(1)}, u32[]{:S(2)}, u32[]{:S(2)}) collective-permute-start(bf16[2048,128]{1,0:T(8,128)(2,1)S(1)} %bitcast.342), channel_id=1, source_target_pairs={{0,32},{32,0},{1,33},{33,1},{2,34},{34,2},{3,35},{35,3},{4,36},{36... | collective-permute-start | bytes 1572872 | tf_op jit(solution)/shard_map/ppermute | solution.py:20
  155.7 3.5 %collective-permute-start.10 = (bf16[1024,128]{1,0:T(8,128)(2,1)S(1)}, bf16[1024,128]{1,0:T(8,128)(2,1)S(1)}, u32[]{:S(2)}, u32[]{:S(2)}) collective-permute-start(bf16[1024,128]{1,0:T(8,128)(2,1)S(1)} %bitcast.344), channel_id=1, source_target_pairs={{0,128},{128,0},{1,129},{129,1},{2,130},{130,2},{3,131},{131,3},{4... | collective-permute-start | bytes 786440 | tf_op jit(solution)/shard_map/ppermute | solution.py:20
  159.2 1.5 collective-permute-done.6
  160.7 10.3 %collective-permute-done.9 = bf16[2048,128]{1,0:T(8,128)(2,1)S(1)} collective-permute-done((bf16[2048,128]{1,0:T(8,128)(2,1)S(1)}, bf16[2048,128]{1,0:T(8,128)(2,1)S(1)}, u32[]{:S(2)}, u32[]{:S(2)}) %collective-permute-start.9) | collective-permute-done | bytes 524320 | tf_op jit(solution)/shard_map/ppermute | solution.py:20
  171.0 3.5 %collective-permute-start.11 = (bf16[1024,128]{1,0:T(8,128)(2,1)S(1)}, bf16[1024,128]{1,0:T(8,128)(2,1)S(1)}, u32[]{:S(2)}, u32[]{:S(2)}) collective-permute-start(bf16[1024,128]{1,0:T(8,128)(2,1)S(1)} %bitcast.345), channel_id=1, source_target_pairs={{0,128},{128,0},{1,129},{129,1},{2,130},{130,2},{3,131},{131,3},{4... | collective-permute-start | bytes 786440 | tf_op jit(solution)/shard_map/ppermute | solution.py:20
  174.6 1.9 collective-permute-start.7
  176.5 3.7 %collective-permute-done.11 = bf16[1024,128]{1,0:T(8,128)(2,1)S(1)} collective-permute-done((bf16[1024,128]{1,0:T(8,128)(2,1)S(1)}, bf16[1024,128]{1,0:T(8,128)(2,1)S(1)}, u32[]{:S(2)}, u32[]{:S(2)}) %collective-permute-start.11) | collective-permute-done | bytes 262176 | tf_op jit(solution)/shard_map/ppermute | solution.py:20
  180.4 1.9 collective-permute-start.12
  182.3 3.5 %collective-permute-start.13 = (bf16[256,512]{1,0:T(8,128)(2,1)S(1)}, bf16[256,512]{1,0:T(8,128)(2,1)S(1)}, u32[]{:S(2)}, u32[]{:S(2)}) collective-permute-start(bf16[256,512]{1,0:T(8,128)(2,1)S(1)} %maximum_maximum_fusion.1), channel_id=1, source_target_pairs={{0,128},{128,0},{1,129},{129,1},{2,130},{130,2},{3,131},{131,3},{4... | collective-permute-start | bytes 786440 | tf_op jit(solution)/shard_map/ppermute | solution.py:20
  185.9 7.2 %collective-permute-start.8 = (bf16[256,256]{1,0:T(8,128)(2,1)S(1)}, bf16[256,256]{1,0:T(8,128)(2,1)S(1)}, u32[]{:S(2)}, u32[]{:S(2)}) collective-permute-start(bf16[256,256]{1,0:T(8,128)(2,1)S(1)} %bitcast.373), channel_id=1, source_target_pairs={{0,2},{2,0},{1,3},{3,1},{4,6},{6,4},{5,7},{7,5},{8,10},{10,8},{9,1... | collective-permute-start | bytes 393224 | tf_op jit(solution)/shard_map/ppermute | solution.py:20
  193.1 2.9 %collective-permute-start.14 = (bf16[256,512]{1,0:T(8,128)(2,1)S(1)}, bf16[256,512]{1,0:T(8,128)(2,1)S(1)}, u32[]{:S(2)}, u32[]{:S(2)}) collective-permute-start(bf16[256,512]{1,0:T(8,128)(2,1)S(1)} %collective-permute-done.6), channel_id=1, source_target_pairs={{0,128},{128,0},{1,129},{129,1},{2,130},{130,2},{3,131},{131,3},{4... | collective-permute-start | bytes 786440 | tf_op jit(solution)/shard_map/ppermute | solution.py:20
  196.0 1.4 collective-permute-done.8
  197.5 0.8 fusion.1
  198.3 4.9 %collective-permute-done.14 = bf16[256,512]{1,0:T(8,128)(2,1)S(1)} collective-permute-done((bf16[256,512]{1,0:T(8,128)(2,1)S(1)}, bf16[256,512]{1,0:T(8,128)(2,1)S(1)}, u32[]{:S(2)}, u32[]{:S(2)}) %collective-permute-start.14) | collective-permute-done | bytes 262176 | tf_op jit(solution)/shard_map/ppermute | solution.py:20
  203.2 1.7 add_convert_fusion
  204.9 10.3 %all-to-all-start.2 = ((bf16[8,128,512]{2,1,0:T(8,128)(2,1)}), bf16[8,128,512]{2,1,0:T(8,128)(2,1)S(1)}, u32[]{:S(2)}, u32[]{:S(2)}) async-start(bf16[8,128,512]{2,1,0:T(8,128)(2,1)} %bitcast.333), calls=%async_computation.2 | async-start | bytes 2097152 | tf_op jit(solution)/shard_map/all_to_all | solution.py:15
  215.2 3.7 %collective-permute-start.15 = (bf16[256,256]{1,0:T(8,128)(2,1)S(1)}, bf16[256,256]{1,0:T(8,128)(2,1)S(1)}, u32[]{:S(2)}, u32[]{:S(2)}) collective-permute-start(bf16[256,256]{1,0:T(8,128)(2,1)S(1)} %bitcast.377), channel_id=1, source_target_pairs={{0,4},{4,0},{8,12},{12,8},{16,20},{20,16},{24,28},{28,24},{1,5},{5... | collective-permute-start | bytes 393224 | tf_op jit(solution)/shard_map/ppermute | solution.py:20
  218.9 0.6 multiply_reduce_fusion
  219.5 2.6 %collective-permute-done.15 = bf16[256,256]{1,0:T(8,128)(2,1)S(1)} collective-permute-done((bf16[256,256]{1,0:T(8,128)(2,1)S(1)}, bf16[256,256]{1,0:T(8,128)(2,1)S(1)}, u32[]{:S(2)}, u32[]{:S(2)}) %collective-permute-start.15) | collective-permute-done | bytes 131104 | tf_op jit(solution)/shard_map/ppermute | solution.py:20
  222.2 3.1 %collective-permute-start.16 = (bf16[256,256]{1,0:T(8,128)(2,1)S(1)}, bf16[256,256]{1,0:T(8,128)(2,1)S(1)}, u32[]{:S(2)}, u32[]{:S(2)}) collective-permute-start(bf16[256,256]{1,0:T(8,128)(2,1)S(1)} %bitcast.378), channel_id=1, source_target_pairs={{0,8},{4,12},{8,0},{12,4},{16,24},{20,28},{24,16},{28,20},{1,9},{5... | collective-permute-start | bytes 393224 | tf_op jit(solution)/shard_map/ppermute | solution.py:20
  225.2 6.1 %collective-permute-done.16 = bf16[256,256]{1,0:T(8,128)(2,1)S(1)} collective-permute-done((bf16[256,256]{1,0:T(8,128)(2,1)S(1)}, bf16[256,256]{1,0:T(8,128)(2,1)S(1)}, u32[]{:S(2)}, u32[]{:S(2)}) %collective-permute-start.16) | collective-permute-done | bytes 131104 | tf_op jit(solution)/shard_map/ppermute | solution.py:20
  231.4 2.4 collective-permute-start.17
  234.3 7.8 %collective-permute-done.17 = bf16[256,256]{1,0:T(8,128)(2,1)S(1)} collective-permute-done((bf16[256,256]{1,0:T(8,128)(2,1)S(1)}, bf16[256,256]{1,0:T(8,128)(2,1)S(1)}, u32[]{:S(2)}, u32[]{:S(2)}) %collective-permute-start.17) | collective-permute-done | bytes 131104 | tf_op jit(solution)/shard_map/ppermute | solution.py:20
  242.5 1.0 maximum_bitcast_fusion
  243.6 0.8 convert_reduce_fusion
  (85 shorter events, 5.8 us)
Async XLA Ops:
  0.6 128.1 %copy-start = (bf16[192,256]{1,0:T(8,128)(2,1)S(1)}, bf16[192,256]{1,0:T(8,128)(2,1)}, u32[]{:S(2)}) copy-start(bf16[192,256]{1,0:T(8,128)(2,1)} %param.9) | copy-start | bytes 294916
  0.6 15.5 %slice-start = ((bf16[1,8,256,256]{3,2,1,0:T(8,128)(2,1)}), bf16[1,8,64,256]{3,2,1,0:T(8,128)(2,1)S(1)}, s32[]{:S(2)}) async-start(bf16[1,8,256,256]{3,2,1,0:T(8,128)(2,1)} %param.6), calls=%async_computation.3 | async-start | bytes 524288 | tf_op jit(solution)/shard_map/slice | solution.py:112
  0.7 41.0 %all-to-all-start = ((bf16[32,8,8,256]{3,2,1,0:T(8,128)(2,1)}), bf16[32,8,8,256]{3,2,1,0:T(8,128)(2,1)S(1)}, u32[]{:S(2)}, u32[]{:S(2)}) async-start(bf16[32,8,8,256]{3,2,1,0:T(8,128)(2,1)} %bitcast.332), calls=%async_computation | async-start | bytes 2097152 | tf_op jit(solution)/shard_map/all_to_all | solution.py:15
  16.1 25.9 %copy-start.1 = (bf16[256,16]{0,1:T(8,128)(2,1)S(1)}, bf16[256,16]{0,1:T(8,128)(2,1)}, u32[]{:S(2)}) copy-start(bf16[256,16]{0,1:T(8,128)(2,1)} %param.7) | copy-start | bytes 24580
  45.4 86.9 %all-to-all-start.1 = ((bf16[16,160,256]{2,1,0:T(8,128)(2,1)}), bf16[16,160,256]{2,1,0:T(8,128)(2,1)}, u32[]{:S(2)}, u32[]{:S(2)}) async-start(bf16[16,160,256]{2,1,0:T(8,128)(2,1)} %pad_maximum_fusion), calls=%async_computation.1 | async-start | bytes 2621440 | tf_op jit(solution)/shard_map/all_to_all | solution.py:15
  61.9 36.5 %collective-permute-start.1 = (bf16[256,256]{1,0:T(8,128)(2,1)S(1)}, bf16[256,256]{1,0:T(8,128)(2,1)S(1)}, u32[]{:S(2)}, u32[]{:S(2)}) collective-permute-start(bf16[256,256]{1,0:T(8,128)(2,1)S(1)} %bitcast.374), channel_id=1, source_target_pairs={{0,4},{4,0},{8,12},{12,8},{16,20},{20,16},{24,28},{28,24},{1,5},{5... | collective-permute-start | bytes 393224 | tf_op jit(solution)/shard_map/ppermute | solution.py:20
  98.5 10.6 %collective-permute-start.2 = (bf16[256,256]{1,0:T(8,128)(2,1)S(1)}, bf16[256,256]{1,0:T(8,128)(2,1)S(1)}, u32[]{:S(2)}, u32[]{:S(2)}) collective-permute-start(bf16[256,256]{1,0:T(8,128)(2,1)S(1)} %bitcast.372), channel_id=1, source_target_pairs={{0,8},{4,12},{8,0},{12,4},{16,24},{20,28},{24,16},{28,20},{1,9},{5... | collective-permute-start | bytes 393224 | tf_op jit(solution)/shard_map/ppermute | solution.py:20
  109.1 10.8 %collective-permute-start.3 = (bf16[256,256]{1,0:T(8,128)(2,1)S(1)}, bf16[256,256]{1,0:T(8,128)(2,1)S(1)}, u32[]{:S(2)}, u32[]{:S(2)}) collective-permute-start(bf16[256,256]{1,0:T(8,128)(2,1)S(1)} %bitcast.370), channel_id=1, source_target_pairs={{0,16},{4,20},{8,24},{12,28},{16,0},{20,4},{24,8},{28,12},{1,17},{... | collective-permute-start | bytes 393224 | tf_op jit(solution)/shard_map/ppermute | solution.py:20
  119.9 11.9 %collective-permute-start.4 = (bf16[256,256]{1,0:T(8,128)(2,1)S(1)}, bf16[256,256]{1,0:T(8,128)(2,1)S(1)}, u32[]{:S(2)}, u32[]{:S(2)}) collective-permute-start(bf16[256,256]{1,0:T(8,128)(2,1)S(1)} %bitcast.376), channel_id=1, source_target_pairs={{0,2},{2,0},{1,3},{3,1},{4,6},{6,4},{5,7},{7,5},{8,10},{10,8},{9,1... | collective-permute-start | bytes 393224 | tf_op jit(solution)/shard_map/ppermute | solution.py:20
  132.2 10.6 %collective-permute-start.5 = (bf16[256,256]{1,0:T(8,128)(2,1)S(1)}, bf16[256,256]{1,0:T(8,128)(2,1)S(1)}, u32[]{:S(2)}, u32[]{:S(2)}) collective-permute-start(bf16[256,256]{1,0:T(8,128)(2,1)S(1)} %bitcast.369), channel_id=1, source_target_pairs={{0,1},{1,0},{2,3},{3,2},{4,5},{5,4},{6,7},{7,6},{8,9},{9,8},{10,11... | collective-permute-start | bytes 393224 | tf_op jit(solution)/shard_map/ppermute | solution.py:20
  134.2 9.0 %collective-permute-start = (bf16[2560,256]{1,0:T(8,128)(2,1)}, bf16[2560,256]{1,0:T(8,128)(2,1)}, u32[]{:S(2)}, u32[]{:S(2)}) collective-permute-start(bf16[2560,256]{1,0:T(8,128)(2,1)} %bitcast.22), channel_id=1, source_target_pairs={{0,1},{1,0},{2,3},{3,2},{4,5},{5,4},{6,7},{7,6},{8,9},{9,8},{10,11... | collective-permute-start | bytes 3932168 | tf_op jit(solution)/shard_map/ppermute | solution.py:20
  149.6 11.1 %collective-permute-start.6 = (bf16[256,512]{1,0:T(8,128)(2,1)S(1)}, bf16[256,512]{1,0:T(8,128)(2,1)S(1)}, u32[]{:S(2)}, u32[]{:S(2)}) collective-permute-start(bf16[256,512]{1,0:T(8,128)(2,1)S(1)} %maximum_maximum_fusion.1), channel_id=1, source_target_pairs={{0,32},{32,0},{1,33},{33,1},{2,34},{34,2},{3,35},{35,3},{4,36},{36... | collective-permute-start | bytes 786440 | tf_op jit(solution)/shard_map/ppermute | solution.py:20
  151.7 19.3 %collective-permute-start.9 = (bf16[2048,128]{1,0:T(8,128)(2,1)S(1)}, bf16[2048,128]{1,0:T(8,128)(2,1)S(1)}, u32[]{:S(2)}, u32[]{:S(2)}) collective-permute-start(bf16[2048,128]{1,0:T(8,128)(2,1)S(1)} %bitcast.342), channel_id=1, source_target_pairs={{0,32},{32,0},{1,33},{33,1},{2,34},{34,2},{3,35},{35,3},{4,36},{36... | collective-permute-start | bytes 1572872 | tf_op jit(solution)/shard_map/ppermute | solution.py:20
  155.7 20.8 %collective-permute-start.10 = (bf16[1024,128]{1,0:T(8,128)(2,1)S(1)}, bf16[1024,128]{1,0:T(8,128)(2,1)S(1)}, u32[]{:S(2)}, u32[]{:S(2)}) collective-permute-start(bf16[1024,128]{1,0:T(8,128)(2,1)S(1)} %bitcast.344), channel_id=1, source_target_pairs={{0,128},{128,0},{1,129},{129,1},{2,130},{130,2},{3,131},{131,3},{4... | collective-permute-start | bytes 786440 | tf_op jit(solution)/shard_map/ppermute | solution.py:20
  171.0 9.3 %collective-permute-start.11 = (bf16[1024,128]{1,0:T(8,128)(2,1)S(1)}, bf16[1024,128]{1,0:T(8,128)(2,1)S(1)}, u32[]{:S(2)}, u32[]{:S(2)}) collective-permute-start(bf16[1024,128]{1,0:T(8,128)(2,1)S(1)} %bitcast.345), channel_id=1, source_target_pairs={{0,128},{128,0},{1,129},{129,1},{2,130},{130,2},{3,131},{131,3},{4... | collective-permute-start | bytes 786440 | tf_op jit(solution)/shard_map/ppermute | solution.py:20
  174.6 11.2 %collective-permute-start.7 = (bf16[256,256]{1,0:T(8,128)(2,1)S(1)}, bf16[256,256]{1,0:T(8,128)(2,1)S(1)}, u32[]{:S(2)}, u32[]{:S(2)}) collective-permute-start(bf16[256,256]{1,0:T(8,128)(2,1)S(1)} %bitcast.371), channel_id=1, source_target_pairs={{0,1},{1,0},{2,3},{3,2},{4,5},{5,4},{6,7},{7,6},{8,9},{9,8},{10,11... | collective-permute-start | bytes 393224 | tf_op jit(solution)/shard_map/ppermute | solution.py:20
  180.4 17.1 %collective-permute-start.12 = (bf16[3072,128]{1,0:T(8,128)(2,1)S(1)}, bf16[3072,128]{1,0:T(8,128)(2,1)S(1)}, u32[]{:S(2)}, u32[]{:S(2)}) collective-permute-start(bf16[3072,128]{1,0:T(8,128)(2,1)S(1)} %bitcast.339), channel_id=1, source_target_pairs={{0,1},{1,0},{2,3},{3,2},{4,5},{5,4},{6,7},{7,6},{8,9},{9,8},{10,11... | collective-permute-start | bytes 2359304 | tf_op jit(solution)/shard_map/ppermute | solution.py:20
  182.3 16.0 %collective-permute-start.13 = (bf16[256,512]{1,0:T(8,128)(2,1)S(1)}, bf16[256,512]{1,0:T(8,128)(2,1)S(1)}, u32[]{:S(2)}, u32[]{:S(2)}) collective-permute-start(bf16[256,512]{1,0:T(8,128)(2,1)S(1)} %maximum_maximum_fusion.1), channel_id=1, source_target_pairs={{0,128},{128,0},{1,129},{129,1},{2,130},{130,2},{3,131},{131,3},{4... | collective-permute-start | bytes 786440 | tf_op jit(solution)/shard_map/ppermute | solution.py:20
  185.9 11.5 %collective-permute-start.8 = (bf16[256,256]{1,0:T(8,128)(2,1)S(1)}, bf16[256,256]{1,0:T(8,128)(2,1)S(1)}, u32[]{:S(2)}, u32[]{:S(2)}) collective-permute-start(bf16[256,256]{1,0:T(8,128)(2,1)S(1)} %bitcast.373), channel_id=1, source_target_pairs={{0,2},{2,0},{1,3},{3,1},{4,6},{6,4},{5,7},{7,5},{8,10},{10,8},{9,1... | collective-permute-start | bytes 393224 | tf_op jit(solution)/shard_map/ppermute | solution.py:20
  193.1 10.0 %collective-permute-start.14 = (bf16[256,512]{1,0:T(8,128)(2,1)S(1)}, bf16[256,512]{1,0:T(8,128)(2,1)S(1)}, u32[]{:S(2)}, u32[]{:S(2)}) collective-permute-start(bf16[256,512]{1,0:T(8,128)(2,1)S(1)} %collective-permute-done.6), channel_id=1, source_target_pairs={{0,128},{128,0},{1,129},{129,1},{2,130},{130,2},{3,131},{131,3},{4... | collective-permute-start | bytes 786440 | tf_op jit(solution)/shard_map/ppermute | solution.py:20
  204.9 38.6 %all-to-all-start.2 = ((bf16[8,128,512]{2,1,0:T(8,128)(2,1)}), bf16[8,128,512]{2,1,0:T(8,128)(2,1)S(1)}, u32[]{:S(2)}, u32[]{:S(2)}) async-start(bf16[8,128,512]{2,1,0:T(8,128)(2,1)} %bitcast.333), calls=%async_computation.2 | async-start | bytes 2097152 | tf_op jit(solution)/shard_map/all_to_all | solution.py:15
  215.2 6.9 %collective-permute-start.15 = (bf16[256,256]{1,0:T(8,128)(2,1)S(1)}, bf16[256,256]{1,0:T(8,128)(2,1)S(1)}, u32[]{:S(2)}, u32[]{:S(2)}) collective-permute-start(bf16[256,256]{1,0:T(8,128)(2,1)S(1)} %bitcast.377), channel_id=1, source_target_pairs={{0,4},{4,0},{8,12},{12,8},{16,20},{20,16},{24,28},{28,24},{1,5},{5... | collective-permute-start | bytes 393224 | tf_op jit(solution)/shard_map/ppermute | solution.py:20
  222.2 9.2 %collective-permute-start.16 = (bf16[256,256]{1,0:T(8,128)(2,1)S(1)}, bf16[256,256]{1,0:T(8,128)(2,1)S(1)}, u32[]{:S(2)}, u32[]{:S(2)}) collective-permute-start(bf16[256,256]{1,0:T(8,128)(2,1)S(1)} %bitcast.378), channel_id=1, source_target_pairs={{0,8},{4,12},{8,0},{12,4},{16,24},{20,28},{24,16},{28,20},{1,9},{5... | collective-permute-start | bytes 393224 | tf_op jit(solution)/shard_map/ppermute | solution.py:20
  231.4 10.8 %collective-permute-start.17 = (bf16[256,256]{1,0:T(8,128)(2,1)S(1)}, bf16[256,256]{1,0:T(8,128)(2,1)S(1)}, u32[]{:S(2)}, u32[]{:S(2)}) collective-permute-start(bf16[256,256]{1,0:T(8,128)(2,1)S(1)} %bitcast.375), channel_id=1, source_target_pairs={{0,16},{4,20},{8,24},{12,28},{16,0},{20,4},{24,8},{28,12},{1,17},{... | collective-permute-start | bytes 393224 | tf_op jit(solution)/shard_map/ppermute | solution.py:20

commit v4 on v3

--- a/solution.py
+++ b/solution.py
@@ -71,8 +71,7 @@
     owners = lax.axis_size(MP)
     peers = owners // 2
     lines = lax.axis_size("x")
-    core, twin, yl, x = (lax.axis_index(name) for name in ("core", "twin", "yl", "x"))
-    far = lax.axis_index("far")
+    core, far, x = (lax.axis_index(name) for name in ("core", "far", "x"))
     group, feats_dev, width = panels.shape[1:]
     samples = group // blocks
     feats = feats_dev * blocks
@@ -91,14 +90,6 @@
     )
     codes = codes.astype(jnp.bfloat16).reshape(samples, code_blocks, width).transpose(1, 0, 2)
 
-    def twin_lanes(blocked, which):
-        return pick(blocked.reshape(*blocked.shape[:-1], 2, lanes), -2, which)
-
-    def yl_blocks(blocked, which):
-        lead = blocked.shape[: blocked.ndim - 3]
-        split = blocked.reshape(*lead, code_blocks // 4, 2, 2, *blocked.shape[-2:])
-        return pick(split, len(lead) + 1, which).reshape(*lead, code_blocks // 2, *blocked.shape[-2:])
-
     def x_swap(buffer, step):
         distance = 1 << step
         split = buffer.reshape(lines // distance // 2, 2, distance, *buffer.shape[1:])
@@ -108,75 +99,60 @@
         rows = rows.reshape(samples, owners, own_feats, width).transpose(1, 2, 0, 3)
         return rows.reshape(lines, 2, 2, own_feats, samples, width)
 
-    steps = range(lines.bit_length() - 1)
-    head_grads = x_swap(by_owner(cotangent[0, :, :NF]), 0)
-
     code_rows = code_blocks * samples
     head_rows = own_feats * samples
+    heads = [by_owner(wide[:, :NF]), by_owner(cotangent[0, :, :NF])]
+    heads = [h.reshape(peers, 2, head_rows, width) for h in heads]
+    heads = [jnp.where(core == 0, h, h[:, ::-1]).reshape(peers, 2 * head_rows, width) for h in heads]
     parcel = jnp.broadcast_to(codes.reshape(-1, width), (peers, code_rows, width))
-    heads = by_owner(wide[:, :NF])
-    heads = jnp.where(core == 0, heads, heads[:, :, ::-1]).reshape(peers, 2 * head_rows, width)
-    parcel = jnp.concatenate([parcel, heads], axis=1)
+    parcel = jnp.concatenate([parcel, *heads], axis=1)
     parcel_mine = swap(parcel, ("x", "far"))
     parcel_other = across(parcel_mine.reshape(-1, width), "core").reshape(parcel_mine.shape)
     mine, other = (
         p[:, :code_rows].reshape(peers, code_blocks, samples, width)
         for p in (parcel_mine, parcel_other)
     )
-    rows_mine = parcel_mine[:, code_rows : code_rows + head_rows]
-    rows_other = parcel_other[:, code_rows + head_rows :]
 
-    head_grads = after(head_grads, parcel)
-    for step in steps[1:]:
-        head_grads = x_swap(head_grads, step)
-    head_grads = cube_swap(head_grads, 1, far, "far").reshape(peers, 2, head_rows, width)
-    grads_mine = pick(head_grads, 1, core)
-    grads_other = after(pick(head_grads, 1, 1 - core), parcel_mine)
-    grads_other = across(grads_other.reshape(-1, width), "core").reshape(grads_mine.shape)
+    def heads_of(part, which):
+        starts = [code_rows + which * head_rows, code_rows + (2 + which) * head_rows]
+        return [tall(part[:, i : i + head_rows]) for i in starts]
 
     def tall(rows):
         rows = rows.reshape(peers, own_feats, samples, width).transpose(1, 0, 2, 3)
         return rows.reshape(own_feats, half, width)
 
-    def exchanged(blocked, axis):
-        return across(blocked.reshape(-1, lanes), axis).reshape(blocked.shape)
+    near_blocks = code_blocks // 2
+    left_mine = mine.reshape(peers, code_blocks // 4, 2, 2, samples, 2, lanes)
+    left_mine = left_mine.transpose(2, 5, 0, 1, 3, 4, 6).reshape(4, -1, lanes)
+    left_mine = swap(left_mine, ("yl", "twin"))
+    left_other = across(left_mine.reshape(-1, lanes), "core")
 
-    own_codes = twin_lanes(mine, twin)
-    twin_codes = exchanged(twin_lanes(mine, 1 - twin), "twin")
-    near_codes = exchanged(yl_blocks(own_codes, 1 - yl), "yl")
+    def columns(left):
+        left = left.reshape(4 * peers, near_blocks, samples, lanes).transpose(0, 2, 1, 3)
+        return left.reshape(4 * half, near_blocks * lanes)
 
     normed, grad_pre = [], []
-    for part, rows, cots in ((mine, rows_mine, grads_mine), (other, rows_other, grads_other)):
-        flat = part.transpose(0, 2, 1, 3).reshape(half, code_cols)
-        y, g = column_block(flat, mlp_weight, tall(rows), tall(cots))
+    for part, blocked, which in ((parcel_mine, mine, 0), (parcel_other, other, 1)):
+        flat = blocked.transpose(0, 2, 1, 3).reshape(half, code_cols)
+        y, g = column_block(flat, mlp_weight, *heads_of(part, which))
         normed.append(y)
         grad_pre.append(g)
     grad_pre = jnp.concatenate(grad_pre, axis=0)
-    twin_grads = across(grad_pre, "twin")
-    near_grads = jnp.concatenate([across(grad_pre, "yl"), across(twin_grads, "yl")], axis=0)
-    grads = jnp.concatenate([grad_pre, twin_grads], axis=0)
+    near_grads = jnp.broadcast_to(grad_pre, (4, *grad_pre.shape))
+    near_grads = after(near_grads, left_mine)
+    back = after(jnp.stack(normed), near_grads)
+    near_grads = swap(near_grads, ("yl", "twin")).reshape(4, 2, half, -1)
 
-    twin_codes = after(twin_codes, grad_pre)
-    near_twin = exchanged(yl_blocks(twin_codes, 1 - yl), "yl")
-    others = jnp.stack([yl_blocks(twin_codes, yl), near_codes, near_twin])
-    left_mine = (yl_blocks(own_codes, yl), *others)
-    left_other = (yl_blocks(twin_lanes(other, twin), yl), *exchanged(others, "core"))
+    def product(left, right):
+        right = right.reshape(4 * half, -1)
+        return jnp.einsum("sc,so->co", columns(left), right, preferred_element_type=jnp.float32)
 
-    def product(neighbour, right):
-        flat = [
-            part[i].transpose(0, 2, 1, 3).reshape(half, code_blocks // 2 * lanes)
-            for i in (neighbour, neighbour + 1)
-            for part in (left_mine, left_other)
-        ]
-        left = jnp.concatenate(flat, axis=0)
-        return jnp.einsum("sc,so->co", left, right, preferred_element_type=jnp.float32)
-
-    term = product(0, grads) + product(2, near_grads)
+    term = product(left_mine, near_grads[:, 0]) + product(left_other, near_grads[:, 1])
     term = term.astype(jnp.bfloat16).reshape(code_blocks // 2, lanes, -1)
     mlp_grad = jnp.sum(swap(term, ("yh", "pair")).astype(jnp.float32), axis=0)
 
-    back = jnp.stack(normed).reshape(2, own_feats, lines, 2, samples, width)
-    back = after(back, twin_grads)
+    steps = range(lines.bit_length() - 1)
+    back = back.reshape(2, own_feats, lines, 2, samples, width)
     back = ordered(back[0], back[1], 0, core).transpose(2, 3, 0, 1, 4, 5)
     back = cube_swap(back, 2, core, "core")
     back = cube_swap(back, 1, far, "far")

time: 245 us -> 217 us (0.89)
  the two profiles are of different devices: /device:TPU:94 before, /device:TPU:16 now
where the time goes in v4:
time: 217 us; the launch traced here: 216 us
  waiting for transfers between devices  105 us (48%)
  starting transfers between devices  83.3 us (38%)
  local copies, waits for them, and re-layouts  10.5 us (5%)
  matrix products  9.03 us (4%)
  other arithmetic  6.72 us (3%)
    all_to_all x5, waiting for transfers between devices, swap(): return lax.all_to_all(chunks, axes, split_axis=0, concat_axis=0, tiled=True)  85.5 us
    all_to_all x5, starting transfers between devices, swap(): return lax.all_to_all(chunks, axes, split_axis=0, concat_axis=0, tiled=True)  52.6 us
    ppermute x7, starting transfers between devices, across(): return lax.ppermute(array, axis, [(i, i ^ distance) for i in range(count)])  30.7 us
    ppermute x7, waiting for transfers between devices, across(): return lax.ppermute(array, axis, [(i, i ^ distance) for i in range(count)])  19.6 us
  transfers between devices with their start and end apart: 12, of which 7 were waited for; matrix products, arithmetic and copies ran while one was open for 9% of the time, Pallas kernels for 0%

profile of v4, /device:TPU:16, one launch (start us, length us, event | category | flops | bytes accessed | tf_op | source)
XLA Modules:
  0.0 215.9 jit_solution(16612393188594270736)
XLA Ops:
  0.7 16.7 %all-to-all-start = ((bf16[32,8,8,256]{3,2,1,0:T(8,128)(2,1)}), bf16[32,8,8,256]{3,2,1,0:T(8,128)(2,1)S(1)}, u32[]{:S(2)}, u32[]{:S(2)}) async-start(bf16[32,8,8,256]{3,2,1,0:T(8,128)(2,1)} %bitcast.258), calls=%async_computation | async-start | bytes 2097152 | tf_op jit(solution)/shard_map/all_to_all | solution.py:15
  17.6 27.4 %all-to-all-done = bf16[32,8,8,256]{3,2,1,0:T(8,128)(2,1)S(1)} async-done(((bf16[32,8,8,256]{3,2,1,0:T(8,128)(2,1)}), bf16[32,8,8,256]{3,2,1,0:T(8,128)(2,1)S(1)}, u32[]{:S(2)}, u32[]{:S(2)}) %all-to-all-start) | async-done | bytes 1048608 | tf_op jit(solution)/shard_map/all_to_all | solution.py:15
  45.3 0.3 fusion.47
  45.5 0.9 fusion
  46.5 0.3 copy.50
  46.8 0.5 reshape.349
  47.3 0.2 reverse_select_fusion
  47.5 1.3 pad_maximum_fusion
  48.8 16.1 %all-to-all-start.1 = ((bf16[16,192,256]{2,1,0:T(8,128)(2,1)}), bf16[16,192,256]{2,1,0:T(8,128)(2,1)}, u32[]{:S(2)}, u32[]{:S(2)}) async-start(bf16[16,192,256]{2,1,0:T(8,128)(2,1)} %pad_maximum_fusion), calls=%async_computation.1 | async-start | bytes 3145728 | tf_op jit(solution)/shard_map/all_to_all | solution.py:15
  65.0 49.2 %all-to-all-done.1 = bf16[16,192,256]{2,1,0:T(8,128)(2,1)} async-done(((bf16[16,192,256]{2,1,0:T(8,128)(2,1)}), bf16[16,192,256]{2,1,0:T(8,128)(2,1)}, u32[]{:S(2)}, u32[]{:S(2)}) %all-to-all-start.1) | async-done | bytes 1572896 | tf_op jit(solution)/shard_map/all_to_all | solution.py:15
  114.1 1.9 collective-permute-start
  116.0 1.3 slice.167
  117.3 2.9 %fusion.53 = f32[128,512]{1,0:T(8,128)S(1)} fusion(bf16[128,4096]{1,0:T(8,128)(2,1)S(1)} %bitcast.250, bf16[4096,512]{1,0:T(8,128)(2,1)} %param.8), kind=kOutput, calls=%fused_computation.142 | convolution fusion | flops 536870912 | bytes 5505024 | tf_op jit(solution)/shard_map/dot_general | solution.py:53
  120.3 1.0 slice_bitcast_fusion.1
  121.8 1.3 copy.54
  123.0 7.3 %all-to-all-start.2 = ((bf16[4,1024,128]{2,1,0:T(8,128)(2,1)}), bf16[4,1024,128]{2,1,0:T(8,128)(2,1)}, u32[]{:S(2)}, u32[]{:S(2)}) async-start(bf16[4,1024,128]{2,1,0:T(8,128)(2,1)} %bitcast.55), calls=%async_computation.2 | async-start | bytes 2097152 | tf_op jit(solution)/shard_map/all_to_all | solution.py:15
  130.3 0.2 multiply_reduce_fusion.4
  130.5 0.2 fusion.13
  130.8 0.2 multiply_convert_fusion.4
  131.0 1.6 slice.173
  132.6 1.0 slice_bitcast_fusion
  133.6 0.7 fusion.54
  134.8 0.2 multiply_reduce_fusion.2
  135.0 0.2 fusion.21
  135.3 0.2 multiply_convert_fusion.2
  135.5 8.8 %all-to-all-done.2 = bf16[4,1024,128]{2,1,0:T(8,128)(2,1)} async-done(((bf16[4,1024,128]{2,1,0:T(8,128)(2,1)}), bf16[4,1024,128]{2,1,0:T(8,128)(2,1)}, u32[]{:S(2)}, u32[]{:S(2)}) %all-to-all-start.2) | async-done | bytes 1048608 | tf_op jit(solution)/shard_map/all_to_all | solution.py:15
  144.4 1.1 broadcast_in_dim.7
  145.4 4.8 %all-to-all-start.3 = ((bf16[4,256,512]{2,1,0:T(8,128)(2,1)}), bf16[4,256,512]{2,1,0:T(8,128)(2,1)}, u32[]{:S(2)}, u32[]{:S(2)}) async-start(bf16[4,256,512]{2,1,0:T(8,128)(2,1)} %broadcast_in_dim.7), calls=%async_computation.3 | async-start | bytes 2097152 | tf_op jit(solution)/shard_map/all_to_all | solution.py:15
  150.4 1.9 collective-permute-start.1
  152.4 0.5 fusion.52
  152.9 2.4 %collective-permute-start.3 = (bf16[4096,128]{1,0:T(8,128)(2,1)}, bf16[4096,128]{1,0:T(8,128)(2,1)S(1)}, u32[]{:S(2)}, u32[]{:S(2)}) collective-permute-start(bf16[4096,128]{1,0:T(8,128)(2,1)} %bitcast.68), channel_id=1, source_target_pairs={{0,1},{1,0},{2,3},{3,2},{4,5},{5,4},{6,7},{7,6},{8,9},{9,8},{10,11... | collective-permute-start | bytes 3145736 | tf_op jit(solution)/shard_map/ppermute | solution.py:20
  155.4 2.6 %collective-permute-start.2 = (bf16[256,256]{1,0:T(8,128)(2,1)S(1)}, bf16[256,256]{1,0:T(8,128)(2,1)S(1)}, u32[]{:S(2)}, u32[]{:S(2)}) collective-permute-start(bf16[256,256]{1,0:T(8,128)(2,1)S(1)} %bitcast.276), channel_id=1, source_target_pairs={{0,2},{2,0},{1,3},{3,1},{4,6},{6,4},{5,7},{7,5},{8,10},{10,8},{9,1... | collective-permute-start | bytes 393224 | tf_op jit(solution)/shard_map/ppermute | solution.py:20
  158.0 8.7 %collective-permute-done.2 = bf16[256,256]{1,0:T(8,128)(2,1)S(1)} collective-permute-done((bf16[256,256]{1,0:T(8,128)(2,1)S(1)}, bf16[256,256]{1,0:T(8,128)(2,1)S(1)}, u32[]{:S(2)}, u32[]{:S(2)}) %collective-permute-start.2) | collective-permute-done | bytes 131104 | tf_op jit(solution)/shard_map/ppermute | solution.py:20
  166.8 1.3 fusion.49
  168.1 2.0 fusion.55
  170.0 1.8 add_convert_fusion
  171.8 7.7 %all-to-all-start.4 = ((bf16[8,128,512]{2,1,0:T(8,128)(2,1)}), bf16[8,128,512]{2,1,0:T(8,128)(2,1)S(1)}, u32[]{:S(2)}, u32[]{:S(2)}) async-start(bf16[8,128,512]{2,1,0:T(8,128)(2,1)} %bitcast.252), calls=%async_computation.4 | async-start | bytes 2097152 | tf_op jit(solution)/shard_map/all_to_all | solution.py:15
  179.5 3.5 %collective-permute-start.4 = (bf16[256,256]{1,0:T(8,128)(2,1)S(1)}, bf16[256,256]{1,0:T(8,128)(2,1)S(1)}, u32[]{:S(2)}, u32[]{:S(2)}) collective-permute-start(bf16[256,256]{1,0:T(8,128)(2,1)S(1)} %bitcast.280), channel_id=1, source_target_pairs={{0,4},{4,0},{8,12},{12,8},{16,20},{20,16},{24,28},{28,24},{1,5},{5... | collective-permute-start | bytes 393224 | tf_op jit(solution)/shard_map/ppermute | solution.py:20
  183.0 0.6 multiply_reduce_fusion
  183.6 2.8 %collective-permute-done.4 = bf16[256,256]{1,0:T(8,128)(2,1)S(1)} collective-permute-done((bf16[256,256]{1,0:T(8,128)(2,1)S(1)}, bf16[256,256]{1,0:T(8,128)(2,1)S(1)}, u32[]{:S(2)}, u32[]{:S(2)}) %collective-permute-start.4) | collective-permute-done | bytes 131104 | tf_op jit(solution)/shard_map/ppermute | solution.py:20
  186.5 8.3 %collective-permute-start.5 = (bf16[256,256]{1,0:T(8,128)(2,1)S(1)}, bf16[256,256]{1,0:T(8,128)(2,1)S(1)}, u32[]{:S(2)}, u32[]{:S(2)}) collective-permute-start(bf16[256,256]{1,0:T(8,128)(2,1)S(1)} %bitcast.277), channel_id=1, source_target_pairs={{0,8},{4,12},{8,0},{12,4},{16,24},{20,28},{24,16},{28,20},{1,9},{5... | collective-permute-start | bytes 393224 | tf_op jit(solution)/shard_map/ppermute | solution.py:20
  194.8 2.9 %collective-permute-done.5 = bf16[256,256]{1,0:T(8,128)(2,1)S(1)} collective-permute-done((bf16[256,256]{1,0:T(8,128)(2,1)S(1)}, bf16[256,256]{1,0:T(8,128)(2,1)S(1)}, u32[]{:S(2)}, u32[]{:S(2)}) %collective-permute-start.5) | collective-permute-done | bytes 131104 | tf_op jit(solution)/shard_map/ppermute | solution.py:20
  197.8 10.1 %collective-permute-start.6 = (bf16[256,256]{1,0:T(8,128)(2,1)S(1)}, bf16[256,256]{1,0:T(8,128)(2,1)S(1)}, u32[]{:S(2)}, u32[]{:S(2)}) collective-permute-start(bf16[256,256]{1,0:T(8,128)(2,1)S(1)} %bitcast.279), channel_id=1, source_target_pairs={{0,16},{4,20},{8,24},{12,28},{16,0},{20,4},{24,8},{28,12},{1,17},{... | collective-permute-start | bytes 393224 | tf_op jit(solution)/shard_map/ppermute | solution.py:20
  208.0 0.5 multiply_convert_fusion
  208.4 5.2 %collective-permute-done.6 = bf16[256,256]{1,0:T(8,128)(2,1)S(1)} collective-permute-done((bf16[256,256]{1,0:T(8,128)(2,1)S(1)}, bf16[256,256]{1,0:T(8,128)(2,1)S(1)}, u32[]{:S(2)}, u32[]{:S(2)}) %collective-permute-start.6) | collective-permute-done | bytes 131104 | tf_op jit(solution)/shard_map/ppermute | solution.py:20
  213.7 0.2 copy.91
  214.0 1.0 maximum_bitcast_fusion
  215.0 0.8 convert_reduce_fusion
  (67 shorter events, 2.2 us)
Async XLA Ops:
  0.6 151.7 %copy-start = (bf16[192,256]{1,0:T(8,128)(2,1)S(1)}, bf16[192,256]{1,0:T(8,128)(2,1)}, u32[]{:S(2)}) copy-start(bf16[192,256]{1,0:T(8,128)(2,1)} %param.9) | copy-start | bytes 294916
  0.6 16.8 %slice-start = ((bf16[1,8,256,256]{3,2,1,0:T(8,128)(2,1)}), bf16[1,8,64,256]{3,2,1,0:T(8,128)(2,1)S(1)}, s32[]{:S(2)}) async-start(bf16[1,8,256,256]{3,2,1,0:T(8,128)(2,1)} %param.6), calls=%async_computation.5 | async-start | bytes 524288 | tf_op jit(solution)/shard_map/slice | solution.py:104
  0.7 44.4 %all-to-all-start = ((bf16[32,8,8,256]{3,2,1,0:T(8,128)(2,1)}), bf16[32,8,8,256]{3,2,1,0:T(8,128)(2,1)S(1)}, u32[]{:S(2)}, u32[]{:S(2)}) async-start(bf16[32,8,8,256]{3,2,1,0:T(8,128)(2,1)} %bitcast.258), calls=%async_computation | async-start | bytes 2097152 | tf_op jit(solution)/shard_map/all_to_all | solution.py:15
  17.6 27.7 %copy-start.2 = (bf16[256,16]{0,1:T(8,128)(2,1)S(1)}, bf16[256,16]{0,1:T(8,128)(2,1)}, u32[]{:S(2)}) copy-start(bf16[256,16]{0,1:T(8,128)(2,1)} %param.7) | copy-start | bytes 24580
  48.8 65.3 %all-to-all-start.1 = ((bf16[16,192,256]{2,1,0:T(8,128)(2,1)}), bf16[16,192,256]{2,1,0:T(8,128)(2,1)}, u32[]{:S(2)}, u32[]{:S(2)}) async-start(bf16[16,192,256]{2,1,0:T(8,128)(2,1)} %pad_maximum_fusion), calls=%async_computation.1 | async-start | bytes 3145728 | tf_op jit(solution)/shard_map/all_to_all | solution.py:15
  114.1 16.9 %collective-permute-start = (bf16[3072,256]{1,0:T(8,128)(2,1)}, bf16[3072,256]{1,0:T(8,128)(2,1)}, u32[]{:S(2)}, u32[]{:S(2)}) collective-permute-start(bf16[3072,256]{1,0:T(8,128)(2,1)} %bitcast.30), channel_id=1, source_target_pairs={{0,1},{1,0},{2,3},{3,2},{4,5},{5,4},{6,7},{7,6},{8,9},{9,8},{10,11... | collective-permute-start | bytes 4718600 | tf_op jit(solution)/shard_map/ppermute | solution.py:20
  123.0 21.3 %all-to-all-start.2 = ((bf16[4,1024,128]{2,1,0:T(8,128)(2,1)}), bf16[4,1024,128]{2,1,0:T(8,128)(2,1)}, u32[]{:S(2)}, u32[]{:S(2)}) async-start(bf16[4,1024,128]{2,1,0:T(8,128)(2,1)} %bitcast.55), calls=%async_computation.2 | async-start | bytes 2097152 | tf_op jit(solution)/shard_map/all_to_all | solution.py:15
  130.5 3.1 %copy-start.1 = (bf16[4096,512]{1,0:T(8,128)(2,1)S(1)}, bf16[4096,512]{1,0:T(8,128)(2,1)}, u32[]{:S(2)}) copy-start(bf16[4096,512]{1,0:T(8,128)(2,1)} %param.8) | copy-start | bytes 12582916
  145.4 21.4 %all-to-all-start.3 = ((bf16[4,256,512]{2,1,0:T(8,128)(2,1)}), bf16[4,256,512]{2,1,0:T(8,128)(2,1)}, u32[]{:S(2)}, u32[]{:S(2)}) async-start(bf16[4,256,512]{2,1,0:T(8,128)(2,1)} %broadcast_in_dim.7), calls=%async_computation.3 | async-start | bytes 2097152 | tf_op jit(solution)/shard_map/all_to_all | solution.py:15
  150.4 4.9 %collective-permute-start.1 = (bf16[256,256]{1,0:T(8,128)(2,1)S(1)}, bf16[256,256]{1,0:T(8,128)(2,1)S(1)}, u32[]{:S(2)}, u32[]{:S(2)}) collective-permute-start(bf16[256,256]{1,0:T(8,128)(2,1)S(1)} %bitcast.278), channel_id=1, source_target_pairs={{0,1},{1,0},{2,3},{3,2},{4,5},{5,4},{6,7},{7,6},{8,9},{9,8},{10,11... | collective-permute-start | bytes 393224 | tf_op jit(solution)/shard_map/ppermute | solution.py:20
  152.9 17.2 %collective-permute-start.3 = (bf16[4096,128]{1,0:T(8,128)(2,1)}, bf16[4096,128]{1,0:T(8,128)(2,1)S(1)}, u32[]{:S(2)}, u32[]{:S(2)}) collective-permute-start(bf16[4096,128]{1,0:T(8,128)(2,1)} %bitcast.68), channel_id=1, source_target_pairs={{0,1},{1,0},{2,3},{3,2},{4,5},{5,4},{6,7},{7,6},{8,9},{9,8},{10,11... | collective-permute-start | bytes 3145736 | tf_op jit(solution)/shard_map/ppermute | solution.py:20
  155.4 11.3 %collective-permute-start.2 = (bf16[256,256]{1,0:T(8,128)(2,1)S(1)}, bf16[256,256]{1,0:T(8,128)(2,1)S(1)}, u32[]{:S(2)}, u32[]{:S(2)}) collective-permute-start(bf16[256,256]{1,0:T(8,128)(2,1)S(1)} %bitcast.276), channel_id=1, source_target_pairs={{0,2},{2,0},{1,3},{3,1},{4,6},{6,4},{5,7},{7,5},{8,10},{10,8},{9,1... | collective-permute-start | bytes 393224 | tf_op jit(solution)/shard_map/ppermute | solution.py:20
  171.8 43.2 %all-to-all-start.4 = ((bf16[8,128,512]{2,1,0:T(8,128)(2,1)}), bf16[8,128,512]{2,1,0:T(8,128)(2,1)S(1)}, u32[]{:S(2)}, u32[]{:S(2)}) async-start(bf16[8,128,512]{2,1,0:T(8,128)(2,1)} %bitcast.252), calls=%async_computation.4 | async-start | bytes 2097152 | tf_op jit(solution)/shard_map/all_to_all | solution.py:15
  179.5 6.9 %collective-permute-start.4 = (bf16[256,256]{1,0:T(8,128)(2,1)S(1)}, bf16[256,256]{1,0:T(8,128)(2,1)S(1)}, u32[]{:S(2)}, u32[]{:S(2)}) collective-permute-start(bf16[256,256]{1,0:T(8,128)(2,1)S(1)} %bitcast.280), channel_id=1, source_target_pairs={{0,4},{4,0},{8,12},{12,8},{16,20},{20,16},{24,28},{28,24},{1,5},{5... | collective-permute-start | bytes 393224 | tf_op jit(solution)/shard_map/ppermute | solution.py:20
  186.5 11.2 %collective-permute-start.5 = (bf16[256,256]{1,0:T(8,128)(2,1)S(1)}, bf16[256,256]{1,0:T(8,128)(2,1)S(1)}, u32[]{:S(2)}, u32[]{:S(2)}) collective-permute-start(bf16[256,256]{1,0:T(8,128)(2,1)S(1)} %bitcast.277), channel_id=1, source_target_pairs={{0,8},{4,12},{8,0},{12,4},{16,24},{20,28},{24,16},{28,20},{1,9},{5... | collective-permute-start | bytes 393224 | tf_op jit(solution)/shard_map/ppermute | solution.py:20
  197.8 15.8 %collective-permute-start.6 = (bf16[256,256]{1,0:T(8,128)(2,1)S(1)}, bf16[256,256]{1,0:T(8,128)(2,1)S(1)}, u32[]{:S(2)}, u32[]{:S(2)}) collective-permute-start(bf16[256,256]{1,0:T(8,128)(2,1)S(1)} %bitcast.279), channel_id=1, source_target_pairs={{0,16},{4,20},{8,24},{12,28},{16,0},{20,4},{24,8},{28,12},{1,17},{... | collective-permute-start | bytes 393224 | tf_op jit(solution)/shard_map/ppermute | solution.py:20

commit v5 on v4

--- a/solution.py
+++ b/solution.py
@@ -82,14 +82,6 @@
     code_blocks = code_cols // width
     lanes = width // 2
 
-    owned = swap(panels.reshape(blocks, samples, feats_dev, width), BATCH)
-    wide = owned.transpose(1, 0, 2, 3).reshape(samples, feats, width)
-    inner = jnp.einsum("snd,nk->sdk", wide, fm_proj, preferred_element_type=jnp.float32)
-    codes = jnp.einsum(
-        "snd,sdk->snk", wide.astype(jnp.float32), inner, precision=lax.Precision.HIGHEST
-    )
-    codes = codes.astype(jnp.bfloat16).reshape(samples, code_blocks, width).transpose(1, 0, 2)
-
     def x_swap(buffer, step):
         distance = 1 << step
         split = buffer.reshape(lines // distance // 2, 2, distance, *buffer.shape[1:])
@@ -99,27 +91,38 @@
         rows = rows.reshape(samples, owners, own_feats, width).transpose(1, 2, 0, 3)
         return rows.reshape(lines, 2, 2, own_feats, samples, width)
 
+    steps = range(lines.bit_length() - 1)
+    head_grads = by_owner(cotangent[0, :, :NF])
+    for step in steps:
+        head_grads = x_swap(head_grads, step)
+
+    owned = swap(panels.reshape(blocks, samples, feats_dev, width), BATCH)
+    owned = after(owned, head_grads)
+    wide = owned.transpose(1, 0, 2, 3).reshape(samples, feats, width)
+    inner = jnp.einsum("snd,nk->sdk", wide, fm_proj, preferred_element_type=jnp.float32)
+    codes = jnp.einsum(
+        "snd,sdk->snk", wide.astype(jnp.float32), inner, precision=lax.Precision.HIGHEST
+    )
+    codes = codes.astype(jnp.bfloat16).reshape(samples, code_blocks, width).transpose(1, 0, 2)
+
     code_rows = code_blocks * samples
     head_rows = own_feats * samples
-    heads = [by_owner(wide[:, :NF]), by_owner(cotangent[0, :, :NF])]
-    heads = [h.reshape(peers, 2, head_rows, width) for h in heads]
-    heads = [jnp.where(core == 0, h, h[:, ::-1]).reshape(peers, 2 * head_rows, width) for h in heads]
+    heads = by_owner(wide[:, :NF]).reshape(peers, 2, head_rows, width)
+    heads = jnp.where(core == 0, heads, heads[:, ::-1]).reshape(peers, 2 * head_rows, width)
     parcel = jnp.broadcast_to(codes.reshape(-1, width), (peers, code_rows, width))
-    parcel = jnp.concatenate([parcel, *heads], axis=1)
-    parcel_mine = swap(parcel, ("x", "far"))
+    parcel = jnp.concatenate([parcel, heads], axis=1)
+    head_grads = cube_swap(after(head_grads, parcel), 2, core, "core")
+    head_grads = cube_swap(head_grads, 1, far, "far").reshape(peers, 2, head_rows, width)
+    parcel_mine = after(swap(parcel, ("x", "far")), head_grads)
     parcel_other = across(parcel_mine.reshape(-1, width), "core").reshape(parcel_mine.shape)
     mine, other = (
         p[:, :code_rows].reshape(peers, code_blocks, samples, width)
         for p in (parcel_mine, parcel_other)
     )
 
-    def heads_of(part, which):
-        starts = [code_rows + which * head_rows, code_rows + (2 + which) * head_rows]
-        return [tall(part[:, i : i + head_rows]) for i in starts]
-
     def tall(rows):
-        rows = rows.reshape(peers, own_feats, samples, width).transpose(1, 0, 2, 3)
-        return rows.reshape(own_feats, half, width)
+        rows = rows.reshape(2 * peers, own_feats, samples, width).transpose(1, 0, 2, 3)
+        return rows.reshape(own_feats, 2 * half, width)
 
     near_blocks = code_blocks // 2
     left_mine = mine.reshape(peers, code_blocks // 4, 2, 2, samples, 2, lanes)
@@ -131,16 +134,15 @@
         left = left.reshape(4 * peers, near_blocks, samples, lanes).transpose(0, 2, 1, 3)
         return left.reshape(4 * half, near_blocks * lanes)
 
-    normed, grad_pre = [], []
-    for part, blocked, which in ((parcel_mine, mine, 0), (parcel_other, other, 1)):
-        flat = blocked.transpose(0, 2, 1, 3).reshape(half, code_cols)
-        y, g = column_block(flat, mlp_weight, *heads_of(part, which))
-        normed.append(y)
-        grad_pre.append(g)
-    grad_pre = jnp.concatenate(grad_pre, axis=0)
+    both = jnp.concatenate([mine, other]).transpose(0, 2, 1, 3).reshape(2 * half, code_cols)
+    rows = jnp.concatenate(
+        [parcel_mine[:, code_rows : code_rows + head_rows], parcel_other[:, code_rows + head_rows :]]
+    )
+    grads = jnp.concatenate([pick(head_grads, 1, core), pick(head_grads, 1, 1 - core)])
+    normed, grad_pre = column_block(both, mlp_weight, tall(rows), tall(grads))
     near_grads = jnp.broadcast_to(grad_pre, (4, *grad_pre.shape))
     near_grads = after(near_grads, left_mine)
-    back = after(jnp.stack(normed), near_grads)
+    back = after(normed, near_grads)
     near_grads = swap(near_grads, ("yl", "twin")).reshape(4, 2, half, -1)
 
     def product(left, right):
@@ -151,8 +153,7 @@
     term = term.astype(jnp.bfloat16).reshape(code_blocks // 2, lanes, -1)
     mlp_grad = jnp.sum(swap(term, ("yh", "pair")).astype(jnp.float32), axis=0)
 
-    steps = range(lines.bit_length() - 1)
-    back = back.reshape(2, own_feats, lines, 2, samples, width)
+    back = back.reshape(own_feats, 2, lines, 2, samples, width).transpose(1, 0, 2, 3, 4, 5)
     back = ordered(back[0], back[1], 0, core).transpose(2, 3, 0, 1, 4, 5)
     back = cube_swap(back, 2, core, "core")
     back = cube_swap(back, 1, far, "far")

time: 217 us -> 209 us (0.963)
  the two profiles are of different devices: /device:TPU:16 before, /device:TPU:80 now
where the time goes in v5:
time: 209 us; the launch traced here: 208 us
  starting transfers between devices  104 us (50%)
  waiting for transfers between devices  79.4 us (38%)
  local copies, waits for them, and re-layouts  10.9 us (5%)
  matrix products  6.64 us (3%)
  other arithmetic  6.55 us (3%)
    ppermute x12, waiting for transfers between devices, across(): return lax.ppermute(array, axis, [(i, i ^ distance) for i in range(count)])  69.5 us
    all_to_all x5, starting transfers between devices, swap(): return lax.all_to_all(chunks, axes, split_axis=0, concat_axis=0, tiled=True)  52.6 us
    ppermute x12, starting transfers between devices, across(): return lax.ppermute(array, axis, [(i, i ^ distance) for i in range(count)])  50.9 us
    all_to_all x5, waiting for transfers between devices, swap(): return lax.all_to_all(chunks, axes, split_axis=0, concat_axis=0, tiled=True)  9.86 us
  transfers between devices with their start and end apart: 17, of which 11 were waited for; matrix products, arithmetic and copies ran while one was open for 7% of the time, Pallas kernels for 0%

profile of v5, /device:TPU:80, one launch (start us, length us, event | category | flops | bytes accessed | tf_op | source)
XLA Modules:
  0.0 208.4 jit_solution(11899070818157280228)
XLA Ops:
  0.7 15.9 %all-to-all-start = ((bf16[32,8,8,256]{3,2,1,0:T(8,128)(2,1)}), bf16[32,8,8,256]{3,2,1,0:T(8,128)(2,1)S(1)}, u32[]{:S(2)}, u32[]{:S(2)}) async-start(bf16[32,8,8,256]{3,2,1,0:T(8,128)(2,1)} %bitcast.201), calls=%async_computation | async-start | bytes 2097152 | tf_op jit(solution)/shard_map/all_to_all | solution.py:15
  16.8 2.9 %collective-permute-start = (bf16[256,256]{1,0:T(8,128)(2,1)S(1)}, bf16[256,256]{1,0:T(8,128)(2,1)S(1)}, u32[]{:S(2)}, u32[]{:S(2)}) collective-permute-start(bf16[256,256]{1,0:T(8,128)(2,1)S(1)} %bitcast.230), channel_id=1, source_target_pairs={{0,4},{4,0},{8,12},{12,8},{16,20},{20,16},{24,28},{28,24},{1,5},{5... | collective-permute-start | bytes 393224 | tf_op jit(solution)/shard_map/ppermute | solution.py:20
  19.7 3.9 %collective-permute-done = bf16[256,256]{1,0:T(8,128)(2,1)S(1)} collective-permute-done((bf16[256,256]{1,0:T(8,128)(2,1)S(1)}, bf16[256,256]{1,0:T(8,128)(2,1)S(1)}, u32[]{:S(2)}, u32[]{:S(2)}) %collective-permute-start) | collective-permute-done | bytes 131104 | tf_op jit(solution)/shard_map/ppermute | solution.py:20
  23.8 3.8 %collective-permute-start.1 = (bf16[256,256]{1,0:T(8,128)(2,1)S(1)}, bf16[256,256]{1,0:T(8,128)(2,1)S(1)}, u32[]{:S(2)}, u32[]{:S(2)}) collective-permute-start(bf16[256,256]{1,0:T(8,128)(2,1)S(1)} %bitcast.224), channel_id=1, source_target_pairs={{0,8},{4,12},{8,0},{12,4},{16,24},{20,28},{24,16},{28,20},{1,9},{5... | collective-permute-start | bytes 393224 | tf_op jit(solution)/shard_map/ppermute | solution.py:20
  27.6 5.3 %collective-permute-done.1 = bf16[256,256]{1,0:T(8,128)(2,1)S(1)} collective-permute-done((bf16[256,256]{1,0:T(8,128)(2,1)S(1)}, bf16[256,256]{1,0:T(8,128)(2,1)S(1)}, u32[]{:S(2)}, u32[]{:S(2)}) %collective-permute-start.1) | collective-permute-done | bytes 131104 | tf_op jit(solution)/shard_map/ppermute | solution.py:20
  33.0 7.2 %collective-permute-start.2 = (bf16[256,256]{1,0:T(8,128)(2,1)S(1)}, bf16[256,256]{1,0:T(8,128)(2,1)S(1)}, u32[]{:S(2)}, u32[]{:S(2)}) collective-permute-start(bf16[256,256]{1,0:T(8,128)(2,1)S(1)} %bitcast.232), channel_id=1, source_target_pairs={{0,16},{4,20},{8,24},{12,28},{16,0},{20,4},{24,8},{28,12},{1,17},{... | collective-permute-start | bytes 393224 | tf_op jit(solution)/shard_map/ppermute | solution.py:20
  40.2 4.0 %collective-permute-done.2 = bf16[256,256]{1,0:T(8,128)(2,1)S(1)} collective-permute-done((bf16[256,256]{1,0:T(8,128)(2,1)S(1)}, bf16[256,256]{1,0:T(8,128)(2,1)S(1)}, u32[]{:S(2)}, u32[]{:S(2)}) %collective-permute-start.2) | collective-permute-done | bytes 131104 | tf_op jit(solution)/shard_map/ppermute | solution.py:20
  44.6 0.9 convolution_convert_fusion
  45.9 0.5 reshape.387
  46.6 1.2 pad_maximum_fusion.1
  47.8 16.4 %all-to-all-start.1 = ((bf16[16,160,256]{2,1,0:T(8,128)(2,1)}), bf16[16,160,256]{2,1,0:T(8,128)(2,1)S(1)}, u32[]{:S(2)}, u32[]{:S(2)}) async-start(bf16[16,160,256]{2,1,0:T(8,128)(2,1)} %pad_maximum_fusion.1), calls=%async_computation.1 | async-start | bytes 2621440 | tf_op jit(solution)/shard_map/all_to_all | solution.py:15
  64.2 1.9 collective-permute-start.3
  66.2 1.3 collective-permute-done.3
  67.6 7.7 %collective-permute-start.4 = (bf16[256,256]{1,0:T(8,128)(2,1)S(1)}, bf16[256,256]{1,0:T(8,128)(2,1)S(1)}, u32[]{:S(2)}, u32[]{:S(2)}) collective-permute-start(bf16[256,256]{1,0:T(8,128)(2,1)S(1)} %bitcast.227), channel_id=1, source_target_pairs={{0,2},{2,0},{1,3},{3,1},{4,6},{6,4},{5,7},{7,5},{8,10},{10,8},{9,1... | collective-permute-start | bytes 393224 | tf_op jit(solution)/shard_map/ppermute | solution.py:20
  75.3 30.8 %collective-permute-done.4 = bf16[256,256]{1,0:T(8,128)(2,1)S(1)} collective-permute-done((bf16[256,256]{1,0:T(8,128)(2,1)S(1)}, bf16[256,256]{1,0:T(8,128)(2,1)S(1)}, u32[]{:S(2)}, u32[]{:S(2)}) %collective-permute-start.4) | collective-permute-done | bytes 131104 | tf_op jit(solution)/shard_map/ppermute | solution.py:20
  106.2 2.9 %all-to-all-done.1 = bf16[16,160,256]{2,1,0:T(8,128)(2,1)S(1)} async-done(((bf16[16,160,256]{2,1,0:T(8,128)(2,1)}), bf16[16,160,256]{2,1,0:T(8,128)(2,1)S(1)}, u32[]{:S(2)}, u32[]{:S(2)}) %all-to-all-start.1) | async-done | bytes 1310752 | tf_op jit(solution)/shard_map/all_to_all | solution.py:15
  109.1 1.9 collective-permute-start.5
  111.4 1.1 fusion.26
  112.5 1.3 copy.76
  113.8 5.7 %all-to-all-start.2 = ((bf16[4,1024,128]{2,1,0:T(8,128)(2,1)}), bf16[4,1024,128]{2,1,0:T(8,128)(2,1)}, u32[]{:S(2)}, u32[]{:S(2)}) async-start(bf16[4,1024,128]{2,1,0:T(8,128)(2,1)} %bitcast.190), calls=%async_computation.2 | async-start | bytes 2097152 | tf_op jit(solution)/shard_map/all_to_all | solution.py:15
  119.5 1.0 slice.196
  120.5 1.3 slice_bitcast_fusion
  122.1 2.0 copy-done.3
  124.0 1.2 fusion.30
  125.8 0.3 fusion.7
  126.1 0.4 multiply_convert_fusion.2
  126.6 7.0 %all-to-all-done.2 = bf16[4,1024,128]{2,1,0:T(8,128)(2,1)} async-done(((bf16[4,1024,128]{2,1,0:T(8,128)(2,1)}), bf16[4,1024,128]{2,1,0:T(8,128)(2,1)}, u32[]{:S(2)}, u32[]{:S(2)}) %all-to-all-start.2) | async-done | bytes 1048608 | tf_op jit(solution)/shard_map/all_to_all | solution.py:15
  133.6 1.1 broadcast_in_dim.7
  134.6 4.8 %all-to-all-start.3 = ((bf16[4,256,512]{2,1,0:T(8,128)(2,1)}), bf16[4,256,512]{2,1,0:T(8,128)(2,1)}, u32[]{:S(2)}, u32[]{:S(2)}) async-start(bf16[4,256,512]{2,1,0:T(8,128)(2,1)} %broadcast_in_dim.7), calls=%async_computation.3 | async-start | bytes 2097152 | tf_op jit(solution)/shard_map/all_to_all | solution.py:15
  139.6 1.9 collective-permute-start.6
  141.5 0.5 fusion.29
  142.0 2.4 %collective-permute-start.8 = (bf16[4096,128]{1,0:T(8,128)(2,1)}, bf16[4096,128]{1,0:T(8,128)(2,1)S(1)}, u32[]{:S(2)}, u32[]{:S(2)}) collective-permute-start(bf16[4096,128]{1,0:T(8,128)(2,1)} %bitcast.64), channel_id=1, source_target_pairs={{0,1},{1,0},{2,3},{3,2},{4,5},{5,4},{6,7},{7,6},{8,9},{9,8},{10,11... | collective-permute-start | bytes 3145736 | tf_op jit(solution)/shard_map/ppermute | solution.py:20
  144.5 5.4 %collective-permute-start.7 = (bf16[256,256]{1,0:T(8,128)(2,1)S(1)}, bf16[256,256]{1,0:T(8,128)(2,1)S(1)}, u32[]{:S(2)}, u32[]{:S(2)}) collective-permute-start(bf16[256,256]{1,0:T(8,128)(2,1)S(1)} %bitcast.225), channel_id=1, source_target_pairs={{0,2},{2,0},{1,3},{3,1},{4,6},{6,4},{5,7},{7,5},{8,10},{10,8},{9,1... | collective-permute-start | bytes 393224 | tf_op jit(solution)/shard_map/ppermute | solution.py:20
  149.9 8.2 %collective-permute-done.7 = bf16[256,256]{1,0:T(8,128)(2,1)S(1)} collective-permute-done((bf16[256,256]{1,0:T(8,128)(2,1)S(1)}, bf16[256,256]{1,0:T(8,128)(2,1)S(1)}, u32[]{:S(2)}, u32[]{:S(2)}) %collective-permute-start.7) | collective-permute-done | bytes 131104 | tf_op jit(solution)/shard_map/ppermute | solution.py:20
  158.2 1.3 fusion.27
  159.5 2.0 fusion.31
  161.5 1.8 add_convert_fusion
  163.2 9.8 %all-to-all-start.4 = ((bf16[8,128,512]{2,1,0:T(8,128)(2,1)}), bf16[8,128,512]{2,1,0:T(8,128)(2,1)S(1)}, u32[]{:S(2)}, u32[]{:S(2)}) async-start(bf16[8,128,512]{2,1,0:T(8,128)(2,1)} %bitcast.191), calls=%async_computation.4 | async-start | bytes 2097152 | tf_op jit(solution)/shard_map/all_to_all | solution.py:15
  173.1 3.1 %collective-permute-start.9 = (bf16[256,256]{1,0:T(8,128)(2,1)S(1)}, bf16[256,256]{1,0:T(8,128)(2,1)S(1)}, u32[]{:S(2)}, u32[]{:S(2)}) collective-permute-start(bf16[256,256]{1,0:T(8,128)(2,1)S(1)} %bitcast.233), channel_id=1, source_target_pairs={{0,4},{4,0},{8,12},{12,8},{16,20},{20,16},{24,28},{28,24},{1,5},{5... | collective-permute-start | bytes 393224 | tf_op jit(solution)/shard_map/ppermute | solution.py:20
  176.2 0.6 multiply_reduce_fusion
  176.8 3.2 %collective-permute-done.9 = bf16[256,256]{1,0:T(8,128)(2,1)S(1)} collective-permute-done((bf16[256,256]{1,0:T(8,128)(2,1)S(1)}, bf16[256,256]{1,0:T(8,128)(2,1)S(1)}, u32[]{:S(2)}, u32[]{:S(2)}) %collective-permute-start.9) | collective-permute-done | bytes 131104 | tf_op jit(solution)/shard_map/ppermute | solution.py:20
  180.0 8.9 %collective-permute-start.10 = (bf16[256,256]{1,0:T(8,128)(2,1)S(1)}, bf16[256,256]{1,0:T(8,128)(2,1)S(1)}, u32[]{:S(2)}, u32[]{:S(2)}) collective-permute-start(bf16[256,256]{1,0:T(8,128)(2,1)S(1)} %bitcast.226), channel_id=1, source_target_pairs={{0,8},{4,12},{8,0},{12,4},{16,24},{20,28},{24,16},{28,20},{1,9},{5... | collective-permute-start | bytes 393224 | tf_op jit(solution)/shard_map/ppermute | solution.py:20
  188.9 5.3 %collective-permute-done.10 = bf16[256,256]{1,0:T(8,128)(2,1)S(1)} collective-permute-done((bf16[256,256]{1,0:T(8,128)(2,1)S(1)}, bf16[256,256]{1,0:T(8,128)(2,1)S(1)}, u32[]{:S(2)}, u32[]{:S(2)}) %collective-permute-start.10) | collective-permute-done | bytes 131104 | tf_op jit(solution)/shard_map/ppermute | solution.py:20
  194.3 3.8 %collective-permute-start.11 = (bf16[256,256]{1,0:T(8,128)(2,1)S(1)}, bf16[256,256]{1,0:T(8,128)(2,1)S(1)}, u32[]{:S(2)}, u32[]{:S(2)}) collective-permute-start(bf16[256,256]{1,0:T(8,128)(2,1)S(1)} %bitcast.231), channel_id=1, source_target_pairs={{0,16},{4,20},{8,24},{12,28},{16,0},{20,4},{24,8},{28,12},{1,17},{... | collective-permute-start | bytes 393224 | tf_op jit(solution)/shard_map/ppermute | solution.py:20
  198.1 0.5 multiply_convert_fusion
  198.6 7.5 %collective-permute-done.11 = bf16[256,256]{1,0:T(8,128)(2,1)S(1)} collective-permute-done((bf16[256,256]{1,0:T(8,128)(2,1)S(1)}, bf16[256,256]{1,0:T(8,128)(2,1)S(1)}, u32[]{:S(2)}, u32[]{:S(2)}) %collective-permute-start.11) | collective-permute-done | bytes 131104 | tf_op jit(solution)/shard_map/ppermute | solution.py:20
  206.5 1.0 maximum_bitcast_fusion
  207.6 0.8 convert_reduce_fusion
  (77 shorter events, 3.4 us)
Async XLA Ops:
  0.6 140.9 %copy-start = (bf16[192,256]{1,0:T(8,128)(2,1)S(1)}, bf16[192,256]{1,0:T(8,128)(2,1)}, u32[]{:S(2)}) copy-start(bf16[192,256]{1,0:T(8,128)(2,1)} %param.9) | copy-start | bytes 294916
  0.6 16.0 %slice-start = ((bf16[1,8,256,256]{3,2,1,0:T(8,128)(2,1)}), bf16[1,8,64,256]{3,2,1,0:T(8,128)(2,1)S(1)}, s32[]{:S(2)}) async-start(bf16[1,8,256,256]{3,2,1,0:T(8,128)(2,1)} %param.6), calls=%async_computation.5 | async-start | bytes 524288 | tf_op jit(solution)/shard_map/slice | solution.py:95
  0.7 43.6 %all-to-all-start = ((bf16[32,8,8,256]{3,2,1,0:T(8,128)(2,1)}), bf16[32,8,8,256]{3,2,1,0:T(8,128)(2,1)S(1)}, u32[]{:S(2)}, u32[]{:S(2)}) async-start(bf16[32,8,8,256]{3,2,1,0:T(8,128)(2,1)} %bitcast.201), calls=%async_computation | async-start | bytes 2097152 | tf_op jit(solution)/shard_map/all_to_all | solution.py:15
  16.8 6.9 %collective-permute-start = (bf16[256,256]{1,0:T(8,128)(2,1)S(1)}, bf16[256,256]{1,0:T(8,128)(2,1)S(1)}, u32[]{:S(2)}, u32[]{:S(2)}) collective-permute-start(bf16[256,256]{1,0:T(8,128)(2,1)S(1)} %bitcast.230), channel_id=1, source_target_pairs={{0,4},{4,0},{8,12},{12,8},{16,20},{20,16},{24,28},{28,24},{1,5},{5... | collective-permute-start | bytes 393224 | tf_op jit(solution)/shard_map/ppermute | solution.py:20
  23.8 9.2 %collective-permute-start.1 = (bf16[256,256]{1,0:T(8,128)(2,1)S(1)}, bf16[256,256]{1,0:T(8,128)(2,1)S(1)}, u32[]{:S(2)}, u32[]{:S(2)}) collective-permute-start(bf16[256,256]{1,0:T(8,128)(2,1)S(1)} %bitcast.224), channel_id=1, source_target_pairs={{0,8},{4,12},{8,0},{12,4},{16,24},{20,28},{24,16},{28,20},{1,9},{5... | collective-permute-start | bytes 393224 | tf_op jit(solution)/shard_map/ppermute | solution.py:20
  32.9 11.4 %copy-start.2 = (bf16[256,16]{0,1:T(8,128)(2,1)S(1)}, bf16[256,16]{0,1:T(8,128)(2,1)}, u32[]{:S(2)}) copy-start(bf16[256,16]{0,1:T(8,128)(2,1)} %param.7) | copy-start | bytes 24580
  33.0 11.1 %collective-permute-start.2 = (bf16[256,256]{1,0:T(8,128)(2,1)S(1)}, bf16[256,256]{1,0:T(8,128)(2,1)S(1)}, u32[]{:S(2)}, u32[]{:S(2)}) collective-permute-start(bf16[256,256]{1,0:T(8,128)(2,1)S(1)} %bitcast.232), channel_id=1, source_target_pairs={{0,16},{4,20},{8,24},{12,28},{16,0},{20,4},{24,8},{28,12},{1,17},{... | collective-permute-start | bytes 393224 | tf_op jit(solution)/shard_map/ppermute | solution.py:20
  47.8 61.3 %all-to-all-start.1 = ((bf16[16,160,256]{2,1,0:T(8,128)(2,1)}), bf16[16,160,256]{2,1,0:T(8,128)(2,1)S(1)}, u32[]{:S(2)}, u32[]{:S(2)}) async-start(bf16[16,160,256]{2,1,0:T(8,128)(2,1)} %pad_maximum_fusion.1), calls=%async_computation.1 | async-start | bytes 2621440 | tf_op jit(solution)/shard_map/all_to_all | solution.py:15
  64.2 3.2 %collective-permute-start.3 = (bf16[256,256]{1,0:T(8,128)(2,1)S(1)}, bf16[256,256]{1,0:T(8,128)(2,1)S(1)}, u32[]{:S(2)}, u32[]{:S(2)}) collective-permute-start(bf16[256,256]{1,0:T(8,128)(2,1)S(1)} %bitcast.228), channel_id=1, source_target_pairs={{0,1},{1,0},{2,3},{3,2},{4,5},{5,4},{6,7},{7,6},{8,9},{9,8},{10,11... | collective-permute-start | bytes 393224 | tf_op jit(solution)/shard_map/ppermute | solution.py:20
  67.6 38.5 %collective-permute-start.4 = (bf16[256,256]{1,0:T(8,128)(2,1)S(1)}, bf16[256,256]{1,0:T(8,128)(2,1)S(1)}, u32[]{:S(2)}, u32[]{:S(2)}) collective-permute-start(bf16[256,256]{1,0:T(8,128)(2,1)S(1)} %bitcast.227), channel_id=1, source_target_pairs={{0,2},{2,0},{1,3},{3,1},{4,6},{6,4},{5,7},{7,5},{8,10},{10,8},{9,1... | collective-permute-start | bytes 393224 | tf_op jit(solution)/shard_map/ppermute | solution.py:20
  109.1 10.4 %collective-permute-start.5 = (bf16[2560,256]{1,0:T(8,128)(2,1)S(1)}, bf16[2560,256]{1,0:T(8,128)(2,1)}, u32[]{:S(2)}, u32[]{:S(2)}) collective-permute-start(bf16[2560,256]{1,0:T(8,128)(2,1)S(1)} %bitcast.188), channel_id=1, source_target_pairs={{0,1},{1,0},{2,3},{3,2},{4,5},{5,4},{6,7},{7,6},{8,9},{9,8},{10,11... | collective-permute-start | bytes 3932168 | tf_op jit(solution)/shard_map/ppermute | solution.py:20
  113.8 19.8 %all-to-all-start.2 = ((bf16[4,1024,128]{2,1,0:T(8,128)(2,1)}), bf16[4,1024,128]{2,1,0:T(8,128)(2,1)}, u32[]{:S(2)}, u32[]{:S(2)}) async-start(bf16[4,1024,128]{2,1,0:T(8,128)(2,1)} %bitcast.190), calls=%async_computation.2 | async-start | bytes 2097152 | tf_op jit(solution)/shard_map/all_to_all | solution.py:15
  119.5 2.4 %copy-start.1 = (bf16[16,16,8,256]{3,2,1,0:T(8,128)(2,1)S(1)}, bf16[16,16,8,256]{3,2,1,0:T(8,128)(2,1)}, u32[]{:S(2)}) copy-start(bf16[16,16,8,256]{3,2,1,0:T(8,128)(2,1)} %get-tuple-element.25) | copy-start | bytes 3145732
  121.8 2.2 %copy-start.3 = (bf16[4096,512]{1,0:T(8,128)(2,1)S(1)}, bf16[4096,512]{1,0:T(8,128)(2,1)}, u32[]{:S(2)}) copy-start(bf16[4096,512]{1,0:T(8,128)(2,1)} %param.8) | copy-start | bytes 12582916
  134.6 23.6 %all-to-all-start.3 = ((bf16[4,256,512]{2,1,0:T(8,128)(2,1)}), bf16[4,256,512]{2,1,0:T(8,128)(2,1)}, u32[]{:S(2)}, u32[]{:S(2)}) async-start(bf16[4,256,512]{2,1,0:T(8,128)(2,1)} %broadcast_in_dim.7), calls=%async_computation.3 | async-start | bytes 2097152 | tf_op jit(solution)/shard_map/all_to_all | solution.py:15
  139.6 4.9 %collective-permute-start.6 = (bf16[256,256]{1,0:T(8,128)(2,1)S(1)}, bf16[256,256]{1,0:T(8,128)(2,1)S(1)}, u32[]{:S(2)}, u32[]{:S(2)}) collective-permute-start(bf16[256,256]{1,0:T(8,128)(2,1)S(1)} %bitcast.229), channel_id=1, source_target_pairs={{0,1},{1,0},{2,3},{3,2},{4,5},{5,4},{6,7},{7,6},{8,9},{9,8},{10,11... | collective-permute-start | bytes 393224 | tf_op jit(solution)/shard_map/ppermute | solution.py:20
  142.0 19.4 %collective-permute-start.8 = (bf16[4096,128]{1,0:T(8,128)(2,1)}, bf16[4096,128]{1,0:T(8,128)(2,1)S(1)}, u32[]{:S(2)}, u32[]{:S(2)}) collective-permute-start(bf16[4096,128]{1,0:T(8,128)(2,1)} %bitcast.64), channel_id=1, source_target_pairs={{0,1},{1,0},{2,3},{3,2},{4,5},{5,4},{6,7},{7,6},{8,9},{9,8},{10,11... | collective-permute-start | bytes 3145736 | tf_op jit(solution)/shard_map/ppermute | solution.py:20
  144.5 13.6 %collective-permute-start.7 = (bf16[256,256]{1,0:T(8,128)(2,1)S(1)}, bf16[256,256]{1,0:T(8,128)(2,1)S(1)}, u32[]{:S(2)}, u32[]{:S(2)}) collective-permute-start(bf16[256,256]{1,0:T(8,128)(2,1)S(1)} %bitcast.225), channel_id=1, source_target_pairs={{0,2},{2,0},{1,3},{3,1},{4,6},{6,4},{5,7},{7,5},{8,10},{10,8},{9,1... | collective-permute-start | bytes 393224 | tf_op jit(solution)/shard_map/ppermute | solution.py:20
  163.2 44.4 %all-to-all-start.4 = ((bf16[8,128,512]{2,1,0:T(8,128)(2,1)}), bf16[8,128,512]{2,1,0:T(8,128)(2,1)S(1)}, u32[]{:S(2)}, u32[]{:S(2)}) async-start(bf16[8,128,512]{2,1,0:T(8,128)(2,1)} %bitcast.191), calls=%async_computation.4 | async-start | bytes 2097152 | tf_op jit(solution)/shard_map/all_to_all | solution.py:15
  173.1 6.9 %collective-permute-start.9 = (bf16[256,256]{1,0:T(8,128)(2,1)S(1)}, bf16[256,256]{1,0:T(8,128)(2,1)S(1)}, u32[]{:S(2)}, u32[]{:S(2)}) collective-permute-start(bf16[256,256]{1,0:T(8,128)(2,1)S(1)} %bitcast.233), channel_id=1, source_target_pairs={{0,4},{4,0},{8,12},{12,8},{16,20},{20,16},{24,28},{28,24},{1,5},{5... | collective-permute-start | bytes 393224 | tf_op jit(solution)/shard_map/ppermute | solution.py:20
  180.0 14.2 %collective-permute-start.10 = (bf16[256,256]{1,0:T(8,128)(2,1)S(1)}, bf16[256,256]{1,0:T(8,128)(2,1)S(1)}, u32[]{:S(2)}, u32[]{:S(2)}) collective-permute-start(bf16[256,256]{1,0:T(8,128)(2,1)S(1)} %bitcast.226), channel_id=1, source_target_pairs={{0,8},{4,12},{8,0},{12,4},{16,24},{20,28},{24,16},{28,20},{1,9},{5... | collective-permute-start | bytes 393224 | tf_op jit(solution)/shard_map/ppermute | solution.py:20
  194.3 11.8 %collective-permute-start.11 = (bf16[256,256]{1,0:T(8,128)(2,1)S(1)}, bf16[256,256]{1,0:T(8,128)(2,1)S(1)}, u32[]{:S(2)}, u32[]{:S(2)}) collective-permute-start(bf16[256,256]{1,0:T(8,128)(2,1)S(1)} %bitcast.231), channel_id=1, source_target_pairs={{0,16},{4,20},{8,24},{12,28},{16,0},{20,4},{24,8},{28,12},{1,17},{... | collective-permute-start | bytes 393224 | tf_op jit(solution)/shard_map/ppermute | solution.py:20

commit v6 on v5

--- a/solution.py
+++ b/solution.py
@@ -38,6 +38,26 @@
     sent = pick(buffer, axis, 1 - index)
     received = across(sent.reshape(-1, sent.shape[-1]), name, distance).reshape(sent.shape)
     return ordered(pick(buffer, axis, index), received, axis, index)
+
+
+def two_bits(buffer, x):
+    def relative(entries):
+        low, high = x & 1 == 0, x & 2 == 0
+        return [
+            jnp.where(
+                high,
+                jnp.where(low, entries[d], entries[1 ^ d]),
+                jnp.where(low, entries[2 ^ d], entries[3 ^ d]),
+            )
+            for d in range(4)
+        ]
+
+    buffer = buffer.reshape(2, 4, *buffer.shape[1:])
+    entries = relative([buffer[:, i] for i in range(4)])
+    flat = [entry.reshape(-1, entry.shape[-1]) for entry in entries]
+    moved = [flat[0]] + [across(flat[d], "x", d) for d in (1, 2, 3)]
+    moved = relative([entry.reshape(entries[0].shape) for entry in moved])
+    return jnp.stack(moved, axis=1).reshape(-1, *buffer.shape[2:])
 
 
 def normalise(rows):
@@ -71,7 +91,7 @@
     owners = lax.axis_size(MP)
     peers = owners // 2
     lines = lax.axis_size("x")
-    core, far, x = (lax.axis_index(name) for name in ("core", "far", "x"))
+    core, far, x, yl, twin = (lax.axis_index(name) for name in ("core", "far", "x", "yl", "twin"))
     group, feats_dev, width = panels.shape[1:]
     samples = group // blocks
     feats = feats_dev * blocks
@@ -128,7 +148,6 @@
     left_mine = mine.reshape(peers, code_blocks // 4, 2, 2, samples, 2, lanes)
     left_mine = left_mine.transpose(2, 5, 0, 1, 3, 4, 6).reshape(4, -1, lanes)
     left_mine = swap(left_mine, ("yl", "twin"))
-    left_other = across(left_mine.reshape(-1, lanes), "core")
 
     def columns(left):
         left = left.reshape(4 * peers, near_blocks, samples, lanes).transpose(0, 2, 1, 3)
@@ -140,25 +159,34 @@
     )
     grads = jnp.concatenate([pick(head_grads, 1, core), pick(head_grads, 1, 1 - core)])
     normed, grad_pre = column_block(both, mlp_weight, tall(rows), tall(grads))
-    near_grads = jnp.broadcast_to(grad_pre, (4, *grad_pre.shape))
-    near_grads = after(near_grads, left_mine)
-    back = after(normed, near_grads)
-    near_grads = swap(near_grads, ("yl", "twin")).reshape(4, 2, half, -1)
+    near_own = across(grad_pre, "yl")
+    twin_grads = across(grad_pre, "twin")
+    near_twin = across(twin_grads, "yl")
+    left_other = across(after(left_mine, grad_pre).reshape(-1, lanes), "core")
+    back = after(normed, grad_pre)
+
+    def halves_of(index):
+        here = jnp.where(twin == index % 2, grad_pre, twin_grads)
+        there = jnp.where(twin == index % 2, near_own, near_twin)
+        return jnp.where(yl == index // 2, here, there).reshape(2, half, -1)
+
+    grads = [halves_of(index) for index in range(4)]
 
     def product(left, right):
-        right = right.reshape(4 * half, -1)
+        right = jnp.concatenate(right, axis=0)
         return jnp.einsum("sc,so->co", columns(left), right, preferred_element_type=jnp.float32)
 
-    term = product(left_mine, near_grads[:, 0]) + product(left_other, near_grads[:, 1])
+    term = product(left_mine, [g[0] for g in grads]) + product(left_other, [g[1] for g in grads])
     term = term.astype(jnp.bfloat16).reshape(code_blocks // 2, lanes, -1)
-    mlp_grad = jnp.sum(swap(term, ("yh", "pair")).astype(jnp.float32), axis=0)
-
     back = back.reshape(own_feats, 2, lines, 2, samples, width).transpose(1, 0, 2, 3, 4, 5)
     back = ordered(back[0], back[1], 0, core).transpose(2, 3, 0, 1, 4, 5)
     back = cube_swap(back, 2, core, "core")
     back = cube_swap(back, 1, far, "far")
     back = after(back, term)
-    for step in steps:
+    mlp_grad = jnp.sum(swap(term, ("yh", "pair")).astype(jnp.float32), axis=0)
+    if lines == 8:
+        back = two_bits(back, x)
+    for step in steps[2 if lines == 8 else 0 :]:
         back = x_swap(back, step)
     head = back.transpose(4, 0, 1, 2, 3, 5).reshape(samples, NF, width)
 

time: 209 us -> 199 us (0.952)
  the two profiles are of different devices: /device:TPU:80 before, /device:TPU:22 now
where the time goes in v6:
time: 199 us; the launch traced here: 198 us
  starting transfers between devices  94.5 us (47%)
  waiting for transfers between devices  78.6 us (39%)
  local copies, waits for them, and re-layouts  10.4 us (5%)
  other arithmetic  6.77 us (3%)
  matrix products  6.66 us (3%)
    ppermute x16, waiting for transfers between devices, across(): return lax.ppermute(array, axis, [(i, i ^ distance) for i in range(count)])  68.5 us
    ppermute x16, starting transfers between devices, across(): return lax.ppermute(array, axis, [(i, i ^ distance) for i in range(count)])  47.8 us
    all_to_all x4, starting transfers between devices, swap(): return lax.all_to_all(chunks, axes, split_axis=0, concat_axis=0, tiled=True)  46.7 us
    all_to_all x4, waiting for transfers between devices, swap(): return lax.all_to_all(chunks, axes, split_axis=0, concat_axis=0, tiled=True)  10.1 us
  transfers between devices with their start and end apart: 20, of which 12 were waited for; matrix products, arithmetic and copies ran while one was open for 9% of the time, Pallas kernels for 0%

profile of v6, /device:TPU:22, one launch (start us, length us, event | category | flops | bytes accessed | tf_op | source)
XLA Modules:
  0.0 198.4 jit_solution(18354376614538545318)
XLA Ops:
  0.7 16.3 %all-to-all-start = ((bf16[32,8,8,256]{3,2,1,0:T(8,128)(2,1)}), bf16[32,8,8,256]{3,2,1,0:T(8,128)(2,1)S(1)}, u32[]{:S(2)}, u32[]{:S(2)}) async-start(bf16[32,8,8,256]{3,2,1,0:T(8,128)(2,1)} %bitcast.202), calls=%async_computation | async-start | bytes 2097152 | tf_op jit(solution)/shard_map/all_to_all | solution.py:15
  17.2 2.4 %collective-permute-start = (bf16[256,256]{1,0:T(8,128)(2,1)S(1)}, bf16[256,256]{1,0:T(8,128)(2,1)S(1)}, u32[]{:S(2)}, u32[]{:S(2)}) collective-permute-start(bf16[256,256]{1,0:T(8,128)(2,1)S(1)} %bitcast.227), channel_id=1, source_target_pairs={{0,4},{4,0},{8,12},{12,8},{16,20},{20,16},{24,28},{28,24},{1,5},{5... | collective-permute-start | bytes 393224 | tf_op jit(solution)/shard_map/ppermute | solution.py:20
  19.7 4.4 %collective-permute-done = bf16[256,256]{1,0:T(8,128)(2,1)S(1)} collective-permute-done((bf16[256,256]{1,0:T(8,128)(2,1)S(1)}, bf16[256,256]{1,0:T(8,128)(2,1)S(1)}, u32[]{:S(2)}, u32[]{:S(2)}) %collective-permute-start) | collective-permute-done | bytes 131104 | tf_op jit(solution)/shard_map/ppermute | solution.py:20
  24.2 2.4 %collective-permute-start.1 = (bf16[256,256]{1,0:T(8,128)(2,1)S(1)}, bf16[256,256]{1,0:T(8,128)(2,1)S(1)}, u32[]{:S(2)}, u32[]{:S(2)}) collective-permute-start(bf16[256,256]{1,0:T(8,128)(2,1)S(1)} %bitcast.224), channel_id=1, source_target_pairs={{0,8},{4,12},{8,0},{12,4},{16,24},{20,28},{24,16},{28,20},{1,9},{5... | collective-permute-start | bytes 393224 | tf_op jit(solution)/shard_map/ppermute | solution.py:20
  26.6 7.0 %collective-permute-done.1 = bf16[256,256]{1,0:T(8,128)(2,1)S(1)} collective-permute-done((bf16[256,256]{1,0:T(8,128)(2,1)S(1)}, bf16[256,256]{1,0:T(8,128)(2,1)S(1)}, u32[]{:S(2)}, u32[]{:S(2)}) %collective-permute-start.1) | collective-permute-done | bytes 131104 | tf_op jit(solution)/shard_map/ppermute | solution.py:20
  33.7 4.7 %collective-permute-start.2 = (bf16[256,256]{1,0:T(8,128)(2,1)S(1)}, bf16[256,256]{1,0:T(8,128)(2,1)S(1)}, u32[]{:S(2)}, u32[]{:S(2)}) collective-permute-start(bf16[256,256]{1,0:T(8,128)(2,1)S(1)} %bitcast.229), channel_id=1, source_target_pairs={{0,16},{4,20},{8,24},{12,28},{16,0},{20,4},{24,8},{28,12},{1,17},{... | collective-permute-start | bytes 393224 | tf_op jit(solution)/shard_map/ppermute | solution.py:20
  38.4 7.4 %collective-permute-done.2 = bf16[256,256]{1,0:T(8,128)(2,1)S(1)} collective-permute-done((bf16[256,256]{1,0:T(8,128)(2,1)S(1)}, bf16[256,256]{1,0:T(8,128)(2,1)S(1)}, u32[]{:S(2)}, u32[]{:S(2)}) %collective-permute-start.2) | collective-permute-done | bytes 131104 | tf_op jit(solution)/shard_map/ppermute | solution.py:20
  46.2 0.9 convolution_convert_fusion
  48.3 1.1 pad_maximum_fusion.1
  49.4 16.0 %all-to-all-start.1 = ((bf16[16,160,256]{2,1,0:T(8,128)(2,1)}), bf16[16,160,256]{2,1,0:T(8,128)(2,1)}, u32[]{:S(2)}, u32[]{:S(2)}) async-start(bf16[16,160,256]{2,1,0:T(8,128)(2,1)} %pad_maximum_fusion.1), calls=%async_computation.1 | async-start | bytes 2621440 | tf_op jit(solution)/shard_map/all_to_all | solution.py:15
  65.5 1.9 collective-permute-start.3
  67.4 1.3 collective-permute-done.3
  68.8 7.3 %collective-permute-start.4 = (bf16[256,256]{1,0:T(8,128)(2,1)S(1)}, bf16[256,256]{1,0:T(8,128)(2,1)S(1)}, u32[]{:S(2)}, u32[]{:S(2)}) collective-permute-start(bf16[256,256]{1,0:T(8,128)(2,1)S(1)} %bitcast.223), channel_id=1, source_target_pairs={{0,2},{2,0},{1,3},{3,1},{4,6},{6,4},{5,7},{7,5},{8,10},{10,8},{9,1... | collective-permute-start | bytes 393224 | tf_op jit(solution)/shard_map/ppermute | solution.py:20
  76.1 32.4 %collective-permute-done.4 = bf16[256,256]{1,0:T(8,128)(2,1)S(1)} collective-permute-done((bf16[256,256]{1,0:T(8,128)(2,1)S(1)}, bf16[256,256]{1,0:T(8,128)(2,1)S(1)}, u32[]{:S(2)}, u32[]{:S(2)}) %collective-permute-start.4) | collective-permute-done | bytes 131104 | tf_op jit(solution)/shard_map/ppermute | solution.py:20
  108.6 6.7 %all-to-all-done.1 = bf16[16,160,256]{2,1,0:T(8,128)(2,1)} async-done(((bf16[16,160,256]{2,1,0:T(8,128)(2,1)}), bf16[16,160,256]{2,1,0:T(8,128)(2,1)}, u32[]{:S(2)}, u32[]{:S(2)}) %all-to-all-start.1) | async-done | bytes 1310752 | tf_op jit(solution)/shard_map/all_to_all | solution.py:15
  115.3 1.9 collective-permute-start.5
  117.3 0.5 fusion.49
  118.2 0.9 slice.181
  119.1 1.4 fusion.43
  120.6 1.3 copy.84
  121.8 4.2 %all-to-all-start.2 = ((bf16[4,1024,128]{2,1,0:T(8,128)(2,1)}), bf16[4,1024,128]{2,1,0:T(8,128)(2,1)}, u32[]{:S(2)}, u32[]{:S(2)}) async-start(bf16[4,1024,128]{2,1,0:T(8,128)(2,1)} %bitcast.58), calls=%async_computation.2 | async-start | bytes 2097152 | tf_op jit(solution)/shard_map/all_to_all | solution.py:15
  126.1 0.9 slice.224
  127.0 1.3 slice_bitcast_fusion
  128.5 2.0 %copy-done.2 = bf16[4096,512]{1,0:T(8,128)(2,1)S(1)} copy-done((bf16[4096,512]{1,0:T(8,128)(2,1)S(1)}, bf16[4096,512]{1,0:T(8,128)(2,1)}, u32[]{:S(2)}) %copy-start.2) | copy-done | bytes 4194328
  130.5 1.2 fusion.50
  133.1 3.1 %collective-permute-start.8 = (bf16[256,512]{1,0:T(8,128)(2,1)S(1)}, bf16[256,512]{1,0:T(8,128)(2,1)S(1)}, u32[]{:S(2)}, u32[]{:S(2)}) collective-permute-start(bf16[256,512]{1,0:T(8,128)(2,1)S(1)} %pad_maximum_fusion.3), channel_id=1, source_target_pairs={{0,32},{32,0},{1,33},{33,1},{2,34},{34,2},{3,35},{35,3},{4,36},{36... | collective-permute-start | bytes 786440 | tf_op jit(solution)/shard_map/ppermute | solution.py:20
  136.3 1.9 collective-permute-start.6
  138.3 0.6 multiply_reduce_fusion
  138.9 2.5 %collective-permute-start.9 = (bf16[256,512]{1,0:T(8,128)(2,1)S(1)}, bf16[256,512]{1,0:T(8,128)(2,1)S(1)}, u32[]{:S(2)}, u32[]{:S(2)}) collective-permute-start(bf16[256,512]{1,0:T(8,128)(2,1)S(1)} %pad_maximum_fusion.3), channel_id=1, source_target_pairs={{0,128},{128,0},{1,129},{129,1},{2,130},{130,2},{3,131},{131,3},{4... | collective-permute-start | bytes 786440 | tf_op jit(solution)/shard_map/ppermute | solution.py:20
  141.3 4.0 %collective-permute-done.8 = bf16[256,512]{1,0:T(8,128)(2,1)S(1)} collective-permute-done((bf16[256,512]{1,0:T(8,128)(2,1)S(1)}, bf16[256,512]{1,0:T(8,128)(2,1)S(1)}, u32[]{:S(2)}, u32[]{:S(2)}) %collective-permute-start.8) | collective-permute-done | bytes 262176 | tf_op jit(solution)/shard_map/ppermute | solution.py:20
  145.3 2.5 %collective-permute-start.10 = (bf16[256,512]{1,0:T(8,128)(2,1)S(1)}, bf16[256,512]{1,0:T(8,128)(2,1)S(1)}, u32[]{:S(2)}, u32[]{:S(2)}) collective-permute-start(bf16[256,512]{1,0:T(8,128)(2,1)S(1)} %collective-permute-done.8), channel_id=1, source_target_pairs={{0,128},{128,0},{1,129},{129,1},{2,130},{130,2},{3,131},{131,3},{4... | collective-permute-start | bytes 786440 | tf_op jit(solution)/shard_map/ppermute | solution.py:20
  147.9 0.7 copy.81
  148.6 3.4 %collective-permute-start.7 = (bf16[256,256]{1,0:T(8,128)(2,1)}, bf16[256,256]{1,0:T(8,128)(2,1)S(1)}, u32[]{:S(2)}, u32[]{:S(2)}) collective-permute-start(bf16[256,256]{1,0:T(8,128)(2,1)} %bitcast.54), channel_id=1, source_target_pairs={{0,2},{2,0},{1,3},{3,1},{4,6},{6,4},{5,7},{7,5},{8,10},{10,8},{9,1... | collective-permute-start | bytes 393224 | tf_op jit(solution)/shard_map/ppermute | solution.py:20
  152.0 1.9 collective-permute-start.11
  153.9 1.6 collective-permute-done.10
  155.9 2.0 fusion
  157.9 1.8 add_convert_fusion
  159.6 10.2 %all-to-all-start.3 = ((bf16[8,128,512]{2,1,0:T(8,128)(2,1)}), bf16[8,128,512]{2,1,0:T(8,128)(2,1)S(1)}, u32[]{:S(2)}, u32[]{:S(2)}) async-start(bf16[8,128,512]{2,1,0:T(8,128)(2,1)} %bitcast.203), calls=%async_computation.3 | async-start | bytes 2097152 | tf_op jit(solution)/shard_map/all_to_all | solution.py:15
  169.9 1.9 collective-permute-start.13
  171.8 1.9 collective-permute-start.14
  173.8 5.4 %collective-permute-start.12 = (bf16[128,256]{1,0:T(8,128)(2,1)S(1)}, bf16[128,256]{1,0:T(8,128)(2,1)S(1)}, u32[]{:S(2)}, u32[]{:S(2)}) collective-permute-start(bf16[128,256]{1,0:T(8,128)(2,1)S(1)} %bitcast.230), channel_id=1, source_target_pairs={{0,4},{4,0},{8,12},{12,8},{16,20},{20,16},{24,28},{28,24},{1,5},{5... | collective-permute-start | bytes 196616 | tf_op jit(solution)/shard_map/ppermute | solution.py:20
  179.2 1.1 collective-permute-done.14
  180.3 1.1 collective-permute-done.12
  181.5 2.6 %collective-permute-start.15 = (bf16[256,256]{1,0:T(8,128)(2,1)S(1)}, bf16[256,256]{1,0:T(8,128)(2,1)S(1)}, u32[]{:S(2)}, u32[]{:S(2)}) collective-permute-start(bf16[256,256]{1,0:T(8,128)(2,1)S(1)} %bitcast.228), channel_id=1, source_target_pairs={{0,16},{4,20},{8,24},{12,28},{16,0},{20,4},{24,8},{28,12},{1,17},{... | collective-permute-start | bytes 393224 | tf_op jit(solution)/shard_map/ppermute | solution.py:20
  184.6 8.2 %collective-permute-done.15 = bf16[256,256]{1,0:T(8,128)(2,1)S(1)} collective-permute-done((bf16[256,256]{1,0:T(8,128)(2,1)S(1)}, bf16[256,256]{1,0:T(8,128)(2,1)S(1)}, u32[]{:S(2)}, u32[]{:S(2)}) %collective-permute-start.15) | collective-permute-done | bytes 131104 | tf_op jit(solution)/shard_map/ppermute | solution.py:20
  193.2 1.0 maximum_bitcast_fusion
  194.2 3.3 %all-to-all-done.3 = bf16[8,128,512]{2,1,0:T(8,128)(2,1)S(1)} async-done(((bf16[8,128,512]{2,1,0:T(8,128)(2,1)}), bf16[8,128,512]{2,1,0:T(8,128)(2,1)S(1)}, u32[]{:S(2)}, u32[]{:S(2)}) %all-to-all-start.3) | async-done | bytes 1048608 | tf_op jit(solution)/shard_map/all_to_all | solution.py:15
  197.5 0.8 convert_reduce_fusion
  (82 shorter events, 5.4 us)
Async XLA Ops:
  0.6 116.6 %copy-start = (bf16[192,256]{1,0:T(8,128)(2,1)S(1)}, bf16[192,256]{1,0:T(8,128)(2,1)}, u32[]{:S(2)}) copy-start(bf16[192,256]{1,0:T(8,128)(2,1)} %param.9) | copy-start | bytes 294916
  0.6 16.4 %slice-start = ((bf16[1,8,256,256]{3,2,1,0:T(8,128)(2,1)}), bf16[1,8,64,256]{3,2,1,0:T(8,128)(2,1)S(1)}, s32[]{:S(2)}) async-start(bf16[1,8,256,256]{3,2,1,0:T(8,128)(2,1)} %param.6), calls=%async_computation.4 | async-start | bytes 524288 | tf_op jit(solution)/shard_map/slice | solution.py:115
  0.7 45.2 %all-to-all-start = ((bf16[32,8,8,256]{3,2,1,0:T(8,128)(2,1)}), bf16[32,8,8,256]{3,2,1,0:T(8,128)(2,1)S(1)}, u32[]{:S(2)}, u32[]{:S(2)}) async-start(bf16[32,8,8,256]{3,2,1,0:T(8,128)(2,1)} %bitcast.202), calls=%async_computation | async-start | bytes 2097152 | tf_op jit(solution)/shard_map/all_to_all | solution.py:15
  17.2 6.9 %collective-permute-start = (bf16[256,256]{1,0:T(8,128)(2,1)S(1)}, bf16[256,256]{1,0:T(8,128)(2,1)S(1)}, u32[]{:S(2)}, u32[]{:S(2)}) collective-permute-start(bf16[256,256]{1,0:T(8,128)(2,1)S(1)} %bitcast.227), channel_id=1, source_target_pairs={{0,4},{4,0},{8,12},{12,8},{16,20},{20,16},{24,28},{28,24},{1,5},{5... | collective-permute-start | bytes 393224 | tf_op jit(solution)/shard_map/ppermute | solution.py:20
  24.2 9.4 %collective-permute-start.1 = (bf16[256,256]{1,0:T(8,128)(2,1)S(1)}, bf16[256,256]{1,0:T(8,128)(2,1)S(1)}, u32[]{:S(2)}, u32[]{:S(2)}) collective-permute-start(bf16[256,256]{1,0:T(8,128)(2,1)S(1)} %bitcast.224), channel_id=1, source_target_pairs={{0,8},{4,12},{8,0},{12,4},{16,24},{20,28},{24,16},{28,20},{1,9},{5... | collective-permute-start | bytes 393224 | tf_op jit(solution)/shard_map/ppermute | solution.py:20
  33.6 12.4 %copy-start.1 = (bf16[256,16]{0,1:T(8,128)(2,1)S(1)}, bf16[256,16]{0,1:T(8,128)(2,1)}, u32[]{:S(2)}) copy-start(bf16[256,16]{0,1:T(8,128)(2,1)} %param.7) | copy-start | bytes 24580
  33.7 12.2 %collective-permute-start.2 = (bf16[256,256]{1,0:T(8,128)(2,1)S(1)}, bf16[256,256]{1,0:T(8,128)(2,1)S(1)}, u32[]{:S(2)}, u32[]{:S(2)}) collective-permute-start(bf16[256,256]{1,0:T(8,128)(2,1)S(1)} %bitcast.229), channel_id=1, source_target_pairs={{0,16},{4,20},{8,24},{12,28},{16,0},{20,4},{24,8},{28,12},{1,17},{... | collective-permute-start | bytes 393224 | tf_op jit(solution)/shard_map/ppermute | solution.py:20
  49.4 65.9 %all-to-all-start.1 = ((bf16[16,160,256]{2,1,0:T(8,128)(2,1)}), bf16[16,160,256]{2,1,0:T(8,128)(2,1)}, u32[]{:S(2)}, u32[]{:S(2)}) async-start(bf16[16,160,256]{2,1,0:T(8,128)(2,1)} %pad_maximum_fusion.1), calls=%async_computation.1 | async-start | bytes 2621440 | tf_op jit(solution)/shard_map/all_to_all | solution.py:15
  65.5 3.2 %collective-permute-start.3 = (bf16[256,256]{1,0:T(8,128)(2,1)S(1)}, bf16[256,256]{1,0:T(8,128)(2,1)S(1)}, u32[]{:S(2)}, u32[]{:S(2)}) collective-permute-start(bf16[256,256]{1,0:T(8,128)(2,1)S(1)} %bitcast.226), channel_id=1, source_target_pairs={{0,1},{1,0},{2,3},{3,2},{4,5},{5,4},{6,7},{7,6},{8,9},{9,8},{10,11... | collective-permute-start | bytes 393224 | tf_op jit(solution)/shard_map/ppermute | solution.py:20
  68.8 39.7 %collective-permute-start.4 = (bf16[256,256]{1,0:T(8,128)(2,1)S(1)}, bf16[256,256]{1,0:T(8,128)(2,1)S(1)}, u32[]{:S(2)}, u32[]{:S(2)}) collective-permute-start(bf16[256,256]{1,0:T(8,128)(2,1)S(1)} %bitcast.223), channel_id=1, source_target_pairs={{0,2},{2,0},{1,3},{3,1},{4,6},{6,4},{5,7},{7,5},{8,10},{10,8},{9,1... | collective-permute-start | bytes 393224 | tf_op jit(solution)/shard_map/ppermute | solution.py:20
  115.3 10.7 %collective-permute-start.5 = (bf16[2560,256]{1,0:T(8,128)(2,1)}, bf16[2560,256]{1,0:T(8,128)(2,1)}, u32[]{:S(2)}, u32[]{:S(2)}) collective-permute-start(bf16[2560,256]{1,0:T(8,128)(2,1)} %bitcast.32), channel_id=1, source_target_pairs={{0,1},{1,0},{2,3},{3,2},{4,5},{5,4},{6,7},{7,6},{8,9},{9,8},{10,11... | collective-permute-start | bytes 3932168 | tf_op jit(solution)/shard_map/ppermute | solution.py:20
  121.8 30.1 %all-to-all-start.2 = ((bf16[4,1024,128]{2,1,0:T(8,128)(2,1)}), bf16[4,1024,128]{2,1,0:T(8,128)(2,1)}, u32[]{:S(2)}, u32[]{:S(2)}) async-start(bf16[4,1024,128]{2,1,0:T(8,128)(2,1)} %bitcast.58), calls=%async_computation.2 | async-start | bytes 2097152 | tf_op jit(solution)/shard_map/all_to_all | solution.py:15
  128.3 2.2 %copy-start.2 = (bf16[4096,512]{1,0:T(8,128)(2,1)S(1)}, bf16[4096,512]{1,0:T(8,128)(2,1)}, u32[]{:S(2)}) copy-start(bf16[4096,512]{1,0:T(8,128)(2,1)} %param.8) | copy-start | bytes 12582916
  133.1 12.2 %collective-permute-start.8 = (bf16[256,512]{1,0:T(8,128)(2,1)S(1)}, bf16[256,512]{1,0:T(8,128)(2,1)S(1)}, u32[]{:S(2)}, u32[]{:S(2)}) collective-permute-start(bf16[256,512]{1,0:T(8,128)(2,1)S(1)} %pad_maximum_fusion.3), channel_id=1, source_target_pairs={{0,32},{32,0},{1,33},{33,1},{2,34},{34,2},{3,35},{35,3},{4,36},{36... | collective-permute-start | bytes 786440 | tf_op jit(solution)/shard_map/ppermute | solution.py:20
  136.3 11.5 %collective-permute-start.6 = (bf16[256,256]{1,0:T(8,128)(2,1)S(1)}, bf16[256,256]{1,0:T(8,128)(2,1)S(1)}, u32[]{:S(2)}, u32[]{:S(2)}) collective-permute-start(bf16[256,256]{1,0:T(8,128)(2,1)S(1)} %bitcast.225), channel_id=1, source_target_pairs={{0,1},{1,0},{2,3},{3,2},{4,5},{5,4},{6,7},{7,6},{8,9},{9,8},{10,11... | collective-permute-start | bytes 393224 | tf_op jit(solution)/shard_map/ppermute | solution.py:20
  138.9 15.0 %collective-permute-start.9 = (bf16[256,512]{1,0:T(8,128)(2,1)S(1)}, bf16[256,512]{1,0:T(8,128)(2,1)S(1)}, u32[]{:S(2)}, u32[]{:S(2)}) collective-permute-start(bf16[256,512]{1,0:T(8,128)(2,1)S(1)} %pad_maximum_fusion.3), channel_id=1, source_target_pairs={{0,128},{128,0},{1,129},{129,1},{2,130},{130,2},{3,131},{131,3},{4... | collective-permute-start | bytes 786440 | tf_op jit(solution)/shard_map/ppermute | solution.py:20
  145.3 10.2 %collective-permute-start.10 = (bf16[256,512]{1,0:T(8,128)(2,1)S(1)}, bf16[256,512]{1,0:T(8,128)(2,1)S(1)}, u32[]{:S(2)}, u32[]{:S(2)}) collective-permute-start(bf16[256,512]{1,0:T(8,128)(2,1)S(1)} %collective-permute-done.8), channel_id=1, source_target_pairs={{0,128},{128,0},{1,129},{129,1},{2,130},{130,2},{3,131},{131,3},{4... | collective-permute-start | bytes 786440 | tf_op jit(solution)/shard_map/ppermute | solution.py:20
  148.6 21.2 %collective-permute-start.7 = (bf16[256,256]{1,0:T(8,128)(2,1)}, bf16[256,256]{1,0:T(8,128)(2,1)S(1)}, u32[]{:S(2)}, u32[]{:S(2)}) collective-permute-start(bf16[256,256]{1,0:T(8,128)(2,1)} %bitcast.54), channel_id=1, source_target_pairs={{0,2},{2,0},{1,3},{3,1},{4,6},{6,4},{5,7},{7,5},{8,10},{10,8},{9,1... | collective-permute-start | bytes 393224 | tf_op jit(solution)/shard_map/ppermute | solution.py:20
  152.0 5.9 %collective-permute-start.11 = (bf16[4096,128]{1,0:T(8,128)(2,1)}, bf16[4096,128]{1,0:T(8,128)(2,1)S(1)}, u32[]{:S(2)}, u32[]{:S(2)}) collective-permute-start(bf16[4096,128]{1,0:T(8,128)(2,1)} %bitcast.62), channel_id=1, source_target_pairs={{0,1},{1,0},{2,3},{3,2},{4,5},{5,4},{6,7},{7,6},{8,9},{9,8},{10,11... | collective-permute-start | bytes 3145736 | tf_op jit(solution)/shard_map/ppermute | solution.py:20
  159.6 37.9 %all-to-all-start.3 = ((bf16[8,128,512]{2,1,0:T(8,128)(2,1)}), bf16[8,128,512]{2,1,0:T(8,128)(2,1)S(1)}, u32[]{:S(2)}, u32[]{:S(2)}) async-start(bf16[8,128,512]{2,1,0:T(8,128)(2,1)} %bitcast.203), calls=%async_computation.3 | async-start | bytes 2097152 | tf_op jit(solution)/shard_map/all_to_all | solution.py:15
  169.9 9.3 %collective-permute-start.13 = (bf16[128,256]{1,0:T(8,128)(2,1)S(1)}, bf16[128,256]{1,0:T(8,128)(2,1)S(1)}, u32[]{:S(2)}, u32[]{:S(2)}) collective-permute-start(bf16[128,256]{1,0:T(8,128)(2,1)S(1)} %bitcast.233), channel_id=1, source_target_pairs={{0,8},{4,12},{8,0},{12,4},{16,24},{20,28},{24,16},{28,20},{1,9},{5... | collective-permute-start | bytes 196616 | tf_op jit(solution)/shard_map/ppermute | solution.py:20
  171.8 8.5 %collective-permute-start.14 = (bf16[128,256]{1,0:T(8,128)(2,1)S(1)}, bf16[128,256]{1,0:T(8,128)(2,1)S(1)}, u32[]{:S(2)}, u32[]{:S(2)}) collective-permute-start(bf16[128,256]{1,0:T(8,128)(2,1)S(1)} %bitcast.232), channel_id=1, source_target_pairs={{0,12},{4,8},{8,4},{12,0},{16,28},{20,24},{24,20},{28,16},{1,13},{... | collective-permute-start | bytes 196616 | tf_op jit(solution)/shard_map/ppermute | solution.py:20
  173.8 7.6 %collective-permute-start.12 = (bf16[128,256]{1,0:T(8,128)(2,1)S(1)}, bf16[128,256]{1,0:T(8,128)(2,1)S(1)}, u32[]{:S(2)}, u32[]{:S(2)}) collective-permute-start(bf16[128,256]{1,0:T(8,128)(2,1)S(1)} %bitcast.230), channel_id=1, source_target_pairs={{0,4},{4,0},{8,12},{12,8},{16,20},{20,16},{24,28},{28,24},{1,5},{5... | collective-permute-start | bytes 196616 | tf_op jit(solution)/shard_map/ppermute | solution.py:20
  181.5 11.3 %collective-permute-start.15 = (bf16[256,256]{1,0:T(8,128)(2,1)S(1)}, bf16[256,256]{1,0:T(8,128)(2,1)S(1)}, u32[]{:S(2)}, u32[]{:S(2)}) collective-permute-start(bf16[256,256]{1,0:T(8,128)(2,1)S(1)} %bitcast.228), channel_id=1, source_target_pairs={{0,16},{4,20},{8,24},{12,28},{16,0},{20,4},{24,8},{28,12},{1,17},{... | collective-permute-start | bytes 393224 | tf_op jit(solution)/shard_map/ppermute | solution.py:20

commit v7 on v6

--- a/solution.py
+++ b/solution.py
@@ -159,9 +159,9 @@
     )
     grads = jnp.concatenate([pick(head_grads, 1, core), pick(head_grads, 1, 1 - core)])
     normed, grad_pre = column_block(both, mlp_weight, tall(rows), tall(grads))
+    near_twin = across(grad_pre, ("yl", "twin"), 3)
+    twin_grads = across(grad_pre, "twin")
     near_own = across(grad_pre, "yl")
-    twin_grads = across(grad_pre, "twin")
-    near_twin = across(twin_grads, "yl")
     left_other = across(after(left_mine, grad_pre).reshape(-1, lanes), "core")
     back = after(normed, grad_pre)
 

time: 199 us -> 200 us (level)
  the two profiles are of different devices: /device:TPU:22 before, /device:TPU:6 now
where the time goes in v7:
time: 200 us; the launch traced here: 199 us
  starting transfers between devices  98.3 us (49%)
  waiting for transfers between devices  75.7 us (38%)
  local copies, waits for them, and re-layouts  10.4 us (5%)
  other arithmetic  6.77 us (3%)
  matrix products  6.65 us (3%)
    ppermute x16, waiting for transfers between devices, across(): return lax.ppermute(array, axis, [(i, i ^ distance) for i in range(count)])  66.7 us
    all_to_all x4, starting transfers between devices, swap(): return lax.all_to_all(chunks, axes, split_axis=0, concat_axis=0, tiled=True)  49.7 us
    ppermute x16, starting transfers between devices, across(): return lax.ppermute(array, axis, [(i, i ^ distance) for i in range(count)])  48.6 us
    all_to_all x4, waiting for transfers between devices, swap(): return lax.all_to_all(chunks, axes, split_axis=0, concat_axis=0, tiled=True)  9.02 us
  transfers between devices with their start and end apart: 20, of which 12 were waited for; matrix products, arithmetic and copies ran while one was open for 9% of the time, Pallas kernels for 0%

profile of v7, /device:TPU:6, one launch (start us, length us, event | category | flops | bytes accessed | tf_op | source)
XLA Modules:
  0.0 199.2 jit_solution(13707243167697094498)
XLA Ops:
  0.7 16.2 %all-to-all-start = ((bf16[32,8,8,256]{3,2,1,0:T(8,128)(2,1)}), bf16[32,8,8,256]{3,2,1,0:T(8,128)(2,1)S(1)}, u32[]{:S(2)}, u32[]{:S(2)}) async-start(bf16[32,8,8,256]{3,2,1,0:T(8,128)(2,1)} %bitcast.202), calls=%async_computation | async-start | bytes 2097152 | tf_op jit(solution)/shard_map/all_to_all | solution.py:15
  17.1 2.4 %collective-permute-start = (bf16[256,256]{1,0:T(8,128)(2,1)S(1)}, bf16[256,256]{1,0:T(8,128)(2,1)S(1)}, u32[]{:S(2)}, u32[]{:S(2)}) collective-permute-start(bf16[256,256]{1,0:T(8,128)(2,1)S(1)} %bitcast.227), channel_id=1, source_target_pairs={{0,4},{4,0},{8,12},{12,8},{16,20},{20,16},{24,28},{28,24},{1,5},{5... | collective-permute-start | bytes 393224 | tf_op jit(solution)/shard_map/ppermute | solution.py:20
  19.6 4.4 %collective-permute-done = bf16[256,256]{1,0:T(8,128)(2,1)S(1)} collective-permute-done((bf16[256,256]{1,0:T(8,128)(2,1)S(1)}, bf16[256,256]{1,0:T(8,128)(2,1)S(1)}, u32[]{:S(2)}, u32[]{:S(2)}) %collective-permute-start) | collective-permute-done | bytes 131104 | tf_op jit(solution)/shard_map/ppermute | solution.py:20
  24.1 2.4 %collective-permute-start.1 = (bf16[256,256]{1,0:T(8,128)(2,1)S(1)}, bf16[256,256]{1,0:T(8,128)(2,1)S(1)}, u32[]{:S(2)}, u32[]{:S(2)}) collective-permute-start(bf16[256,256]{1,0:T(8,128)(2,1)S(1)} %bitcast.224), channel_id=1, source_target_pairs={{0,8},{4,12},{8,0},{12,4},{16,24},{20,28},{24,16},{28,20},{1,9},{5... | collective-permute-start | bytes 393224 | tf_op jit(solution)/shard_map/ppermute | solution.py:20
  26.5 7.2 %collective-permute-done.1 = bf16[256,256]{1,0:T(8,128)(2,1)S(1)} collective-permute-done((bf16[256,256]{1,0:T(8,128)(2,1)S(1)}, bf16[256,256]{1,0:T(8,128)(2,1)S(1)}, u32[]{:S(2)}, u32[]{:S(2)}) %collective-permute-start.1) | collective-permute-done | bytes 131104 | tf_op jit(solution)/shard_map/ppermute | solution.py:20
  33.8 4.7 %collective-permute-start.2 = (bf16[256,256]{1,0:T(8,128)(2,1)S(1)}, bf16[256,256]{1,0:T(8,128)(2,1)S(1)}, u32[]{:S(2)}, u32[]{:S(2)}) collective-permute-start(bf16[256,256]{1,0:T(8,128)(2,1)S(1)} %bitcast.229), channel_id=1, source_target_pairs={{0,16},{4,20},{8,24},{12,28},{16,0},{20,4},{24,8},{28,12},{1,17},{... | collective-permute-start | bytes 393224 | tf_op jit(solution)/shard_map/ppermute | solution.py:20
  38.5 7.4 %collective-permute-done.2 = bf16[256,256]{1,0:T(8,128)(2,1)S(1)} collective-permute-done((bf16[256,256]{1,0:T(8,128)(2,1)S(1)}, bf16[256,256]{1,0:T(8,128)(2,1)S(1)}, u32[]{:S(2)}, u32[]{:S(2)}) %collective-permute-start.2) | collective-permute-done | bytes 131104 | tf_op jit(solution)/shard_map/ppermute | solution.py:20
  46.3 0.9 convolution_convert_fusion
  48.4 1.1 pad_maximum_fusion.1
  49.5 16.2 %all-to-all-start.1 = ((bf16[16,160,256]{2,1,0:T(8,128)(2,1)}), bf16[16,160,256]{2,1,0:T(8,128)(2,1)}, u32[]{:S(2)}, u32[]{:S(2)}) async-start(bf16[16,160,256]{2,1,0:T(8,128)(2,1)} %pad_maximum_fusion.1), calls=%async_computation.1 | async-start | bytes 2621440 | tf_op jit(solution)/shard_map/all_to_all | solution.py:15
  65.8 1.9 collective-permute-start.3
  67.7 1.3 collective-permute-done.3
  69.1 7.3 %collective-permute-start.4 = (bf16[256,256]{1,0:T(8,128)(2,1)S(1)}, bf16[256,256]{1,0:T(8,128)(2,1)S(1)}, u32[]{:S(2)}, u32[]{:S(2)}) collective-permute-start(bf16[256,256]{1,0:T(8,128)(2,1)S(1)} %bitcast.223), channel_id=1, source_target_pairs={{0,2},{2,0},{1,3},{3,1},{4,6},{6,4},{5,7},{7,5},{8,10},{10,8},{9,1... | collective-permute-start | bytes 393224 | tf_op jit(solution)/shard_map/ppermute | solution.py:20
  76.4 32.3 %collective-permute-done.4 = bf16[256,256]{1,0:T(8,128)(2,1)S(1)} collective-permute-done((bf16[256,256]{1,0:T(8,128)(2,1)S(1)}, bf16[256,256]{1,0:T(8,128)(2,1)S(1)}, u32[]{:S(2)}, u32[]{:S(2)}) %collective-permute-start.4) | collective-permute-done | bytes 131104 | tf_op jit(solution)/shard_map/ppermute | solution.py:20
  108.9 5.9 %all-to-all-done.1 = bf16[16,160,256]{2,1,0:T(8,128)(2,1)} async-done(((bf16[16,160,256]{2,1,0:T(8,128)(2,1)}), bf16[16,160,256]{2,1,0:T(8,128)(2,1)}, u32[]{:S(2)}, u32[]{:S(2)}) %all-to-all-start.1) | async-done | bytes 1310752 | tf_op jit(solution)/shard_map/all_to_all | solution.py:15
  114.7 1.9 collective-permute-start.5
  116.6 0.5 fusion.49
  117.6 0.9 slice.181
  118.5 1.4 fusion.43
  119.9 1.3 copy.84
  121.2 4.3 %all-to-all-start.2 = ((bf16[4,1024,128]{2,1,0:T(8,128)(2,1)}), bf16[4,1024,128]{2,1,0:T(8,128)(2,1)}, u32[]{:S(2)}, u32[]{:S(2)}) async-start(bf16[4,1024,128]{2,1,0:T(8,128)(2,1)} %bitcast.58), calls=%async_computation.2 | async-start | bytes 2097152 | tf_op jit(solution)/shard_map/all_to_all | solution.py:15
  125.5 0.9 slice.224
  126.4 1.3 slice_bitcast_fusion
  128.0 2.0 copy-done.2
  129.9 1.2 fusion.50
  132.7 2.4 %collective-permute-start.6 = (bf16[256,256]{1,0:T(8,128)(2,1)S(1)}, bf16[256,256]{1,0:T(8,128)(2,1)S(1)}, u32[]{:S(2)}, u32[]{:S(2)}) collective-permute-start(bf16[256,256]{1,0:T(8,128)(2,1)S(1)} %bitcast.225), channel_id=1, source_target_pairs={{0,1},{1,0},{2,3},{3,2},{4,5},{5,4},{6,7},{7,6},{8,9},{9,8},{10,11... | collective-permute-start | bytes 393224 | tf_op jit(solution)/shard_map/ppermute | solution.py:20
  135.1 0.6 multiply_reduce_fusion
  135.7 4.5 %collective-permute-start.10 = (bf16[256,512]{1,0:T(8,128)(2,1)S(1)}, bf16[256,512]{1,0:T(8,128)(2,1)S(1)}, u32[]{:S(2)}, u32[]{:S(2)}) collective-permute-start(bf16[256,512]{1,0:T(8,128)(2,1)S(1)} %pad_maximum_fusion.3), channel_id=1, source_target_pairs={{0,160},{32,128},{128,32},{160,0},{1,161},{33,129},{129,33},{161,1... | collective-permute-start | bytes 786440 | tf_op jit(solution)/shard_map/ppermute | solution.py:20
  140.2 2.5 %collective-permute-start.9 = (bf16[256,512]{1,0:T(8,128)(2,1)S(1)}, bf16[256,512]{1,0:T(8,128)(2,1)S(1)}, u32[]{:S(2)}, u32[]{:S(2)}) collective-permute-start(bf16[256,512]{1,0:T(8,128)(2,1)S(1)} %pad_maximum_fusion.3), channel_id=1, source_target_pairs={{0,128},{128,0},{1,129},{129,1},{2,130},{130,2},{3,131},{131,3},{4... | collective-permute-start | bytes 786440 | tf_op jit(solution)/shard_map/ppermute | solution.py:20
  142.7 2.5 %collective-permute-start.8 = (bf16[256,512]{1,0:T(8,128)(2,1)S(1)}, bf16[256,512]{1,0:T(8,128)(2,1)S(1)}, u32[]{:S(2)}, u32[]{:S(2)}) collective-permute-start(bf16[256,512]{1,0:T(8,128)(2,1)S(1)} %pad_maximum_fusion.3), channel_id=1, source_target_pairs={{0,32},{32,0},{1,33},{33,1},{2,34},{34,2},{3,35},{35,3},{4,36},{36... | collective-permute-start | bytes 786440 | tf_op jit(solution)/shard_map/ppermute | solution.py:20
  145.3 0.7 copy.81
  145.9 2.8 %collective-permute-start.7 = (bf16[256,256]{1,0:T(8,128)(2,1)}, bf16[256,256]{1,0:T(8,128)(2,1)S(1)}, u32[]{:S(2)}, u32[]{:S(2)}) collective-permute-start(bf16[256,256]{1,0:T(8,128)(2,1)} %bitcast.54), channel_id=1, source_target_pairs={{0,2},{2,0},{1,3},{3,1},{4,6},{6,4},{5,7},{7,5},{8,10},{10,8},{9,1... | collective-permute-start | bytes 393224 | tf_op jit(solution)/shard_map/ppermute | solution.py:20
  148.8 1.9 collective-permute-start.11
  150.7 2.1 %collective-permute-done.9 = bf16[256,512]{1,0:T(8,128)(2,1)S(1)} collective-permute-done((bf16[256,512]{1,0:T(8,128)(2,1)S(1)}, bf16[256,512]{1,0:T(8,128)(2,1)S(1)}, u32[]{:S(2)}, u32[]{:S(2)}) %collective-permute-start.9) | collective-permute-done | bytes 262176 | tf_op jit(solution)/shard_map/ppermute | solution.py:20
  152.8 1.0 collective-permute-done.8
  154.1 2.0 fusion
  156.1 1.8 add_convert_fusion
  157.9 13.0 %all-to-all-start.3 = ((bf16[8,128,512]{2,1,0:T(8,128)(2,1)}), bf16[8,128,512]{2,1,0:T(8,128)(2,1)S(1)}, u32[]{:S(2)}, u32[]{:S(2)}) async-start(bf16[8,128,512]{2,1,0:T(8,128)(2,1)} %bitcast.203), calls=%async_computation.3 | async-start | bytes 2097152 | tf_op jit(solution)/shard_map/all_to_all | solution.py:15
  171.0 1.9 collective-permute-start.13
  172.9 1.9 collective-permute-start.14
  174.8 5.4 %collective-permute-start.12 = (bf16[128,256]{1,0:T(8,128)(2,1)S(1)}, bf16[128,256]{1,0:T(8,128)(2,1)S(1)}, u32[]{:S(2)}, u32[]{:S(2)}) collective-permute-start(bf16[128,256]{1,0:T(8,128)(2,1)S(1)} %bitcast.230), channel_id=1, source_target_pairs={{0,4},{4,0},{8,12},{12,8},{16,20},{20,16},{24,28},{28,24},{1,5},{5... | collective-permute-start | bytes 196616 | tf_op jit(solution)/shard_map/ppermute | solution.py:20
  180.2 0.6 collective-permute-done.14
  180.9 1.6 collective-permute-done.12
  182.6 2.0 %collective-permute-start.15 = (bf16[256,256]{1,0:T(8,128)(2,1)S(1)}, bf16[256,256]{1,0:T(8,128)(2,1)S(1)}, u32[]{:S(2)}, u32[]{:S(2)}) collective-permute-start(bf16[256,256]{1,0:T(8,128)(2,1)S(1)} %bitcast.228), channel_id=1, source_target_pairs={{0,16},{4,20},{8,24},{12,28},{16,0},{20,4},{24,8},{28,12},{1,17},{... | collective-permute-start | bytes 393224 | tf_op jit(solution)/shard_map/ppermute | solution.py:20
  185.1 8.8 %collective-permute-done.15 = bf16[256,256]{1,0:T(8,128)(2,1)S(1)} collective-permute-done((bf16[256,256]{1,0:T(8,128)(2,1)S(1)}, bf16[256,256]{1,0:T(8,128)(2,1)S(1)}, u32[]{:S(2)}, u32[]{:S(2)}) %collective-permute-start.15) | collective-permute-done | bytes 131104 | tf_op jit(solution)/shard_map/ppermute | solution.py:20
  194.2 1.0 maximum_bitcast_fusion
  195.2 3.1 %all-to-all-done.3 = bf16[8,128,512]{2,1,0:T(8,128)(2,1)S(1)} async-done(((bf16[8,128,512]{2,1,0:T(8,128)(2,1)}), bf16[8,128,512]{2,1,0:T(8,128)(2,1)S(1)}, u32[]{:S(2)}, u32[]{:S(2)}) %all-to-all-start.3) | async-done | bytes 1048608 | tf_op jit(solution)/shard_map/all_to_all | solution.py:15
  198.4 0.8 convert_reduce_fusion
  (82 shorter events, 5.4 us)
Async XLA Ops:
  0.6 116.0 %copy-start = (bf16[192,256]{1,0:T(8,128)(2,1)S(1)}, bf16[192,256]{1,0:T(8,128)(2,1)}, u32[]{:S(2)}) copy-start(bf16[192,256]{1,0:T(8,128)(2,1)} %param.9) | copy-start | bytes 294916
  0.6 16.3 %slice-start = ((bf16[1,8,256,256]{3,2,1,0:T(8,128)(2,1)}), bf16[1,8,64,256]{3,2,1,0:T(8,128)(2,1)S(1)}, s32[]{:S(2)}) async-start(bf16[1,8,256,256]{3,2,1,0:T(8,128)(2,1)} %param.6), calls=%async_computation.4 | async-start | bytes 524288 | tf_op jit(solution)/shard_map/slice | solution.py:115
  0.7 45.3 %all-to-all-start = ((bf16[32,8,8,256]{3,2,1,0:T(8,128)(2,1)}), bf16[32,8,8,256]{3,2,1,0:T(8,128)(2,1)S(1)}, u32[]{:S(2)}, u32[]{:S(2)}) async-start(bf16[32,8,8,256]{3,2,1,0:T(8,128)(2,1)} %bitcast.202), calls=%async_computation | async-start | bytes 2097152 | tf_op jit(solution)/shard_map/all_to_all | solution.py:15
  17.1 6.9 %collective-permute-start = (bf16[256,256]{1,0:T(8,128)(2,1)S(1)}, bf16[256,256]{1,0:T(8,128)(2,1)S(1)}, u32[]{:S(2)}, u32[]{:S(2)}) collective-permute-start(bf16[256,256]{1,0:T(8,128)(2,1)S(1)} %bitcast.227), channel_id=1, source_target_pairs={{0,4},{4,0},{8,12},{12,8},{16,20},{20,16},{24,28},{28,24},{1,5},{5... | collective-permute-start | bytes 393224 | tf_op jit(solution)/shard_map/ppermute | solution.py:20
  24.1 9.6 %collective-permute-start.1 = (bf16[256,256]{1,0:T(8,128)(2,1)S(1)}, bf16[256,256]{1,0:T(8,128)(2,1)S(1)}, u32[]{:S(2)}, u32[]{:S(2)}) collective-permute-start(bf16[256,256]{1,0:T(8,128)(2,1)S(1)} %bitcast.224), channel_id=1, source_target_pairs={{0,8},{4,12},{8,0},{12,4},{16,24},{20,28},{24,16},{28,20},{1,9},{5... | collective-permute-start | bytes 393224 | tf_op jit(solution)/shard_map/ppermute | solution.py:20
  33.7 12.4 %copy-start.1 = (bf16[256,16]{0,1:T(8,128)(2,1)S(1)}, bf16[256,16]{0,1:T(8,128)(2,1)}, u32[]{:S(2)}) copy-start(bf16[256,16]{0,1:T(8,128)(2,1)} %param.7) | copy-start | bytes 24580
  33.8 12.2 %collective-permute-start.2 = (bf16[256,256]{1,0:T(8,128)(2,1)S(1)}, bf16[256,256]{1,0:T(8,128)(2,1)S(1)}, u32[]{:S(2)}, u32[]{:S(2)}) collective-permute-start(bf16[256,256]{1,0:T(8,128)(2,1)S(1)} %bitcast.229), channel_id=1, source_target_pairs={{0,16},{4,20},{8,24},{12,28},{16,0},{20,4},{24,8},{28,12},{1,17},{... | collective-permute-start | bytes 393224 | tf_op jit(solution)/shard_map/ppermute | solution.py:20
  49.5 65.2 %all-to-all-start.1 = ((bf16[16,160,256]{2,1,0:T(8,128)(2,1)}), bf16[16,160,256]{2,1,0:T(8,128)(2,1)}, u32[]{:S(2)}, u32[]{:S(2)}) async-start(bf16[16,160,256]{2,1,0:T(8,128)(2,1)} %pad_maximum_fusion.1), calls=%async_computation.1 | async-start | bytes 2621440 | tf_op jit(solution)/shard_map/all_to_all | solution.py:15
  65.8 3.2 %collective-permute-start.3 = (bf16[256,256]{1,0:T(8,128)(2,1)S(1)}, bf16[256,256]{1,0:T(8,128)(2,1)S(1)}, u32[]{:S(2)}, u32[]{:S(2)}) collective-permute-start(bf16[256,256]{1,0:T(8,128)(2,1)S(1)} %bitcast.226), channel_id=1, source_target_pairs={{0,1},{1,0},{2,3},{3,2},{4,5},{5,4},{6,7},{7,6},{8,9},{9,8},{10,11... | collective-permute-start | bytes 393224 | tf_op jit(solution)/shard_map/ppermute | solution.py:20
  69.1 39.6 %collective-permute-start.4 = (bf16[256,256]{1,0:T(8,128)(2,1)S(1)}, bf16[256,256]{1,0:T(8,128)(2,1)S(1)}, u32[]{:S(2)}, u32[]{:S(2)}) collective-permute-start(bf16[256,256]{1,0:T(8,128)(2,1)S(1)} %bitcast.223), channel_id=1, source_target_pairs={{0,2},{2,0},{1,3},{3,1},{4,6},{6,4},{5,7},{7,5},{8,10},{10,8},{9,1... | collective-permute-start | bytes 393224 | tf_op jit(solution)/shard_map/ppermute | solution.py:20
  114.7 10.7 %collective-permute-start.5 = (bf16[2560,256]{1,0:T(8,128)(2,1)}, bf16[2560,256]{1,0:T(8,128)(2,1)}, u32[]{:S(2)}, u32[]{:S(2)}) collective-permute-start(bf16[2560,256]{1,0:T(8,128)(2,1)} %bitcast.32), channel_id=1, source_target_pairs={{0,1},{1,0},{2,3},{3,2},{4,5},{5,4},{6,7},{7,6},{8,9},{9,8},{10,11... | collective-permute-start | bytes 3932168 | tf_op jit(solution)/shard_map/ppermute | solution.py:20
  121.2 27.6 %all-to-all-start.2 = ((bf16[4,1024,128]{2,1,0:T(8,128)(2,1)}), bf16[4,1024,128]{2,1,0:T(8,128)(2,1)}, u32[]{:S(2)}, u32[]{:S(2)}) async-start(bf16[4,1024,128]{2,1,0:T(8,128)(2,1)} %bitcast.58), calls=%async_computation.2 | async-start | bytes 2097152 | tf_op jit(solution)/shard_map/all_to_all | solution.py:15
  127.8 2.2 %copy-start.2 = (bf16[4096,512]{1,0:T(8,128)(2,1)S(1)}, bf16[4096,512]{1,0:T(8,128)(2,1)}, u32[]{:S(2)}) copy-start(bf16[4096,512]{1,0:T(8,128)(2,1)} %param.8) | copy-start | bytes 12582916
  132.7 12.5 %collective-permute-start.6 = (bf16[256,256]{1,0:T(8,128)(2,1)S(1)}, bf16[256,256]{1,0:T(8,128)(2,1)S(1)}, u32[]{:S(2)}, u32[]{:S(2)}) collective-permute-start(bf16[256,256]{1,0:T(8,128)(2,1)S(1)} %bitcast.225), channel_id=1, source_target_pairs={{0,1},{1,0},{2,3},{3,2},{4,5},{5,4},{6,7},{7,6},{8,9},{9,8},{10,11... | collective-permute-start | bytes 393224 | tf_op jit(solution)/shard_map/ppermute | solution.py:20
  135.7 15.0 %collective-permute-start.10 = (bf16[256,512]{1,0:T(8,128)(2,1)S(1)}, bf16[256,512]{1,0:T(8,128)(2,1)S(1)}, u32[]{:S(2)}, u32[]{:S(2)}) collective-permute-start(bf16[256,512]{1,0:T(8,128)(2,1)S(1)} %pad_maximum_fusion.3), channel_id=1, source_target_pairs={{0,160},{32,128},{128,32},{160,0},{1,161},{33,129},{129,33},{161,1... | collective-permute-start | bytes 786440 | tf_op jit(solution)/shard_map/ppermute | solution.py:20
  140.2 12.6 %collective-permute-start.9 = (bf16[256,512]{1,0:T(8,128)(2,1)S(1)}, bf16[256,512]{1,0:T(8,128)(2,1)S(1)}, u32[]{:S(2)}, u32[]{:S(2)}) collective-permute-start(bf16[256,512]{1,0:T(8,128)(2,1)S(1)} %pad_maximum_fusion.3), channel_id=1, source_target_pairs={{0,128},{128,0},{1,129},{129,1},{2,130},{130,2},{3,131},{131,3},{4... | collective-permute-start | bytes 786440 | tf_op jit(solution)/shard_map/ppermute | solution.py:20
  142.7 11.1 %collective-permute-start.8 = (bf16[256,512]{1,0:T(8,128)(2,1)S(1)}, bf16[256,512]{1,0:T(8,128)(2,1)S(1)}, u32[]{:S(2)}, u32[]{:S(2)}) collective-permute-start(bf16[256,512]{1,0:T(8,128)(2,1)S(1)} %pad_maximum_fusion.3), channel_id=1, source_target_pairs={{0,32},{32,0},{1,33},{33,1},{2,34},{34,2},{3,35},{35,3},{4,36},{36... | collective-permute-start | bytes 786440 | tf_op jit(solution)/shard_map/ppermute | solution.py:20
  145.9 24.9 %collective-permute-start.7 = (bf16[256,256]{1,0:T(8,128)(2,1)}, bf16[256,256]{1,0:T(8,128)(2,1)S(1)}, u32[]{:S(2)}, u32[]{:S(2)}) collective-permute-start(bf16[256,256]{1,0:T(8,128)(2,1)} %bitcast.54), channel_id=1, source_target_pairs={{0,2},{2,0},{1,3},{3,1},{4,6},{6,4},{5,7},{7,5},{8,10},{10,8},{9,1... | collective-permute-start | bytes 393224 | tf_op jit(solution)/shard_map/ppermute | solution.py:20
  148.8 7.3 %collective-permute-start.11 = (bf16[4096,128]{1,0:T(8,128)(2,1)}, bf16[4096,128]{1,0:T(8,128)(2,1)S(1)}, u32[]{:S(2)}, u32[]{:S(2)}) collective-permute-start(bf16[4096,128]{1,0:T(8,128)(2,1)} %bitcast.62), channel_id=1, source_target_pairs={{0,1},{1,0},{2,3},{3,2},{4,5},{5,4},{6,7},{7,6},{8,9},{9,8},{10,11... | collective-permute-start | bytes 3145736 | tf_op jit(solution)/shard_map/ppermute | solution.py:20
  157.9 40.5 %all-to-all-start.3 = ((bf16[8,128,512]{2,1,0:T(8,128)(2,1)}), bf16[8,128,512]{2,1,0:T(8,128)(2,1)S(1)}, u32[]{:S(2)}, u32[]{:S(2)}) async-start(bf16[8,128,512]{2,1,0:T(8,128)(2,1)} %bitcast.203), calls=%async_computation.3 | async-start | bytes 2097152 | tf_op jit(solution)/shard_map/all_to_all | solution.py:15
  171.0 9.3 %collective-permute-start.13 = (bf16[128,256]{1,0:T(8,128)(2,1)S(1)}, bf16[128,256]{1,0:T(8,128)(2,1)S(1)}, u32[]{:S(2)}, u32[]{:S(2)}) collective-permute-start(bf16[128,256]{1,0:T(8,128)(2,1)S(1)} %bitcast.233), channel_id=1, source_target_pairs={{0,8},{4,12},{8,0},{12,4},{16,24},{20,28},{24,16},{28,20},{1,9},{5... | collective-permute-start | bytes 196616 | tf_op jit(solution)/shard_map/ppermute | solution.py:20
  172.9 8.0 %collective-permute-start.14 = (bf16[128,256]{1,0:T(8,128)(2,1)S(1)}, bf16[128,256]{1,0:T(8,128)(2,1)S(1)}, u32[]{:S(2)}, u32[]{:S(2)}) collective-permute-start(bf16[128,256]{1,0:T(8,128)(2,1)S(1)} %bitcast.232), channel_id=1, source_target_pairs={{0,12},{4,8},{8,4},{12,0},{16,28},{20,24},{24,20},{28,16},{1,13},{... | collective-permute-start | bytes 196616 | tf_op jit(solution)/shard_map/ppermute | solution.py:20
  174.8 7.6 %collective-permute-start.12 = (bf16[128,256]{1,0:T(8,128)(2,1)S(1)}, bf16[128,256]{1,0:T(8,128)(2,1)S(1)}, u32[]{:S(2)}, u32[]{:S(2)}) collective-permute-start(bf16[128,256]{1,0:T(8,128)(2,1)S(1)} %bitcast.230), channel_id=1, source_target_pairs={{0,4},{4,0},{8,12},{12,8},{16,20},{20,16},{24,28},{28,24},{1,5},{5... | collective-permute-start | bytes 196616 | tf_op jit(solution)/shard_map/ppermute | solution.py:20
  182.6 11.3 %collective-permute-start.15 = (bf16[256,256]{1,0:T(8,128)(2,1)S(1)}, bf16[256,256]{1,0:T(8,128)(2,1)S(1)}, u32[]{:S(2)}, u32[]{:S(2)}) collective-permute-start(bf16[256,256]{1,0:T(8,128)(2,1)S(1)} %bitcast.228), channel_id=1, source_target_pairs={{0,16},{4,20},{8,24},{12,28},{16,0},{20,4},{24,8},{28,12},{1,17},{... | collective-permute-start | bytes 393224 | tf_op jit(solution)/shard_map/ppermute | solution.py:20

commit v8 on v6

--- a/solution.py
+++ b/solution.py
@@ -182,11 +182,13 @@
     back = ordered(back[0], back[1], 0, core).transpose(2, 3, 0, 1, 4, 5)
     back = cube_swap(back, 2, core, "core")
     back = cube_swap(back, 1, far, "far")
+    if lines == 8:
+        back = x_swap(back, 2)
     back = after(back, term)
     mlp_grad = jnp.sum(swap(term, ("yh", "pair")).astype(jnp.float32), axis=0)
     if lines == 8:
         back = two_bits(back, x)
-    for step in steps[2 if lines == 8 else 0 :]:
+    for step in steps[3 if lines == 8 else 0 :]:
         back = x_swap(back, step)
     head = back.transpose(4, 0, 1, 2, 3, 5).reshape(samples, NF, width)
 

time: 199 us -> 201 us (1.010)
  no operation moved by 1% of the time
where the time goes in v8:
time: 201 us; the launch traced here: 200 us
  starting transfers between devices  93.8 us (47%)
  waiting for transfers between devices  80.2 us (40%)
  local copies, waits for them, and re-layouts  10.2 us (5%)
  other arithmetic  7.46 us (4%)
  matrix products  6.65 us (3%)
    ppermute x16, waiting for transfers between devices, across(): return lax.ppermute(array, axis, [(i, i ^ distance) for i in range(count)])  69.4 us
    ppermute x16, starting transfers between devices, across(): return lax.ppermute(array, axis, [(i, i ^ distance) for i in range(count)])  47.1 us
    all_to_all x4, starting transfers between devices, swap(): return lax.all_to_all(chunks, axes, split_axis=0, concat_axis=0, tiled=True)  46.7 us
    all_to_all x4, waiting for transfers between devices, swap(): return lax.all_to_all(chunks, axes, split_axis=0, concat_axis=0, tiled=True)  10.8 us
  transfers between devices with their start and end apart: 20, of which 12 were waited for; matrix products, arithmetic and copies ran while one was open for 9% of the time, Pallas kernels for 0%

profile of v8, /device:TPU:22, one launch (start us, length us, event | category | flops | bytes accessed | tf_op | source)
XLA Modules:
  0.0 199.7 jit_solution(12473024157198539878)
XLA Ops:
  0.7 16.3 %all-to-all-start = ((bf16[32,8,8,256]{3,2,1,0:T(8,128)(2,1)}), bf16[32,8,8,256]{3,2,1,0:T(8,128)(2,1)S(1)}, u32[]{:S(2)}, u32[]{:S(2)}) async-start(bf16[32,8,8,256]{3,2,1,0:T(8,128)(2,1)} %bitcast.206), calls=%async_computation | async-start | bytes 2097152 | tf_op jit(solution)/shard_map/all_to_all | solution.py:15
  17.2 2.4 %collective-permute-start = (bf16[256,256]{1,0:T(8,128)(2,1)S(1)}, bf16[256,256]{1,0:T(8,128)(2,1)S(1)}, u32[]{:S(2)}, u32[]{:S(2)}) collective-permute-start(bf16[256,256]{1,0:T(8,128)(2,1)S(1)} %bitcast.231), channel_id=1, source_target_pairs={{0,4},{4,0},{8,12},{12,8},{16,20},{20,16},{24,28},{28,24},{1,5},{5... | collective-permute-start | bytes 393224 | tf_op jit(solution)/shard_map/ppermute | solution.py:20
  19.7 4.4 %collective-permute-done = bf16[256,256]{1,0:T(8,128)(2,1)S(1)} collective-permute-done((bf16[256,256]{1,0:T(8,128)(2,1)S(1)}, bf16[256,256]{1,0:T(8,128)(2,1)S(1)}, u32[]{:S(2)}, u32[]{:S(2)}) %collective-permute-start) | collective-permute-done | bytes 131104 | tf_op jit(solution)/shard_map/ppermute | solution.py:20
  24.2 2.4 %collective-permute-start.1 = (bf16[256,256]{1,0:T(8,128)(2,1)S(1)}, bf16[256,256]{1,0:T(8,128)(2,1)S(1)}, u32[]{:S(2)}, u32[]{:S(2)}) collective-permute-start(bf16[256,256]{1,0:T(8,128)(2,1)S(1)} %bitcast.228), channel_id=1, source_target_pairs={{0,8},{4,12},{8,0},{12,4},{16,24},{20,28},{24,16},{28,20},{1,9},{5... | collective-permute-start | bytes 393224 | tf_op jit(solution)/shard_map/ppermute | solution.py:20
  26.6 7.0 %collective-permute-done.1 = bf16[256,256]{1,0:T(8,128)(2,1)S(1)} collective-permute-done((bf16[256,256]{1,0:T(8,128)(2,1)S(1)}, bf16[256,256]{1,0:T(8,128)(2,1)S(1)}, u32[]{:S(2)}, u32[]{:S(2)}) %collective-permute-start.1) | collective-permute-done | bytes 131104 | tf_op jit(solution)/shard_map/ppermute | solution.py:20
  33.7 4.7 %collective-permute-start.2 = (bf16[256,256]{1,0:T(8,128)(2,1)S(1)}, bf16[256,256]{1,0:T(8,128)(2,1)S(1)}, u32[]{:S(2)}, u32[]{:S(2)}) collective-permute-start(bf16[256,256]{1,0:T(8,128)(2,1)S(1)} %bitcast.232), channel_id=1, source_target_pairs={{0,16},{4,20},{8,24},{12,28},{16,0},{20,4},{24,8},{28,12},{1,17},{... | collective-permute-start | bytes 393224 | tf_op jit(solution)/shard_map/ppermute | solution.py:20
  38.4 7.4 %collective-permute-done.2 = bf16[256,256]{1,0:T(8,128)(2,1)S(1)} collective-permute-done((bf16[256,256]{1,0:T(8,128)(2,1)S(1)}, bf16[256,256]{1,0:T(8,128)(2,1)S(1)}, u32[]{:S(2)}, u32[]{:S(2)}) %collective-permute-start.2) | collective-permute-done | bytes 131104 | tf_op jit(solution)/shard_map/ppermute | solution.py:20
  46.2 0.9 convolution_convert_fusion
  48.3 1.1 pad_maximum_fusion.1
  49.4 16.0 %all-to-all-start.1 = ((bf16[16,160,256]{2,1,0:T(8,128)(2,1)}), bf16[16,160,256]{2,1,0:T(8,128)(2,1)}, u32[]{:S(2)}, u32[]{:S(2)}) async-start(bf16[16,160,256]{2,1,0:T(8,128)(2,1)} %pad_maximum_fusion.1), calls=%async_computation.1 | async-start | bytes 2621440 | tf_op jit(solution)/shard_map/all_to_all | solution.py:15
  65.5 1.9 collective-permute-start.3
  67.4 1.3 collective-permute-done.3
  68.8 7.3 %collective-permute-start.4 = (bf16[256,256]{1,0:T(8,128)(2,1)S(1)}, bf16[256,256]{1,0:T(8,128)(2,1)S(1)}, u32[]{:S(2)}, u32[]{:S(2)}) collective-permute-start(bf16[256,256]{1,0:T(8,128)(2,1)S(1)} %bitcast.227), channel_id=1, source_target_pairs={{0,2},{2,0},{1,3},{3,1},{4,6},{6,4},{5,7},{7,5},{8,10},{10,8},{9,1... | collective-permute-start | bytes 393224 | tf_op jit(solution)/shard_map/ppermute | solution.py:20
  76.1 32.4 %collective-permute-done.4 = bf16[256,256]{1,0:T(8,128)(2,1)S(1)} collective-permute-done((bf16[256,256]{1,0:T(8,128)(2,1)S(1)}, bf16[256,256]{1,0:T(8,128)(2,1)S(1)}, u32[]{:S(2)}, u32[]{:S(2)}) %collective-permute-start.4) | collective-permute-done | bytes 131104 | tf_op jit(solution)/shard_map/ppermute | solution.py:20
  108.6 6.7 %all-to-all-done.1 = bf16[16,160,256]{2,1,0:T(8,128)(2,1)} async-done(((bf16[16,160,256]{2,1,0:T(8,128)(2,1)}), bf16[16,160,256]{2,1,0:T(8,128)(2,1)}, u32[]{:S(2)}, u32[]{:S(2)}) %all-to-all-start.1) | async-done | bytes 1310752 | tf_op jit(solution)/shard_map/all_to_all | solution.py:15
  115.4 1.9 collective-permute-start.5
  117.3 0.5 fusion.49
  118.2 0.9 slice.181
  119.1 1.4 fusion.43
  120.6 1.3 copy.79
  121.8 4.2 %all-to-all-start.2 = ((bf16[4,1024,128]{2,1,0:T(8,128)(2,1)}), bf16[4,1024,128]{2,1,0:T(8,128)(2,1)}, u32[]{:S(2)}, u32[]{:S(2)}) async-start(bf16[4,1024,128]{2,1,0:T(8,128)(2,1)} %bitcast.64), calls=%async_computation.2 | async-start | bytes 2097152 | tf_op jit(solution)/shard_map/all_to_all | solution.py:15
  126.1 0.9 slice.224
  127.0 1.3 slice_bitcast_fusion
  128.6 2.0 copy-done.2
  130.5 1.2 fusion.50
  133.1 0.7 pad_maximum_fusion.3
  133.8 3.0 %collective-permute-start.9 = (bf16[256,512]{1,0:T(8,128)(2,1)}, bf16[256,512]{1,0:T(8,128)(2,1)S(1)}, u32[]{:S(2)}, u32[]{:S(2)}) collective-permute-start(bf16[256,512]{1,0:T(8,128)(2,1)} %pad_maximum_fusion.3), channel_id=1, source_target_pairs={{0,32},{32,0},{1,33},{33,1},{2,34},{34,2},{3,35},{35,3},{4,36},{36... | collective-permute-start | bytes 786440 | tf_op jit(solution)/shard_map/ppermute | solution.py:20
  137.0 1.9 collective-permute-start.6
  138.9 0.6 multiply_reduce_fusion
  139.5 2.5 %collective-permute-start.10 = (bf16[256,512]{1,0:T(8,128)(2,1)}, bf16[256,512]{1,0:T(8,128)(2,1)S(1)}, u32[]{:S(2)}, u32[]{:S(2)}) collective-permute-start(bf16[256,512]{1,0:T(8,128)(2,1)} %pad_maximum_fusion.3), channel_id=1, source_target_pairs={{0,128},{128,0},{1,129},{129,1},{2,130},{130,2},{3,131},{131,3},{4... | collective-permute-start | bytes 786440 | tf_op jit(solution)/shard_map/ppermute | solution.py:20
  142.0 3.3 %collective-permute-done.9 = bf16[256,512]{1,0:T(8,128)(2,1)S(1)} collective-permute-done((bf16[256,512]{1,0:T(8,128)(2,1)}, bf16[256,512]{1,0:T(8,128)(2,1)S(1)}, u32[]{:S(2)}, u32[]{:S(2)}) %collective-permute-start.9) | collective-permute-done | bytes 262176 | tf_op jit(solution)/shard_map/ppermute | solution.py:20
  145.3 2.5 %collective-permute-start.11 = (bf16[256,512]{1,0:T(8,128)(2,1)S(1)}, bf16[256,512]{1,0:T(8,128)(2,1)S(1)}, u32[]{:S(2)}, u32[]{:S(2)}) collective-permute-start(bf16[256,512]{1,0:T(8,128)(2,1)S(1)} %collective-permute-done.9), channel_id=1, source_target_pairs={{0,128},{128,0},{1,129},{129,1},{2,130},{130,2},{3,131},{131,3},{4... | collective-permute-start | bytes 786440 | tf_op jit(solution)/shard_map/ppermute | solution.py:20
  147.9 0.7 copy.76
  148.6 3.4 %collective-permute-start.7 = (bf16[256,256]{1,0:T(8,128)(2,1)}, bf16[256,256]{1,0:T(8,128)(2,1)S(1)}, u32[]{:S(2)}, u32[]{:S(2)}) collective-permute-start(bf16[256,256]{1,0:T(8,128)(2,1)} %bitcast.55), channel_id=1, source_target_pairs={{0,2},{2,0},{1,3},{3,1},{4,6},{6,4},{5,7},{7,5},{8,10},{10,8},{9,1... | collective-permute-start | bytes 393224 | tf_op jit(solution)/shard_map/ppermute | solution.py:20
  152.0 1.9 collective-permute-start.12
  153.9 2.1 %collective-permute-done.11 = bf16[256,512]{1,0:T(8,128)(2,1)S(1)} collective-permute-done((bf16[256,512]{1,0:T(8,128)(2,1)S(1)}, bf16[256,512]{1,0:T(8,128)(2,1)S(1)}, u32[]{:S(2)}, u32[]{:S(2)}) %collective-permute-start.11) | collective-permute-done | bytes 262176 | tf_op jit(solution)/shard_map/ppermute | solution.py:20
  156.3 2.0 fusion
  158.3 1.8 add_convert_fusion
  160.1 10.2 %all-to-all-start.3 = ((bf16[8,128,512]{2,1,0:T(8,128)(2,1)}), bf16[8,128,512]{2,1,0:T(8,128)(2,1)S(1)}, u32[]{:S(2)}, u32[]{:S(2)}) async-start(bf16[8,128,512]{2,1,0:T(8,128)(2,1)} %bitcast.207), calls=%async_computation.3 | async-start | bytes 2097152 | tf_op jit(solution)/shard_map/all_to_all | solution.py:15
  170.3 2.0 collective-permute-start.8
  172.3 9.3 %collective-permute-done.8 = bf16[256,256]{1,0:T(8,128)(2,1)S(1)} collective-permute-done((bf16[256,256]{1,0:T(8,128)(2,1)S(1)}, bf16[256,256]{1,0:T(8,128)(2,1)S(1)}, u32[]{:S(2)}, u32[]{:S(2)}) %collective-permute-start.8) | collective-permute-done | bytes 131104 | tf_op jit(solution)/shard_map/ppermute | solution.py:20
  181.7 1.9 collective-permute-start.14
  183.6 1.9 collective-permute-start.15
  186.0 5.4 %collective-permute-start.13 = (bf16[128,256]{1,0:T(8,128)(2,1)S(1)}, bf16[128,256]{1,0:T(8,128)(2,1)S(1)}, u32[]{:S(2)}, u32[]{:S(2)}) collective-permute-start(bf16[128,256]{1,0:T(8,128)(2,1)S(1)} %bitcast.234), channel_id=1, source_target_pairs={{0,4},{4,0},{8,12},{12,8},{16,20},{20,16},{24,28},{28,24},{1,5},{5... | collective-permute-start | bytes 196616 | tf_op jit(solution)/shard_map/ppermute | solution.py:20
  191.7 1.9 collective-permute-done.13
  193.8 1.0 maximum_bitcast_fusion
  194.8 4.1 %all-to-all-done.3 = bf16[8,128,512]{2,1,0:T(8,128)(2,1)S(1)} async-done(((bf16[8,128,512]{2,1,0:T(8,128)(2,1)}), bf16[8,128,512]{2,1,0:T(8,128)(2,1)S(1)}, u32[]{:S(2)}, u32[]{:S(2)}) %all-to-all-start.3) | async-done | bytes 1048608 | tf_op jit(solution)/shard_map/all_to_all | solution.py:15
  198.9 0.8 convert_reduce_fusion
  (81 shorter events, 5.3 us)
Async XLA Ops:
  0.6 116.6 %copy-start = (bf16[192,256]{1,0:T(8,128)(2,1)S(1)}, bf16[192,256]{1,0:T(8,128)(2,1)}, u32[]{:S(2)}) copy-start(bf16[192,256]{1,0:T(8,128)(2,1)} %param.9) | copy-start | bytes 294916
  0.6 16.4 %slice-start = ((bf16[1,8,256,256]{3,2,1,0:T(8,128)(2,1)}), bf16[1,8,64,256]{3,2,1,0:T(8,128)(2,1)S(1)}, s32[]{:S(2)}) async-start(bf16[1,8,256,256]{3,2,1,0:T(8,128)(2,1)} %param.6), calls=%async_computation.4 | async-start | bytes 524288 | tf_op jit(solution)/shard_map/slice | solution.py:115
  0.7 45.2 %all-to-all-start = ((bf16[32,8,8,256]{3,2,1,0:T(8,128)(2,1)}), bf16[32,8,8,256]{3,2,1,0:T(8,128)(2,1)S(1)}, u32[]{:S(2)}, u32[]{:S(2)}) async-start(bf16[32,8,8,256]{3,2,1,0:T(8,128)(2,1)} %bitcast.206), calls=%async_computation | async-start | bytes 2097152 | tf_op jit(solution)/shard_map/all_to_all | solution.py:15
  17.2 6.9 %collective-permute-start = (bf16[256,256]{1,0:T(8,128)(2,1)S(1)}, bf16[256,256]{1,0:T(8,128)(2,1)S(1)}, u32[]{:S(2)}, u32[]{:S(2)}) collective-permute-start(bf16[256,256]{1,0:T(8,128)(2,1)S(1)} %bitcast.231), channel_id=1, source_target_pairs={{0,4},{4,0},{8,12},{12,8},{16,20},{20,16},{24,28},{28,24},{1,5},{5... | collective-permute-start | bytes 393224 | tf_op jit(solution)/shard_map/ppermute | solution.py:20
  24.2 9.4 %collective-permute-start.1 = (bf16[256,256]{1,0:T(8,128)(2,1)S(1)}, bf16[256,256]{1,0:T(8,128)(2,1)S(1)}, u32[]{:S(2)}, u32[]{:S(2)}) collective-permute-start(bf16[256,256]{1,0:T(8,128)(2,1)S(1)} %bitcast.228), channel_id=1, source_target_pairs={{0,8},{4,12},{8,0},{12,4},{16,24},{20,28},{24,16},{28,20},{1,9},{5... | collective-permute-start | bytes 393224 | tf_op jit(solution)/shard_map/ppermute | solution.py:20
  33.6 12.4 %copy-start.1 = (bf16[256,16]{0,1:T(8,128)(2,1)S(1)}, bf16[256,16]{0,1:T(8,128)(2,1)}, u32[]{:S(2)}) copy-start(bf16[256,16]{0,1:T(8,128)(2,1)} %param.7) | copy-start | bytes 24580
  33.7 12.2 %collective-permute-start.2 = (bf16[256,256]{1,0:T(8,128)(2,1)S(1)}, bf16[256,256]{1,0:T(8,128)(2,1)S(1)}, u32[]{:S(2)}, u32[]{:S(2)}) collective-permute-start(bf16[256,256]{1,0:T(8,128)(2,1)S(1)} %bitcast.232), channel_id=1, source_target_pairs={{0,16},{4,20},{8,24},{12,28},{16,0},{20,4},{24,8},{28,12},{1,17},{... | collective-permute-start | bytes 393224 | tf_op jit(solution)/shard_map/ppermute | solution.py:20
  49.4 65.9 %all-to-all-start.1 = ((bf16[16,160,256]{2,1,0:T(8,128)(2,1)}), bf16[16,160,256]{2,1,0:T(8,128)(2,1)}, u32[]{:S(2)}, u32[]{:S(2)}) async-start(bf16[16,160,256]{2,1,0:T(8,128)(2,1)} %pad_maximum_fusion.1), calls=%async_computation.1 | async-start | bytes 2621440 | tf_op jit(solution)/shard_map/all_to_all | solution.py:15
  65.5 3.2 %collective-permute-start.3 = (bf16[256,256]{1,0:T(8,128)(2,1)S(1)}, bf16[256,256]{1,0:T(8,128)(2,1)S(1)}, u32[]{:S(2)}, u32[]{:S(2)}) collective-permute-start(bf16[256,256]{1,0:T(8,128)(2,1)S(1)} %bitcast.230), channel_id=1, source_target_pairs={{0,1},{1,0},{2,3},{3,2},{4,5},{5,4},{6,7},{7,6},{8,9},{9,8},{10,11... | collective-permute-start | bytes 393224 | tf_op jit(solution)/shard_map/ppermute | solution.py:20
  68.8 39.7 %collective-permute-start.4 = (bf16[256,256]{1,0:T(8,128)(2,1)S(1)}, bf16[256,256]{1,0:T(8,128)(2,1)S(1)}, u32[]{:S(2)}, u32[]{:S(2)}) collective-permute-start(bf16[256,256]{1,0:T(8,128)(2,1)S(1)} %bitcast.227), channel_id=1, source_target_pairs={{0,2},{2,0},{1,3},{3,1},{4,6},{6,4},{5,7},{7,5},{8,10},{10,8},{9,1... | collective-permute-start | bytes 393224 | tf_op jit(solution)/shard_map/ppermute | solution.py:20
  115.4 10.7 %collective-permute-start.5 = (bf16[2560,256]{1,0:T(8,128)(2,1)}, bf16[2560,256]{1,0:T(8,128)(2,1)}, u32[]{:S(2)}, u32[]{:S(2)}) collective-permute-start(bf16[2560,256]{1,0:T(8,128)(2,1)} %bitcast.32), channel_id=1, source_target_pairs={{0,1},{1,0},{2,3},{3,2},{4,5},{5,4},{6,7},{7,6},{8,9},{9,8},{10,11... | collective-permute-start | bytes 3932168 | tf_op jit(solution)/shard_map/ppermute | solution.py:20
  121.8 30.1 %all-to-all-start.2 = ((bf16[4,1024,128]{2,1,0:T(8,128)(2,1)}), bf16[4,1024,128]{2,1,0:T(8,128)(2,1)}, u32[]{:S(2)}, u32[]{:S(2)}) async-start(bf16[4,1024,128]{2,1,0:T(8,128)(2,1)} %bitcast.64), calls=%async_computation.2 | async-start | bytes 2097152 | tf_op jit(solution)/shard_map/all_to_all | solution.py:15
  128.3 2.2 %copy-start.2 = (bf16[4096,512]{1,0:T(8,128)(2,1)S(1)}, bf16[4096,512]{1,0:T(8,128)(2,1)}, u32[]{:S(2)}) copy-start(bf16[4096,512]{1,0:T(8,128)(2,1)} %param.8) | copy-start | bytes 12582916
  133.8 11.5 %collective-permute-start.9 = (bf16[256,512]{1,0:T(8,128)(2,1)}, bf16[256,512]{1,0:T(8,128)(2,1)S(1)}, u32[]{:S(2)}, u32[]{:S(2)}) collective-permute-start(bf16[256,512]{1,0:T(8,128)(2,1)} %pad_maximum_fusion.3), channel_id=1, source_target_pairs={{0,32},{32,0},{1,33},{33,1},{2,34},{34,2},{3,35},{35,3},{4,36},{36... | collective-permute-start | bytes 786440 | tf_op jit(solution)/shard_map/ppermute | solution.py:20
  137.0 10.8 %collective-permute-start.6 = (bf16[256,256]{1,0:T(8,128)(2,1)S(1)}, bf16[256,256]{1,0:T(8,128)(2,1)S(1)}, u32[]{:S(2)}, u32[]{:S(2)}) collective-permute-start(bf16[256,256]{1,0:T(8,128)(2,1)S(1)} %bitcast.229), channel_id=1, source_target_pairs={{0,1},{1,0},{2,3},{3,2},{4,5},{5,4},{6,7},{7,6},{8,9},{9,8},{10,11... | collective-permute-start | bytes 393224 | tf_op jit(solution)/shard_map/ppermute | solution.py:20
  139.5 14.4 %collective-permute-start.10 = (bf16[256,512]{1,0:T(8,128)(2,1)}, bf16[256,512]{1,0:T(8,128)(2,1)S(1)}, u32[]{:S(2)}, u32[]{:S(2)}) collective-permute-start(bf16[256,512]{1,0:T(8,128)(2,1)} %pad_maximum_fusion.3), channel_id=1, source_target_pairs={{0,128},{128,0},{1,129},{129,1},{2,130},{130,2},{3,131},{131,3},{4... | collective-permute-start | bytes 786440 | tf_op jit(solution)/shard_map/ppermute | solution.py:20
  145.3 10.6 %collective-permute-start.11 = (bf16[256,512]{1,0:T(8,128)(2,1)S(1)}, bf16[256,512]{1,0:T(8,128)(2,1)S(1)}, u32[]{:S(2)}, u32[]{:S(2)}) collective-permute-start(bf16[256,512]{1,0:T(8,128)(2,1)S(1)} %collective-permute-done.9), channel_id=1, source_target_pairs={{0,128},{128,0},{1,129},{129,1},{2,130},{130,2},{3,131},{131,3},{4... | collective-permute-start | bytes 786440 | tf_op jit(solution)/shard_map/ppermute | solution.py:20
  148.6 21.7 %collective-permute-start.7 = (bf16[256,256]{1,0:T(8,128)(2,1)}, bf16[256,256]{1,0:T(8,128)(2,1)S(1)}, u32[]{:S(2)}, u32[]{:S(2)}) collective-permute-start(bf16[256,256]{1,0:T(8,128)(2,1)} %bitcast.55), channel_id=1, source_target_pairs={{0,2},{2,0},{1,3},{3,1},{4,6},{6,4},{5,7},{7,5},{8,10},{10,8},{9,1... | collective-permute-start | bytes 393224 | tf_op jit(solution)/shard_map/ppermute | solution.py:20
  152.0 6.3 %collective-permute-start.12 = (bf16[4096,128]{1,0:T(8,128)(2,1)}, bf16[4096,128]{1,0:T(8,128)(2,1)S(1)}, u32[]{:S(2)}, u32[]{:S(2)}) collective-permute-start(bf16[4096,128]{1,0:T(8,128)(2,1)} %bitcast.68), channel_id=1, source_target_pairs={{0,1},{1,0},{2,3},{3,2},{4,5},{5,4},{6,7},{7,6},{8,9},{9,8},{10,11... | collective-permute-start | bytes 3145736 | tf_op jit(solution)/shard_map/ppermute | solution.py:20
  160.1 38.8 %all-to-all-start.3 = ((bf16[8,128,512]{2,1,0:T(8,128)(2,1)}), bf16[8,128,512]{2,1,0:T(8,128)(2,1)S(1)}, u32[]{:S(2)}, u32[]{:S(2)}) async-start(bf16[8,128,512]{2,1,0:T(8,128)(2,1)} %bitcast.207), calls=%async_computation.3 | async-start | bytes 2097152 | tf_op jit(solution)/shard_map/all_to_all | solution.py:15
  170.3 11.3 %collective-permute-start.8 = (bf16[256,256]{1,0:T(8,128)(2,1)S(1)}, bf16[256,256]{1,0:T(8,128)(2,1)S(1)}, u32[]{:S(2)}, u32[]{:S(2)}) collective-permute-start(bf16[256,256]{1,0:T(8,128)(2,1)S(1)} %bitcast.233), channel_id=1, source_target_pairs={{0,16},{4,20},{8,24},{12,28},{16,0},{20,4},{24,8},{28,12},{1,17},{... | collective-permute-start | bytes 393224 | tf_op jit(solution)/shard_map/ppermute | solution.py:20
  181.7 9.7 %collective-permute-start.14 = (bf16[128,256]{1,0:T(8,128)(2,1)S(1)}, bf16[128,256]{1,0:T(8,128)(2,1)S(1)}, u32[]{:S(2)}, u32[]{:S(2)}) collective-permute-start(bf16[128,256]{1,0:T(8,128)(2,1)S(1)} %bitcast.237), channel_id=1, source_target_pairs={{0,8},{4,12},{8,0},{12,4},{16,24},{20,28},{24,16},{28,20},{1,9},{5... | collective-permute-start | bytes 196616 | tf_op jit(solution)/shard_map/ppermute | solution.py:20
  183.6 8.1 %collective-permute-start.15 = (bf16[128,256]{1,0:T(8,128)(2,1)S(1)}, bf16[128,256]{1,0:T(8,128)(2,1)S(1)}, u32[]{:S(2)}, u32[]{:S(2)}) collective-permute-start(bf16[128,256]{1,0:T(8,128)(2,1)S(1)} %bitcast.236), channel_id=1, source_target_pairs={{0,12},{4,8},{8,4},{12,0},{16,28},{20,24},{24,20},{28,16},{1,13},{... | collective-permute-start | bytes 196616 | tf_op jit(solution)/shard_map/ppermute | solution.py:20
  186.0 7.6 %collective-permute-start.13 = (bf16[128,256]{1,0:T(8,128)(2,1)S(1)}, bf16[128,256]{1,0:T(8,128)(2,1)S(1)}, u32[]{:S(2)}, u32[]{:S(2)}) collective-permute-start(bf16[128,256]{1,0:T(8,128)(2,1)S(1)} %bitcast.234), channel_id=1, source_target_pairs={{0,4},{4,0},{8,12},{12,8},{16,20},{20,16},{24,28},{28,24},{1,5},{5... | collective-permute-start | bytes 196616 | tf_op jit(solution)/shard_map/ppermute | solution.py:20
